TPU v7x, 32 devices: a whole 2x2x4 slice. The times are simulated.
32 devices in a mesh: dp: 4 (over y, x), seq: 4 (over z), mp: 2 (over core).
Axes of the slice: x: 2, y: 2, z: 4, core: 2. Of those that a mesh axis runs over, the one named last changes fastest.
Arguments:
- hidden_states: bfloat16 [2048, 2048], P(('dp', 'seq')), may hold values from -6 to 6
- embeddings: bfloat16 [2048, 2048], P(('dp', 'seq')), may hold values from -6 to 6
- norm_gain: float32 [4096], replicated, may hold values from 0.1 to 1.9
- input_weights: bfloat16 [4096, 3, 2, 2048], P('dp', None, 'mp', 'seq'), may hold values from -0.09375 to 0.09375
- adapter_down: bfloat16 [4096, 384], P(('seq', 'mp')), may hold values from -0.09375 to 0.09375
- adapter_up: bfloat16 [3, 128, 2, 2048], P(None, None, 'mp', 'seq'), may hold values from -0.5 to 0.5
- output_weights: bfloat16 [2, 2048, 2048], P('mp', 'seq', 'dp'), may hold values from -3 to 3
- own_keys: bfloat16 [4, 4096, 4096], P('dp', 'seq', 'mp'), may hold values from -164 to 164
- own_values: bfloat16 [4, 4096, 4096], P('dp', 'seq', 'mp'), may hold values from -6 to 6
- shared_keys: bfloat16 [2, 512, 4096], P(None, 'seq', 'mp'), may hold values from -164 to 164
- shared_values: bfloat16 [2, 512, 4096], P(None, 'seq', 'mp'), may hold values from -6 to 6
- cached_lengths: int32 [4], P('dp'), may hold values from 1 to 4096, 8192 in all
- prompt_group: int32 [4], P('dp'), may hold values from 0 to 1
- slot_pages: int32 [4, 64], P('dp', 'seq'), may hold values from 0 to 63, as said below
- padding_mask: int32 [2048], P(('dp', 'seq', 'mp')), may hold values from 0 to 1, as said below
Outputs:
- mixed: bfloat16 [2048, 2048], P(('dp', 'seq', 'mp'))
Inputs may be any that keep to these rules, and one draw needn't show every extreme that they name: `slot_pages`: row r maps the 64 page slots of request r one to one onto its pages: slot u holds page (u + c * 16) mod 64 for a whole number c of request r; page p holds own positions p * 64 to p * 64 + 63. `padding_mask`: within each request's 512 tokens the ones come first, then the zeros; at least 128 ones.
All inputs are finite; a program needn't handle non-finite values. No bound on the sum of `cached_lengths` on one device may be relied on, other than what follows from the above.
Results may differ from a plain program's by a relative error of at most 0.025.
The roundings to bfloat16 on the way count: a program that leaves them out, or rounds other values in their place, can miss the bound.
Values may be sent and summed in bfloat16 or wider, within the bound.
No kernel may reach another device: no remote copies, remote signals or barrier semaphores. Data moves between devices by JAX's collectives and lax.ppermute only.
A program may use at most 128 MiB of HBM per device.

v0:
```python
import math

import jax
import jax.numpy as jnp
from jax import lax
from jax.sharding import PartitionSpec as P

HD = 128
PAGE = 64


eps = 1e-05
neg_fill = -1e30
head_block = 4


def joined_2(array, axis, combine):
    everything = jax.tree.map(lambda part: lax.all_gather(part, axis), array)
    leading = jax.tree.map(lambda part: part[0], everything)

    def hop(k, so_far):
        return combine(so_far, jax.tree.map(lambda part: part[k], everything))

    return lax.fori_loop(1, lax.axis_size(axis), hop, leading)


def normalize(hidden_states, embeddings, norm_gain):
    joined = jnp.concatenate([hidden_states, embeddings], axis=1).astype(jnp.float32)
    factor = lax.rsqrt(jnp.mean(joined * joined, axis=1, keepdims=True) + eps)
    return (joined * factor * norm_gain).astype(jnp.bfloat16)


def block_partial(queries, keys, values, usable):
    head_count = queries.shape[1]
    group_size = min(head_block, head_count)
    scaling = 1.0 / math.sqrt(queries.shape[2])

    def one_group(group_index):
        offset = group_index * group_size
        query_part = lax.dynamic_slice_in_dim(queries, offset, group_size, 1)
        key_part = lax.dynamic_slice_in_dim(keys, offset, group_size, 1)
        value_part = lax.dynamic_slice_in_dim(values, offset, group_size, 1)
        scores = (
            jnp.einsum("ihd,jhd->hij", query_part, key_part, preferred_element_type=jnp.float32)
            * scaling
        )
        scores = jnp.where(usable[None], scores, neg_fill)
        peak_score = jnp.max(scores, axis=2)
        exponent = jnp.exp(scores - peak_score[:, :, None])
        totals = jnp.sum(exponent, axis=2)
        weighted = jnp.einsum(
            "hij,jhd->ihd",
            exponent.astype(jnp.bfloat16),
            value_part,
            preferred_element_type=jnp.float32,
        )
        weighted = weighted / jnp.transpose(totals)[:, :, None]
        return (weighted.astype(jnp.bfloat16), jnp.transpose(peak_score), jnp.transpose(totals))

    outputs, peak_rows, total_rows = lax.map(one_group, jnp.arange(head_count // group_size))
    row_count = queries.shape[0]
    outputs = jnp.transpose(outputs, (1, 0, 2, 3)).reshape(row_count, head_count, queries.shape[2])
    peak_rows = jnp.transpose(peak_rows, (1, 0, 2)).reshape(row_count, head_count)
    total_rows = jnp.transpose(total_rows, (1, 0, 2)).reshape(row_count, head_count)
    return (outputs, peak_rows, total_rows)


def join_partials(earlier, later):
    out_first, peak_first, total_first = earlier
    out_second, peak_second, total_second = later
    highest = jnp.maximum(peak_first, peak_second)
    weight_first = total_first * jnp.exp(peak_first - highest)
    weight_second = total_second * jnp.exp(peak_second - highest)
    summed = weight_first + weight_second
    joined = (weight_first[..., None] * out_first + weight_second[..., None] * out_second) / summed[
        ..., None
    ]
    return (joined, highest, summed)


def fold_partials(outputs, peak_scores, totals):
    highest = jnp.max(peak_scores, axis=0)
    weight = totals * jnp.exp(peak_scores - highest)
    return jnp.sum(weight[..., None] * outputs, axis=0) / jnp.sum(weight, axis=0)[..., None]


def shards(
    hidden_states,
    embeddings,
    norm_gain,
    input_weights,
    adapter_down,
    adapter_up,
    output_weights,
    own_keys,
    own_values,
    shared_keys,
    shared_values,
    cached_lengths,
    prompt_group,
    slot_pages,
    padding_mask,
):
    normed = normalize(hidden_states, embeddings, norm_gain)
    gathered = lax.all_gather(normed, "seq", axis=0, tiled=True)
    new_count = gathered.shape[0]
    columns = gathered
    low_sum = jnp.dot(
        columns,
        lax.all_gather(adapter_down, ("seq", "mp"), axis=0, tiled=True),
        preferred_element_type=jnp.float32,
    )
    low_rank = low_sum.astype(jnp.bfloat16)
    width = input_weights.shape[3]
    piece = lax.all_gather(input_weights, "dp", axis=0, tiled=True)
    columns = gathered
    base_terms = jnp.dot(
        columns, piece.reshape(piece.shape[0], 3 * width), preferred_element_type=jnp.float32
    )
    rank_size = adapter_up.shape[1]
    lifted = jnp.einsum(
        "ipr,prc->ipc",
        low_rank.reshape(new_count, 3, rank_size),
        adapter_up[:, :, 0, :],
        preferred_element_type=jnp.float32,
    )
    projected = (base_terms.reshape(new_count, 3, width) + lifted).astype(jnp.bfloat16)
    query_local = projected[:, 0]
    key_local = projected[:, 1]
    value_local = projected[:, 2]
    local_heads = width // HD
    query_all = lax.all_gather(query_local, "seq", axis=1, tiled=True)
    mp_heads = query_all.shape[1] // HD
    group_index = prompt_group[0]
    shared_k = lax.dynamic_index_in_dim(shared_keys, group_index, 0, keepdims=False)
    shared_v = lax.dynamic_index_in_dim(shared_values, group_index, 0, keepdims=False)
    slot_count = own_keys.shape[1]
    cache_keys = jnp.concatenate([own_keys[0], shared_k], axis=0).reshape(-1, mp_heads, HD)
    cache_values = jnp.concatenate([own_values[0], shared_v], axis=0).reshape(-1, mp_heads, HD)
    positions = (
        jnp.repeat(slot_pages[0], PAGE, total_repeat_length=slot_count) * PAGE
        + jnp.arange(slot_count, dtype=jnp.int32) % PAGE
    )
    usable = jnp.concatenate(
        [positions < cached_lengths[0], jnp.ones((shared_k.shape[0],), dtype=jnp.bool_)]
    )[None, :]
    cache_out, cache_peak, cache_total = block_partial(
        query_all.reshape(new_count, mp_heads, HD), cache_keys, cache_values, usable
    )
    places = jnp.arange(new_count, dtype=jnp.int32)
    causal = places[:, None] >= places[None, :]
    new_out, new_peak, new_total = block_partial(
        query_local.reshape(new_count, local_heads, HD),
        key_local.reshape(new_count, local_heads, HD),
        value_local.reshape(new_count, local_heads, HD),
        causal,
    )
    merged_out, merged_peak, merged_total = joined_2(
        (cache_out.astype(jnp.float32), cache_peak, cache_total), "seq", join_partials
    )
    first_head = lax.axis_index("seq") * local_heads
    own_out = lax.dynamic_slice_in_dim(merged_out, first_head, local_heads, 1)
    own_peak = lax.dynamic_slice_in_dim(merged_peak, first_head, local_heads, 1)
    own_total = lax.dynamic_slice_in_dim(merged_total, first_head, local_heads, 1)
    outputs = jnp.stack([own_out, new_out.astype(jnp.float32)])
    peak_scores = jnp.stack([own_peak, new_peak])
    totals = jnp.stack([own_total, new_total])
    attended = (
        fold_partials(outputs, peak_scores, totals)
        .astype(jnp.bfloat16)
        .reshape(new_count, local_heads * HD)
    )
    out_matrix = lax.all_gather(output_weights, "dp", axis=2, tiled=True)[0]
    summed = lax.psum_scatter(
        jnp.dot(attended, out_matrix, preferred_element_type=jnp.float32).astype(jnp.bfloat16),
        ("seq", "mp"),
        scatter_dimension=0,
        tiled=True,
    ).astype(jnp.float32)
    return (padding_mask.astype(jnp.float32)[:, None] * summed).astype(jnp.bfloat16)


def solution(mesh):
    placed = (
        P(("dp", "seq"), None),
        P(("dp", "seq"), None),
        P(),
        P("dp", None, "mp", "seq"),
        P(("seq", "mp"), None),
        P(None, None, "mp", "seq"),
        P("mp", "seq", "dp"),
        P("dp", "seq", "mp"),
        P("dp", "seq", "mp"),
        P(None, "seq", "mp"),
        P(None, "seq", "mp"),
        P("dp"),
        P("dp"),
        P("dp", "seq"),
        P(("dp", "seq", "mp")),
    )
    return jax.shard_map(
        shards, mesh=mesh, in_specs=placed, out_specs=P(("dp", "seq", "mp"), None), check_vma=False
    )
```

profile of v0, /device:TPU:16, one launch (start us, length us, event | category | flops | bytes accessed | tf_op | source)
XLA Modules:
  0.0 728.8 jit_solution(14897936978581266438)
XLA Ops:
  7.3 1.7 fusion.41
  9.0 2.6 fusion.43
  11.7 3.1 copy.54
  14.9 32.5 %all-gather.12.cloned.1.call-done = bf16[4096,384]{1,0:T(8,128)(2,1)} async-done(((bf16[512,384]{1,0:T(8,128)(2,1)}), bf16[4096,384]{1,0:T(8,128)(2,1)}) %all-gather.12.cloned.1.call-update) | async-done | bytes 3145744 | tf_op jit(solution)/shard_map/all_gather | solution.py:110
  47.3 80.9 %all-gather.8.cloned.1.call-done = bf16[512,4096]{1,0:T(8,128)(2,1)} async-done(((bf16[128,4096]{1,0:T(8,128)(2,1)}), bf16[512,4096]{1,0:T(8,128)(2,1)}) %all-gather.8.cloned.1.call-update) | async-done | bytes 4194320 | tf_op jit(solution)/shard_map/all_gather | solution.py:105
  128.2 5.0 convolution_convert_fusion.1
  133.8 118.8 %all-gather.10.cloned.1.call-done = bf16[4096,3,1,512]{0,3,1,2:T(8,128)(2,1)} async-done(((bf16[1024,3,1,512]{0,3,1,2:T(8,128)(2,1)}), bf16[4096,3,1,512]{0,3,1,2:T(8,128)(2,1)}) %all-gather.10.cloned.1.call-update) | async-done | bytes 12582928 | tf_op jit(solution)/shard_map/all_gather | solution.py:115
  252.6 10.9 %fusion.40 = bf16[512,3,512]{0,2,1:T(8,128)(2,1)S(1)} fusion(f32[3,512,512]{1,2,0:T(8,128)S(1)} %fusion.67, bf16[4096,3,1,512]{0,3,1,2:T(8,128)(2,1)} %all-gather.10.cloned.1.call-done, bf16[512,4096]{1,0:T(8,128)(2,1)} %all-gather.8.cloned.1.call-done), kind=kOutput, calls=%fused_computation.44 | convolution fusion | flops 6444023808 | bytes 21495808 | tf_op jit(solution)/shard_map/dot_general | solution.py:117
  263.5 1.2 fusion.80
  265.7 2.2 constant_dynamic-slice_fusion.4
  268.1 6.5 copy.52
  275.3 1.3 copy.81
  276.6 6.3 copy.57
  283.7 4.3 compare_select_fusion.1
  288.2 5.6 fusion.71
  293.8 5.1 pad_maximum_fusion
  298.9 2.8 pad_maximum_fusion.1
  301.8 7.7 %all-gather.18.cloned.1.call-done = bf16[512,1,2048]{0,2,1:T(8,128)(2,1)} async-done(((bf16[512,1,512]{0,2,1:T(8,128)(2,1)}), bf16[512,1,2048]{0,2,1:T(8,128)(2,1)}) %all-gather.18.cloned.1.call-update) | async-done | bytes 2097168 | tf_op jit(solution)/shard_map/all_gather | solution.py:132
  309.5 42.9 %while.40 = (s32[]{:T(128)}, bf16[4,512,4,128]{1,3,2,0:T(8,128)(2,1)S(1)}, f32[4,512,4]{1,2,0:T(4,128)S(1)}, f32[4,512,4]{1,2,0:T(4,128)S(1)}, s32[4]{0:T(128)S(...) while((s32[]{:T(128)}, ...), condition=%wide.region_4.5_spmd, body=%wide.region_1.0_spmd.sunk | while | flops 1234432000 | bytes 31798732 | solution.py:60
  310.8 3.2 fusion.98
  314.0 2.3 fusion.99
  316.3 3.9 fusion.100
  321.5 3.2 fusion.98
  324.7 2.3 fusion.99
  327.0 3.9 fusion.100
  332.2 3.2 fusion.98
  335.5 2.3 fusion.99
  337.7 3.9 fusion.100
  342.9 3.2 fusion.98
  346.2 2.3 fusion.99
  348.5 3.9 fusion.100
  352.4 2.5 convert_bitcast_fusion
  354.9 5.4 copy.61
  361.5 1.0 fusion.37
  363.4 2.4 fusion.64
  365.8 21.1 %all_gather.30 = f32[4,512,16]{1,2,0:T(8,128)S(1)} all-gather(f32[1,512,16]{1,2,0:T(8,128)S(1)} %all_gather_reshape.6), channel_id=1, replica_groups=mesh['dp'=4,'seq'=4,'mp'=2] {'seq'}, dimensions={0}, use_global_device_ids=true | all-gather | bytes 163840 | tf_op jit(solution)/shard_map/all_gather | solution.py:18
  387.1 23.8 %all_gather.31 = f32[4,512,16]{1,2,0:T(8,128)S(1)} all-gather(f32[1,512,16]{1,2,0:T(8,128)S(1)} %all_gather_reshape.7), channel_id=1, replica_groups=mesh['dp'=4,'seq'=4,'mp'=2] {'seq'}, dimensions={0}, use_global_device_ids=true | all-gather | bytes 163840 | tf_op jit(solution)/shard_map/all_gather | solution.py:18
  411.0 237.3 %all-gather.14.cloned.1.call-done = f32[4,512,16,128]{3,2,1,0:T(8,128)} async-done(((f32[1,512,16,128]{3,2,1,0:T(8,128)}), f32[4,512,16,128]{3,2,1,0:T(8,128)}) %all-gather.14.cloned.1.call-update) | async-done | bytes 16777232 | tf_op jit(solution)/shard_map/all_gather | solution.py:18
  648.4 4.4 slice_bitcast_fusion
  652.8 28.4 %while.41 = (s32[]{:T(128)}, f32[512,16,128]{2,1,0:T(8,128)}, f32[512,16]{1,0:T(8,128)S(1)}, f32[512,16]{1,0:T(8,128)S(1)}, f32[4,512,16]{1,2,0:T(8,128)S(1)}, /...) while((s32[]{:T(128)}, f32[512,16,128]{2,1,0:T(8,128)}, ...), condition=%wide.region_6.7_spmd, body=%wide.region_5.6_spmd.sunk | while | flops 4243461 | bytes 13205655 | solution.py:24
  653.3 9.0 %fusion.102 = f32[512,16,128]{2,1,0:T(8,128)} fusion(f32[4,512,16,128]{3,2,1,0:T(8,128)} %get-tuple-element.580, s32[]{:T(128)S(6)} %select_n.136, f32[512,16,128]{2,1,0:T(8,128)} %get-tuple-element.565, f32[512,16]{1,0:T(8,128)S(1)} %get-tuple-element.577, f32[512,16]{1,0:T(8,128)S(1)} %get-tuple-element.512, f32[512,16]{1,0:T(8,128)S(1)} %get-tuple-element.513), kind=kLoop, calls=%fused_computation.23.clone.1 | loop fusion | flops 4194304 | bytes 12681220 | tf_op jit(solution)/shard_map/while/body/eval_jaxpr/div | solution.py:75
  662.8 8.9 %fusion.102 = f32[512,16,128]{2,1,0:T(8,128)} fusion(f32[4,512,16,128]{3,2,1,0:T(8,128)} %get-tuple-element.580, s32[]{:T(128)S(6)} %select_n.136, f32[512,16,128]{2,1,0:T(8,128)} %get-tuple-element.565, f32[512,16]{1,0:T(8,128)S(1)} %get-tuple-element.577, f32[512,16]{1,0:T(8,128)S(1)} %get-tuple-element.512, f32[512,16]{1,0:T(8,128)S(1)} %get-tuple-element.513), kind=kLoop, calls=%fused_computation.23.clone.1 | loop fusion | flops 4194304 | bytes 12681220 | tf_op jit(solution)/shard_map/while/body/eval_jaxpr/div | solution.py:75
  672.2 9.0 %fusion.102 = f32[512,16,128]{2,1,0:T(8,128)} fusion(f32[4,512,16,128]{3,2,1,0:T(8,128)} %get-tuple-element.580, s32[]{:T(128)S(6)} %select_n.136, f32[512,16,128]{2,1,0:T(8,128)} %get-tuple-element.565, f32[512,16]{1,0:T(8,128)S(1)} %get-tuple-element.577, f32[512,16]{1,0:T(8,128)S(1)} %get-tuple-element.512, f32[512,16]{1,0:T(8,128)S(1)} %get-tuple-element.513), kind=kLoop, calls=%fused_computation.23.clone.1 | loop fusion | flops 4194304 | bytes 12681220 | tf_op jit(solution)/shard_map/while/body/eval_jaxpr/div | solution.py:75
  681.2 1.8 constant_dynamic-slice_fusion.2
  683.8 1.7 fusion.46
  685.6 4.3 convolution_convert_fusion
  689.9 30.2 %reduce-scatter.2.cloned.1.call-done = bf16[64,2048]{1,0:T(8,128)(2,1)} async-done(((bf16[512,2048]{1,0:T(8,128)(2,1)}), bf16[64,2048]{1,0:T(8,128)(2,1)}) %reduce-scatter.2.cloned.1.call-update) | async-done | bytes 262160 | tf_op jit(solution)/shard_map/reduce_scatter | solution.py:174
  720.2 1.8 multiply_convert_fusion
  (83 shorter events, 10.3 us)
Async XLA Ops:
  6.5 126.7 %copy-start = (bf16[3,128,1,512]{3,1,2,0:T(8,128)(2,1)S(1)}, bf16[3,128,1,512]{3,1,2,0:T(8,128)(2,1)}, u32[]{:S(2)}) copy-start(bf16[3,128,1,512]{3,1,2,0:T(8,128)(2,1)} %param.26) | copy-start | bytes 1179652
  6.5 5.1 copy-start.4
  6.5 40.8 %all-gather.12.cloned.1.call-start = ((), (), s32[]{:S(2)}) async-start(), calls=%async_computation.3 | async-start | bytes 3538944 | tf_op jit(solution)/shard_map/all_gather | solution.py:110
  7.3 120.9 %all-gather.8.cloned.1.call-start = ((), (), s32[]{:S(2)}) async-start(), calls=%async_computation.1 | async-start | bytes 5242880 | tf_op jit(solution)/shard_map/all_gather | solution.py:105
  11.6 241.0 %all-gather.10.cloned.1.call-start = ((), (), s32[]{:S(2)}) async-start(), calls=%async_computation.2 | async-start | bytes 15728640 | tf_op jit(solution)/shard_map/all_gather | solution.py:115
  14.8 294.7 %all-gather.18.cloned.1.call-start = ((), (), s32[]{:S(2)}) async-start(), calls=%async_computation.7 | async-start | bytes 2621440 | tf_op jit(solution)/shard_map/all_gather | solution.py:132
  264.7 383.6 %all-gather.14.cloned.1.call-start = ((), (), s32[]{:S(2)}) async-start(), calls=%async_computation.4 | async-start | bytes 20971520 | tf_op jit(solution)/shard_map/all_gather | solution.py:18
  276.6 6.3 copy-start.7
  276.6 7.1 copy-start.8
  293.8 5.1 copy-start.2
  360.3 1.0 copy-start.3
  360.3 1.2 copy-start.5
  360.4 325.2 %all-gather.16.cloned.1.call-start = ((), (), s32[]{:S(2)}) async-start(), calls=%async_computation.5 | async-start | bytes 2621440 | tf_op jit(solution)/shard_map/all_gather | solution.py:173
  360.9 359.2 %reduce-scatter.2.cloned.1.call-start = ((), (), s32[]{:S(2)}) async-start(), calls=%async_computation.6 | async-start | bytes 2359296 | tf_op jit(solution)/shard_map/reduce_scatter | solution.py:174
  361.5 1.9 copy-start.6
  685.6 4.3 copy-start.9
  685.6 36.3 %copy-start.1 = (bf16[3,128,1,512]{3,1,2,0:T(8,128)(2,1)S(1)}, bf16[3,128,1,512]{3,1,2,0:T(8,128)(2,1)}, u32[]{:S(2)}) copy-start(bf16[3,128,1,512]{3,1,2,0:T(8,128)(2,1)} %param.26) | copy-start | bytes 1179652
Sparse Core Ops, SparseCore 0:
  9.0 38.2 all-gather.11
  48.9 79.2 all-gather.7
  130.0 122.4 all-gather.9
  264.9 44.5 all-gather.17
  360.5 287.8 all-gather.13
  650.1 35.3 all-gather.15
  690.0 30.0 reduce-scatter.1
where the time goes:
time: 738 us; the launch traced here: 729 us
  waiting for transfers between devices  509 us (69%)
  other arithmetic  66.2 us (9%)
  matrix products  52.7 us (7%)
  blocking collectives  44.9 us (6%)
  local copies, waits for them, and re-layouts  38.1 us (5%)
  between operations  15.1 us (2%)
    all_gather x1, waiting for transfers between devices, joined_2(): everything = jax.tree.map(lambda part: lax.all_gather(part, axis), array)  237 us
    all_gather x1, waiting for transfers between devices, shards(): piece = lax.all_gather(input_weights, 'dp', axis=0, tiled=True)  119 us
    all_gather x1, waiting for transfers between devices, shards(): gathered = lax.all_gather(normed, 'seq', axis=0, tiled=True)  80.9 us
    all_gather x2, blocking collectives, joined_2(): everything = jax.tree.map(lambda part: lax.all_gather(part, axis), array)  44.9 us
    all_gather x1, waiting for transfers between devices, shards(): lax.all_gather(adapter_down, ('seq', 'mp'), axis=0, tiled=True)  32.5 us
    reduce_scatter x1, waiting for transfers between devices, shards(): lax.psum_scatter(jnp.dot(attended, out_matrix, preferred_element_type=jnp...  30.2 us
    div x3, other arithmetic, join_partials(): (weight_first[..., None] * out_first + weight_second[..., None] * out_sec...  27 us
    dot_general x5, matrix products, one_group(): jnp.einsum('hij,jhd->ihd', exponent.astype(jnp.bfloat16), value_part, pre...  18 us
  transfers between devices with their start and end apart: 7, of which 6 were waited for; matrix products, arithmetic and copies ran while one was open for 12% of the time, Pallas kernels for 0%

commit v1 on v0

v1 whole, which is shorter than its diff:
```python
import functools
import math

import jax
import jax.numpy as jnp
from jax import lax
from jax.experimental import pallas as pl
from jax.experimental.pallas import tpu as pltpu
from jax.sharding import PartitionSpec as P

HD = 128
PAGE = 64
EPS = 1e-05
NEG = -1e30
STAT_ROWS = 16
VMEM_LIMIT = 56 * 1024 * 1024

SMEM = pltpu.MemorySpace.SMEM
F32 = jnp.float32
BF16 = jnp.bfloat16


def swap(count, k):
    return [(i, i ^ k) for i in range(count)]


def after(value, *earlier):
    return lax.optimization_barrier((value, *earlier))[0]


def last(pieces):
    return [piece[0] for piece in pieces[-2:]]


def params():
    return pltpu.CompilerParams(vmem_limit_bytes=VMEM_LIMIT)


def cost(flops, moved, transcendentals=0):
    return pl.CostEstimate(flops=flops, bytes_accessed=moved, transcendentals=transcendentals)


def spread(x):
    count = lax.axis_size("seq")
    if count != 4:
        return [[lax.ppermute(x, "seq", swap(count, k))] for k in range(1, count)]
    outward = [(1, 0), (2, 3)]
    middle = [(1, 2), (2, 1)]
    near = lax.ppermute(x, "seq", swap(4, 1))
    across = lax.ppermute(x, "seq", middle)
    second_end = lax.ppermute(across, "seq", outward)
    second_middle = lax.ppermute(near, "seq", middle)
    third_end = lax.ppermute(second_middle, "seq", outward)
    return [[near], [second_end, second_middle], [third_end, across]]


def gather_dp(x):
    count = lax.axis_size("dp")
    if count != 4:
        return [(lax.all_gather(x, "dp", axis=0, tiled=True), None, 0)]
    half = x.shape[0] // 2
    top, bottom = x[:half], x[half:]
    top_1 = lax.ppermute(top, "dp", swap(4, 1))
    bottom_2 = lax.ppermute(bottom, "dp", swap(4, 2))
    top_2 = lax.ppermute(top, "dp", swap(4, 2))
    bottom_1 = lax.ppermute(bottom, "dp", swap(4, 1))
    top_3 = lax.ppermute(top_1, "dp", swap(4, 2))
    bottom_3 = lax.ppermute(bottom_2, "dp", swap(4, 1))
    return [
        (x, 0, 0),
        (top_1, 1, 0),
        (bottom_1, 1, half),
        (top_2, 2, 0),
        (bottom_2, 2, half),
        (top_3, 3, 0),
        (bottom_3, 3, half),
    ]


def gather_down(part):
    dp_count, seq_count = lax.axis_size("dp"), lax.axis_size("seq")
    rows = part.shape[0] // dp_count
    width = part.shape[1]
    own = lax.dynamic_slice_in_dim(part, lax.axis_index("dp") * rows, rows, 0)
    along = lax.all_gather(own, "seq", axis=0, tiled=True)
    if dp_count != 4:
        whole = lax.all_gather(along, "dp", axis=0, tiled=False)
    else:
        pieces = gather_dp(along)
        blocks = [along] + [
            jnp.concatenate([pieces[2 * k - 1][0], pieces[2 * k][0]], axis=0) for k in (1, 2, 3)
        ]
        index = lax.axis_index("dp")
        odd, high = (index & 1) == 1, (index & 2) == 2
        blocks = [jnp.where(odd, blocks[k ^ 1], blocks[k]) for k in range(4)]
        blocks = [jnp.where(high, blocks[k ^ 2], blocks[k]) for k in range(4)]
        whole = jnp.stack(blocks)
    other = lax.ppermute(whole, "mp", swap(2, 1))
    first = lax.axis_index("mp") == 0
    both = jnp.stack([jnp.where(first, whole, other), jnp.where(first, other, whole)])
    both = both.reshape(2, dp_count, seq_count, rows, width)
    return jnp.transpose(both, (2, 0, 1, 3, 4)).reshape(-1, width)


def norm_kernel(at, hidden_ref, embed_ref, gain_ref, out_ref):
    hidden = hidden_ref[...].astype(F32)
    embed = embed_ref[...].astype(F32)
    width = hidden.shape[1]
    squares = jnp.sum(hidden * hidden, axis=1, keepdims=True) + jnp.sum(
        embed * embed, axis=1, keepdims=True
    )
    factor = lax.rsqrt(squares / (2 * width) + EPS)

    @pl.when(at[2] == 0)
    def _():
        out_ref[...] = (hidden * factor * gain_ref[:, :width]).astype(BF16)

    @pl.when(at[2] != 0)
    def _():
        out_ref[...] = (embed * factor * gain_ref[:, width:]).astype(BF16)


def norm(at, hidden, embed, gain):
    return pl.pallas_call(
        norm_kernel,
        out_shape=jax.ShapeDtypeStruct(hidden.shape, BF16),
        in_specs=[pl.BlockSpec(memory_space=SMEM)] + [pl.BlockSpec(memory_space=pltpu.VMEM)] * 3,
        out_specs=pl.BlockSpec(memory_space=pltpu.VMEM),
        compiler_params=params(),
        name="norm",
    )(at, hidden, embed, gain)


def project_kernel(plan, at, *refs):
    seq_slots, pieces = plan
    refs = list(refs)
    mine = [[refs.pop(0) for _ in range(count)] for count in seq_slots]
    other = [[refs.pop(0) for _ in range(count)] for count in seq_slots]
    weights = [refs.pop(0) for _ in pieces]
    down_ref, up_ref, out_ref, joined = refs
    dp, seq, first, is_end = at[0], at[1], at[2] == 0, at[3] == 1
    rows, width = mine[0][0].shape

    def pick(candidates):
        if len(candidates) == 1:
            return candidates[0][...]
        return jnp.where(is_end, candidates[0][...], candidates[1][...])

    for k in range(len(seq_slots)):
        here, there = pick(mine[k]), pick(other[k])
        at_row = pl.ds(pl.multiple_of((seq ^ k) * rows, rows), rows)
        joined[at_row, :width] = jnp.where(first, here, there)
        joined[at_row, width:] = jnp.where(first, there, here)
    low = jnp.dot(joined[...], down_ref[...], preferred_element_type=F32).astype(BF16)
    total = jnp.dot(low, up_ref[...], preferred_element_type=F32)
    for (k, start, size, shard), ref in zip(pieces, weights):
        if k is None:
            columns = joined[...]
        else:
            begin = (dp ^ k) * shard + start
            columns = joined[:, pl.ds(pl.multiple_of(begin, size), size)]
        total += jnp.dot(columns, ref[...], preferred_element_type=F32)
    out_ref[...] = total.astype(BF16)


def project(at, mine, other, pieces, shard, down, up):
    rows = mine[0][0].shape[0] * len(mine)
    width = 2 * mine[0][0].shape[1]
    plan = (
        tuple(len(slot) for slot in mine),
        tuple((k, start, array.shape[0], shard) for array, k, start in pieces),
    )
    arrays = [x for slot in mine for x in slot] + [x for slot in other for x in slot]
    arrays += [array for array, _, _ in pieces] + [down, up]
    columns = up.shape[1]
    return pl.pallas_call(
        functools.partial(project_kernel, plan),
        out_shape=jax.ShapeDtypeStruct((rows, columns), BF16),
        in_specs=[pl.BlockSpec(memory_space=SMEM)]
        + [pl.BlockSpec(memory_space=pltpu.VMEM)] * len(arrays),
        out_specs=pl.BlockSpec(memory_space=pltpu.VMEM),
        scratch_shapes=[pltpu.VMEM((rows, width), BF16)],
        compiler_params=params(),
        cost_estimate=cost(2 * rows * width * (columns + HD), 2 * width * (rows + columns)),
        name="project",
    )(at, *arrays)


def finish_head(head, heads, weighted, peak, total, out_ref, stats):
    level = peak + jnp.log(total)
    high = level.astype(BF16).astype(F32)
    rest = level - high
    mid = rest.astype(BF16).astype(F32)
    stats[pl.ds(3 * head, 1), :] = high
    stats[pl.ds(3 * head + 1, 1), :] = mid
    stats[pl.ds(3 * head + 2, 1), :] = (rest - mid).astype(BF16).astype(F32)
    at_head = pl.ds(pl.multiple_of(head * HD, HD), HD)
    out_ref[at_head, :] = (weighted / total).astype(BF16)

    @pl.when(head == heads - 1)
    def _():
        out_ref[heads * HD :, :] = stats[...].astype(BF16)


def over_keys(left, right):
    return lax.dot_general(left, right, (((0,), (0,)), ((), ())), preferred_element_type=F32)


def scores_of(keys, queries):
    return lax.dot_general(keys, queries, (((1,), (1,)), ((), ())), preferred_element_type=F32)


def cache_kernel(heads, query_count, at, pages, *refs):
    query_refs = refs[:query_count]
    key_ref, value_ref, shared_key_ref, shared_value_ref, out_ref, stats = refs[query_count:]
    head = pl.program_id(0)

    @pl.when(head == 0)
    def _():
        stats[...] = jnp.zeros_like(stats)

    queries = query_refs[0][...]
    if query_count == 2:
        queries = jnp.where(at[3] == 1, queries, query_refs[1][...])
    scale = 1.0 / math.sqrt(HD)
    own = scores_of(key_ref[0], queries) * scale
    shared = scores_of(shared_key_ref[0], queries) * scale
    offset = lax.broadcasted_iota(jnp.int32, (PAGE, own.shape[1]), 0)
    masked = []
    for u in range(own.shape[0] // PAGE):
        usable = offset < at[4] - pages[u] * PAGE
        masked.append(jnp.where(usable, own[u * PAGE : (u + 1) * PAGE], NEG))
    own = jnp.concatenate(masked, axis=0)
    peak = jnp.maximum(
        jnp.max(own, axis=0, keepdims=True), jnp.max(shared, axis=0, keepdims=True)
    )
    own = jnp.exp(own - peak)
    shared = jnp.exp(shared - peak)
    total = jnp.sum(own, axis=0, keepdims=True) + jnp.sum(shared, axis=0, keepdims=True)
    weighted = over_keys(value_ref[0], own.astype(BF16)) + over_keys(
        shared_value_ref[0], shared.astype(BF16)
    )
    finish_head(head, heads, weighted, peak, total, out_ref, stats)


def cache_attention(at, pages, slot, queries, own_keys, own_values, shared_keys, shared_values):
    rows, width = queries[0].shape
    heads = width // HD
    slots, shared_slots = own_keys.shape[1], shared_keys.shape[1]

    def own_block(h, at, pages):
        return (0, 0, (at[1] ^ slot) * heads + h)

    def shared_block(h, at, pages):
        return (at[5], 0, (at[1] ^ slot) * heads + h)

    return pl.pallas_call(
        functools.partial(cache_kernel, heads, len(queries)),
        out_shape=jax.ShapeDtypeStruct((width + STAT_ROWS, rows), BF16),
        grid_spec=pltpu.PrefetchScalarGridSpec(
            num_scalar_prefetch=2,
            grid=(heads,),
            in_specs=[pl.BlockSpec((rows, HD), lambda h, at, pages: (0, h))] * len(queries)
            + [pl.BlockSpec((1, slots, HD), own_block)] * 2
            + [pl.BlockSpec((1, shared_slots, HD), shared_block)] * 2,
            out_specs=pl.BlockSpec((width + STAT_ROWS, rows), lambda h, at, pages: (0, 0)),
            scratch_shapes=[pltpu.VMEM((STAT_ROWS, rows), F32)],
        ),
        compiler_params=params(),
        cost_estimate=cost(
            8 * rows * width * (slots + shared_slots),
            4 * width * (slots + shared_slots),
            rows * heads * (slots + shared_slots),
        ),
        name="cache_attention",
    )(at, pages, *queries, own_keys, own_values, shared_keys, shared_values)


def new_kernel(heads, query_ref, key_ref, value_ref, out_ref, stats):
    head = pl.program_id(0)

    @pl.when(head == 0)
    def _():
        stats[...] = jnp.zeros_like(stats)

    scores = scores_of(key_ref[...], query_ref[...]) * (1.0 / math.sqrt(HD))
    places = lax.broadcasted_iota(jnp.int32, scores.shape, 0)
    tokens = lax.broadcasted_iota(jnp.int32, scores.shape, 1)
    scores = jnp.where(places <= tokens, scores, NEG)
    peak = jnp.max(scores, axis=0, keepdims=True)
    exponent = jnp.exp(scores - peak)
    total = jnp.sum(exponent, axis=0, keepdims=True)
    weighted = over_keys(value_ref[...], exponent.astype(BF16))
    finish_head(head, heads, weighted, peak, total, out_ref, stats)


def new_attention(queries, keys, values):
    rows, width = queries.shape
    heads = width // HD
    return pl.pallas_call(
        functools.partial(new_kernel, heads),
        out_shape=jax.ShapeDtypeStruct((width + STAT_ROWS, rows), BF16),
        grid=(heads,),
        in_specs=[pl.BlockSpec((rows, HD), lambda h: (0, h))] * 3,
        out_specs=pl.BlockSpec((width + STAT_ROWS, rows), lambda h: (0, 0)),
        scratch_shapes=[pltpu.VMEM((STAT_ROWS, rows), F32)],
        compiler_params=params(),
        cost_estimate=cost(8 * rows * rows * width, 8 * rows * width, rows * rows * heads),
        name="new_attention",
    )(queries, keys, values)


def merge_kernel(heads, blocks, at, *refs):
    parts = refs[: len(refs) - 3]
    keep_ref, give_ref, attended = refs[len(refs) - 3 :]
    base = heads * HD
    for h in range(heads):
        levels = []
        for part in parts:
            stats = part[base : base + STAT_ROWS, :].astype(F32)
            levels.append(
                stats[3 * h : 3 * h + 1] + (stats[3 * h + 1 : 3 * h + 2] + stats[3 * h + 2 : 3 * h + 3])
            )
        highest = functools.reduce(jnp.maximum, levels)
        weights = [jnp.exp(level - highest) for level in levels]
        mass = functools.reduce(jnp.add, weights)
        joined = functools.reduce(
            jnp.add,
            [w * part[h * HD : (h + 1) * HD, :].astype(F32) for w, part in zip(weights, parts)],
        )
        attended[:, h * HD : (h + 1) * HD] = jnp.transpose(joined / mass)
    step = keep_ref.shape[0] // blocks
    for block in range(blocks):
        here = pl.ds(pl.multiple_of((2 * block + at[2]) * step, step), step)
        there = pl.ds(pl.multiple_of((2 * block + 1 - at[2]) * step, step), step)
        keep_ref[block * step : (block + 1) * step, :] = attended[here, :].astype(BF16)
        give_ref[block * step : (block + 1) * step, :] = attended[there, :].astype(BF16)


def merge(at, parts, blocks):
    rows = parts[0].shape[1]
    width = parts[0].shape[0] - STAT_ROWS
    half = jax.ShapeDtypeStruct((rows // 2, width), BF16)
    return pl.pallas_call(
        functools.partial(merge_kernel, width // HD, blocks),
        out_shape=(half, half),
        in_specs=[pl.BlockSpec(memory_space=SMEM)]
        + [pl.BlockSpec(memory_space=pltpu.VMEM)] * len(parts),
        out_specs=(pl.BlockSpec(memory_space=pltpu.VMEM),) * 2,
        scratch_shapes=[pltpu.VMEM((rows, width), F32)],
        compiler_params=params(),
        name="merge",
    )(at, *parts)


def output_kernel(count, blocks, at, keep_ref, got_ref, *refs):
    mine, other = refs[:count], refs[count : 2 * count]
    outs, total = refs[2 * count : 2 * count + blocks], refs[2 * count + blocks]
    width = total.shape[1] // (len(mine) // 2) if len(mine) > 1 else total.shape[1]
    depth = keep_ref.shape[1]
    if len(mine) == 1:
        total[...] = jnp.dot(keep_ref[...], mine[0][...], preferred_element_type=F32) + jnp.dot(
            got_ref[...], other[0][...], preferred_element_type=F32
        )
    else:
        half = depth // 2
        groups = [(0,)] + [(2 * k - 1, 2 * k) for k in (1, 2, 3)]
        width = total.shape[1] // 4
        for k, group in enumerate(groups):
            result = 0.0
            for n, index in enumerate(group):
                rows = slice(0, depth) if len(group) == 1 else slice(n * half, (n + 1) * half)
                result = (
                    result
                    + jnp.dot(keep_ref[:, rows], mine[index][...], preferred_element_type=F32)
                    + jnp.dot(got_ref[:, rows], other[index][...], preferred_element_type=F32)
                )
            total[:, k * width : (k + 1) * width] = result
    step = total.shape[0] // blocks
    for k in range(blocks):
        at_row = pl.ds(pl.multiple_of((at[1] ^ k) * step, step), step)
        outs[k][...] = total[at_row, :].astype(BF16)


def output_projection(at, keep, got, mine, other, columns, blocks):
    block = jax.ShapeDtypeStruct((keep.shape[0] // blocks, columns), BF16)
    return pl.pallas_call(
        functools.partial(output_kernel, len(mine), blocks),
        out_shape=(block,) * blocks,
        in_specs=[pl.BlockSpec(memory_space=SMEM)]
        + [pl.BlockSpec(memory_space=pltpu.VMEM)] * (2 + 2 * len(mine)),
        out_specs=(pl.BlockSpec(memory_space=pltpu.VMEM),) * blocks,
        scratch_shapes=[pltpu.VMEM((keep.shape[0], columns), F32)],
        compiler_params=params(),
        cost_estimate=cost(4 * keep.shape[0] * keep.shape[1] * columns, 4 * columns * keep.shape[1]),
        name="output_projection",
    )(at, keep, got, *mine, *other)


def sum_kernel(groups, at, mask_ref, *refs):
    parts, out_ref = refs[:-1], refs[-1]
    width = out_ref.shape[1] // groups
    mask = mask_ref[:, :1]
    for k in range(groups):
        here = slice(k * width, (k + 1) * width)
        total = functools.reduce(jnp.add, [part[:, here].astype(F32) for part in parts])
        total = total * mask
        if groups == 1:
            out_ref[...] = total.astype(BF16)
        else:
            begin = pl.multiple_of((at[0] ^ k) * width, width)
            out_ref[:, pl.ds(begin, width)] = total.astype(BF16)


def final_sum(at, mask, parts, groups):
    return pl.pallas_call(
        functools.partial(sum_kernel, groups),
        out_shape=jax.ShapeDtypeStruct(parts[0].shape, BF16),
        in_specs=[pl.BlockSpec(memory_space=SMEM)]
        + [pl.BlockSpec(memory_space=pltpu.VMEM)] * (1 + len(parts)),
        out_specs=pl.BlockSpec(memory_space=pltpu.VMEM),
        compiler_params=params(),
        name="final_sum",
    )(at, mask, *parts)


def shards(
    hidden_states,
    embeddings,
    norm_gain,
    input_weights,
    adapter_down,
    adapter_up,
    output_weights,
    own_keys,
    own_values,
    shared_keys,
    shared_values,
    cached_lengths,
    prompt_group,
    slot_pages,
    padding_mask,
):
    dp, seq, mp = (lax.axis_index(axis) for axis in ("dp", "seq", "mp"))
    seq_count = lax.axis_size("seq")
    is_end = ((seq == 0) | (seq == seq_count - 1)).astype(jnp.int32)
    at = jnp.stack([dp, seq, mp, is_end, cached_lengths[0], prompt_group[0]])
    pages = slot_pages[0]
    shard = input_weights.shape[0]

    half = norm(at, hidden_states, embeddings, norm_gain[None, :])
    mine = [[half]] + spread(half)
    mine = [[jnp.where(is_end == 1, *slot)] if len(slot) == 2 else slot for slot in mine]
    other = [[lax.ppermute(slot[0], "mp", swap(2, 1))] for slot in mine]

    query_weights = gather_dp(input_weights[:, 0, 0])
    down_0 = gather_down(adapter_down[:, :HD])
    query = project(at, mine, other, query_weights, shard, down_0, adapter_up[0, :, 0])

    key_weights = gather_dp(after(input_weights[:, 1, 0], *last(query_weights)))
    value_weights = gather_dp(after(input_weights[:, 2, 0], *last(key_weights)))
    down_rest = gather_down(after(adapter_down[:, HD:], *last(key_weights)))
    key = project(at, mine, other, key_weights, shard, down_rest[:, :HD], adapter_up[1, :, 0])
    value = project(at, mine, other, value_weights, shard, down_rest[:, HD:], adapter_up[2, :, 0])
    out_own = after(output_weights[0], *last(value_weights))
    if lax.axis_size("dp") == 4:
        out_mine = [piece[0] for piece in gather_dp(out_own)]
    else:
        out_mine = [lax.all_gather(out_own, "dp", axis=1, tiled=True)]
    out_other = [lax.ppermute(piece, "mp", swap(2, 1)) for piece in out_mine]

    slots = [[query]] + spread(query)
    parts = []
    for k, candidates in enumerate(slots):
        part = cache_attention(
            at, pages, k, candidates, own_keys, own_values, shared_keys, shared_values
        )
        parts.append(part if k == 0 else lax.ppermute(part, "seq", swap(seq_count, k)))
    parts.append(new_attention(query, key, value))

    keep, give = merge(at, parts, seq_count)
    got = lax.ppermute(give, "mp", swap(2, 1))
    columns = output_weights.shape[2] * lax.axis_size("dp")
    sums = output_projection(at, keep, got, out_mine, out_other, columns, seq_count)
    sums = [sums[0]] + [lax.ppermute(sums[k], "seq", swap(seq_count, k)) for k in range(1, seq_count)]
    mask = jnp.broadcast_to(padding_mask.astype(F32)[:, None], (padding_mask.shape[0], HD))
    return final_sum(at, mask, sums, 4 if lax.axis_size("dp") == 4 else 1)


def solution(mesh):
    placed = (
        P(("dp", "seq"), None),
        P(("dp", "seq"), None),
        P(),
        P("dp", None, "mp", "seq"),
        P(("seq", "mp"), None),
        P(None, None, "mp", "seq"),
        P("mp", "seq", "dp"),
        P("dp", "seq", "mp"),
        P("dp", "seq", "mp"),
        P(None, "seq", "mp"),
        P(None, "seq", "mp"),
        P("dp"),
        P("dp"),
        P("dp", "seq"),
        P(("dp", "seq", "mp")),
    )
    return jax.shard_map(
        shards, mesh=mesh, in_specs=placed, out_specs=P(("dp", "seq", "mp"), None), check_vma=False
    )
```

time: 738 us -> 321 us (0.43); the launches traced: 729 us -> 321 us
  waiting for transfers between devices: 509 us -> 110 us
  Pallas kernels: 0 us -> 80.7 us
  starting transfers between devices: 0.43 us -> 74.3 us
  other arithmetic: 66.2 us -> 2.08 us
  matrix products: 52.7 us -> 0 us
  local copies, waits for them, and re-layouts: 38.1 us -> 17.1 us
  between operations: 15.1 us -> 2.08 us
  blocking collectives: 44.9 us -> 34.4 us
    all_gather x6 -> x0, waiting for transfers between devices: 477 us -> none  [the longest x1 237 us: joined_2(): everything = jax.tree.map(lambda part: lax.all_gather(part, axis), array)]
    ppermute x0 -> x66, waiting for transfers between devices: none -> 110 us  [the longest x3 23.3 us: shards(): lax.ppermute(sums[k], 'seq', swap(seq_count, k))]
    pallas_call x0 -> x12, Pallas kernels: none -> 80.7 us  [the longest x3 32.1 us: project(): pl.pallas_call(functools.partial(project_kernel, plan), out_shape=jax.Sha...]
    ppermute x0 -> x66, starting transfers between devices: none -> 74.3 us  [the longest x2 7.84 us: spread(): second_middle = lax.ppermute(near, 'seq', middle)]
    dot_general x14 -> x0, matrix products: 52.7 us -> none  [the longest x5 18 us: one_group(): jnp.einsum('hij,jhd->ihd', exponent.astype(jnp.bfloat16), value_part, pre...]
    reduce_scatter x1 -> x0, waiting for transfers between devices: 30.2 us -> none  [shards(): lax.psum_scatter(jnp.dot(attended, out_matrix, preferred_element_type=jnp...]
    div x3 -> x0, other arithmetic: 27 us -> none  [join_partials(): (weight_first[..., None] * out_first + weight_second[..., None] * out_sec...]
    unnamed x24 -> x112, local copies, waits for them, and re-layouts: 17.8 us -> 4.12 us
  transfers between devices with their start and end apart: 7 -> 66, of which waited for: 6 -> 22; matrix products, arithmetic and copies ran while one was open for 12% -> 4% of each run, Pallas kernels for 0% -> 22%
where the time goes in v1:
time: 321 us
  waiting for transfers between devices  110 us (34%)
  Pallas kernels  80.7 us (25%)
  starting transfers between devices  74.3 us (23%)
  blocking collectives  34.4 us (11%)
  local copies, waits for them, and re-layouts  17.1 us (5%)
    all_gather x2, blocking collectives, gather_down(): along = lax.all_gather(own, 'seq', axis=0, tiled=True)  34.4 us
    pallas_call x3, Pallas kernels, project(): pl.pallas_call(functools.partial(project_kernel, plan), out_shape=jax.Sha...  32.1 us
    pallas_call x4, Pallas kernels, cache_attention(): pl.pallas_call(functools.partial(cache_kernel, heads, len(queries)), out_...  31.4 us
    ppermute x3, waiting for transfers between devices, shards(): lax.ppermute(sums[k], 'seq', swap(seq_count, k))  23.3 us
    ppermute x3, waiting for transfers between devices, shards(): lax.ppermute(part, 'seq', swap(seq_count, k))  22.6 us
    ppermute x6, waiting for transfers between devices, gather_dp(): bottom_2 = lax.ppermute(bottom, 'dp', swap(4, 2))  18.1 us
    ppermute x6, waiting for transfers between devices, gather_dp(): top_3 = lax.ppermute(top_1, 'dp', swap(4, 2))  15.2 us
    ppermute x2, waiting for transfers between devices, spread(): third_end = lax.ppermute(second_middle, 'seq', outward)  10.9 us
  transfers between devices with their start and end apart: 66, of which 22 were waited for; matrix products, arithmetic and copies ran while one was open for 4% of the time, Pallas kernels for 22%

profile of v1, /device:TPU:16, one launch (start us, length us, event | category | flops | bytes accessed | tf_op | source)
XLA Modules:
  0.0 320.6 jit_solution(13645685592828992464)
XLA Ops:
  1.9 2.4 norm.1.refs_0_
  6.0 1.9 collective-permute-start.1
  7.9 2.3 slice_bitcast_fusion.3
  13.2 14.6 %all_gather.6 = bf16[512,128]{1,0:T(8,128)(2,1)S(1)} all-gather(bf16[128,128]{1,0:T(8,128)(2,1)S(1)} %constant_dynamic-slice_fusion.1), channel_id=1, replica_groups=mesh['dp'=4,'seq'=4,'mp'=2] {'seq'}, dimensions={0}, use_global_device_ids=true | all-gather | bytes 163840 | tf_op jit(solution)/shard_map/all_gather | solution.py:85
  27.8 1.6 collective-permute-start.19
  29.4 3.1 slice_bitcast_fusion
  34.0 2.8 collective-permute-done.15
  37.9 3.2 collective-permute-done.17
  42.6 3.1 collective-permute-done.20
  47.0 3.0 collective-permute-done.16
  50.0 1.7 collective-permute-start.18
  51.7 4.1 %collective-permute-start.2 = (bf16[128,2048]{1,0:T(8,128)(2,1)}, bf16[128,2048]{1,0:T(8,128)(2,1)S(1)}, u32[]{:S(2)}, u32[]{:S(2)}) collective-permute-start(bf16[128,2048]{1,0:T(8,128)(2,1)} %collective-permute-done.1), channel_id=1, source_target_pairs={{2,0},{4,6},{3,1},{5,7},{10,8},{12,14},{11,9},{13,15},{18,16},{20,... | collective-permute-start | bytes 1572872 | tf_op jit(solution)/shard_map/ppermute | solution.py:51
  55.8 3.4 %collective-permute-start.3 = (bf16[128,2048]{1,0:T(8,128)(2,1)S(1)}, bf16[128,2048]{1,0:T(8,128)(2,1)S(1)}, u32[]{:S(2)}, u32[]{:S(2)}) collective-permute-start(bf16[128,2048]{1,0:T(8,128)(2,1)S(1)} %collective-permute-done.refs_1_), channel_id=1, source_target_pairs={{2,4},{4,2},{3,5},{5,3},{10,12},{12,10},{11,13},{13,11},{18,20},{2... | collective-permute-start | bytes 1572872 | tf_op jit(solution)/shard_map/ppermute | solution.py:52
  60.8 10.9 %collective-permute-done.13.refs_13_ = bf16[512,512]{1,0:T(8,128)(2,1)S(1)} collective-permute-done((bf16[512,512]{1,0:T(8,128)(2,1)}, bf16[512,512]{1,0:T(8,128)(2,1)S(1)}, u32[]{:S(2)}, u32[]{:S(2)}) %collective-permute-start.13) | collective-permute-done | bytes 524320 | tf_op jit(solution)/shard_map/ppermute | solution.py:67
  72.3 2.4 collective-permute-done.14.refs_14_
  78.5 10.9 %collective-permute-done.4 = bf16[128,2048]{1,0:T(8,128)(2,1)S(1)} collective-permute-done((bf16[128,2048]{1,0:T(8,128)(2,1)S(1)}, bf16[128,2048]{1,0:T(8,128)(2,1)S(1)}, u32[]{:S(2)}, u32[]{:S(2)}) %collective-permute-start.4) | collective-permute-done | bytes 524320 | tf_op jit(solution)/shard_map/ppermute | solution.py:53
  95.1 9.3 %collective-permute-done.33.refs_12_ = bf16[512,512]{1,0:T(8,128)(2,1)S(1)} collective-permute-done((bf16[512,512]{1,0:T(8,128)(2,1)}, bf16[512,512]{1,0:T(8,128)(2,1)S(1)}, u32[]{:S(2)}, u32[]{:S(2)}) %collective-permute-start.33) | collective-permute-done | bytes 524320 | tf_op jit(solution)/shard_map/ppermute | solution.py:64
  107.5 10.7 %project.3.refs_0_.query_ref = bf16[512,512]{1,0:T(8,128)(2,1)} custom-call(s32[6]{0:T(128)} %stack.67.at, bf16[128,2048]{1,0:T(8,128)(2,1)} %norm.1.refs_0_, bf16[128,2048]{1,0:T(8,128)(2,1)} %copy-done.5, bf16[128,2048]{1,0:T(8,128)(2,1)} %copy-done.3, bf16[128,2048]{1,0:T(8,128)(2,1)} %copy-done.4, bf16[128,2048]{1,0:T(8,128)(2,1)} %copy-done.6, ...), custom_call_target="tpu_custom_call" | custom-call | flops 2684354560 | bytes 8388608 | tf_op jit(solution)/shard_map/project/pallas_call | solution.py:176
  118.2 2.5 collective-permute-start.22
  120.6 2.4 collective-permute-start.24
  123.1 19.9 %all_gather.7 = bf16[512,256]{1,0:T(8,128)(2,1)S(1)} all-gather(bf16[128,256]{1,0:T(8,128)(2,1)S(1)} %constant_dynamic-slice_fusion), channel_id=1, replica_groups=mesh['dp'=4,'seq'=4,'mp'=2] {'seq'}, dimensions={0}, use_global_device_ids=true | all-gather | bytes 327680 | tf_op jit(solution)/shard_map/all_gather | solution.py:85
  147.3 2.1 collective-permute-done.40
  152.3 3.2 %collective-permute-done.41 = bf16[256,256]{1,0:T(8,128)(2,1)S(1)} collective-permute-done((bf16[256,256]{1,0:T(8,128)(2,1)S(1)}, bf16[256,256]{1,0:T(8,128)(2,1)S(1)}, u32[]{:S(2)}, u32[]{:S(2)}) %collective-permute-start.41) | collective-permute-done | bytes 131104 | tf_op jit(solution)/shard_map/ppermute | solution.py:66
  158.6 4.0 %collective-permute-done.39 = bf16[256,256]{1,0:T(8,128)(2,1)S(1)} collective-permute-done((bf16[256,256]{1,0:T(8,128)(2,1)S(1)}, bf16[256,256]{1,0:T(8,128)(2,1)S(1)}, u32[]{:S(2)}, u32[]{:S(2)}) %collective-permute-start.39) | collective-permute-done | bytes 131104 | tf_op jit(solution)/shard_map/ppermute | solution.py:68
  163.8 5.6 %collective-permute-done.46.refs_12_ = bf16[512,512]{1,0:T(8,128)(2,1)S(1)} collective-permute-done((bf16[512,512]{1,0:T(8,128)(2,1)S(1)}, bf16[512,512]{1,0:T(8,128)(2,1)S(1)}, u32[]{:S(2)}, u32[]{:S(2)}) %collective-permute-start.46) | collective-permute-done | bytes 524320 | tf_op jit(solution)/shard_map/ppermute | solution.py:64
  169.5 1.8 collective-permute-start.48
  171.2 2.4 collective-permute-start.25
  173.6 4.4 %collective-permute-start.26 = (bf16[512,512]{1,0:T(8,128)(2,1)}, bf16[512,512]{1,0:T(8,128)(2,1)S(1)}, u32[]{:S(2)}, u32[]{:S(2)}) collective-permute-start(bf16[512,512]{1,0:T(8,128)(2,1)} %collective-permute-done.22.refs_0_), channel_id=1, source_target_pairs={{2,4},{4,2},{3,5},{5,3},{10,12},{12,10},{11,13},{13,11},{18,20},{2... | collective-permute-start | bytes 1572872 | tf_op jit(solution)/shard_map/ppermute | solution.py:52
  178.0 7.8 %cache_attention.4.refs_0_ = bf16[528,512]{1,0:T(8,128)(2,1)} custom-call(s32[6]{0:T(128)} %stack.67.at, s32[16]{0:T(128)} %bitcast.59, bf16[512,512]{1,0:T(8,128)(2,1)} %project.3.refs_0_.query_ref, bf16[1,1024,2048]{2,1,0:T(8,128)(2,1)} %refs_2_.7, bf16[1,1024,2048]{2,1,0:T(8,128)(2,1)} %refs_3_.7, bf16[2,128,2048]{2,1,0:T(8,128)(2,1)} %refs_4_.7, ...), custom_call_target="tpu_custom_call" | custom-call | flops 2415919104 | bytes 2359296 | tf_op jit(solution)/shard_map/cache_attention/pallas_call | solution.py:257
  187.4 7.8 %cache_attention.5 = bf16[528,512]{1,0:T(8,128)(2,1)} custom-call(s32[6]{0:T(128)} %stack.67.at, s32[16]{0:T(128)} %bitcast.60, bf16[512,512]{1,0:T(8,128)(2,1)} %collective-permute-done.22.refs_0_, bf16[1,1024,2048]{2,1,0:T(8,128)(2,1)} %refs_2_.7, bf16[1,1024,2048]{2,1,0:T(8,128)(2,1)} %refs_3_.7, bf16[2,128,2048]{2,1,0:T(8,128)(2,1)} %refs_4_.7, ...), custom_call_target="tpu_custom_call" | custom-call | flops 2415919104 | bytes 2359296 | tf_op jit(solution)/shard_map/cache_attention/pallas_call | solution.py:257
  197.4 2.1 collective-permute-start.28
  199.5 7.8 %cache_attention.6 = bf16[528,512]{1,0:T(8,128)(2,1)} custom-call(s32[6]{0:T(128)} %stack.67.at, s32[16]{0:T(128)} %bitcast.61, bf16[512,512]{1,0:T(8,128)(2,1)} %collective-permute-done.25.refs_0_, bf16[512,512]{1,0:T(8,128)(2,1)} %copy-done.33, bf16[1,1024,2048]{2,1,0:T(8,128)(2,1)} %refs_2_.7, bf16[1,1024,2048]{2,1,0:T(8,128)(2,1)} %refs_3_.7, ...), custom_call_target="tpu_custom_call" | custom-call | flops 2415919104 | bytes 2359296 | tf_op jit(solution)/shard_map/cache_attention/pallas_call | solution.py:257
  210.8 8.0 %cache_attention.7 = bf16[528,512]{1,0:T(8,128)(2,1)} custom-call(s32[6]{0:T(128)} %stack.67.at, s32[16]{0:T(128)} %bitcast.62, bf16[512,512]{1,0:T(8,128)(2,1)} %collective-permute-done.28.refs_0_, bf16[512,512]{1,0:T(8,128)(2,1)} %copy-done.22, bf16[1,1024,2048]{2,1,0:T(8,128)(2,1)} %refs_2_.7, bf16[1,1024,2048]{2,1,0:T(8,128)(2,1)} %refs_3_.7, ...), custom_call_target="tpu_custom_call" | custom-call | flops 2415919104 | bytes 2359296 | tf_op jit(solution)/shard_map/cache_attention/pallas_call | solution.py:257
  221.4 1.7 collective-permute-start.27
  223.1 2.3 collective-permute-start.29
  227.0 10.6 %project.4.key_ref = bf16[512,512]{1,0:T(8,128)(2,1)} custom-call(s32[6]{0:T(128)} %stack.67.at, bf16[128,2048]{1,0:T(8,128)(2,1)} %norm.1.refs_0_, bf16[128,2048]{1,0:T(8,128)(2,1)} %copy-done.5, bf16[128,2048]{1,0:T(8,128)(2,1)} %copy-done.3, bf16[128,2048]{1,0:T(8,128)(2,1)} %copy-done.4, bf16[128,2048]{1,0:T(8,128)(2,1)} %copy-done.6, ...), custom_call_target="tpu_custom_call" | custom-call | flops 2684354560 | bytes 8388608 | tf_op jit(solution)/shard_map/project/pallas_call | solution.py:176
  239.2 12.7 %collective-permute-done.27.refs_2_ = bf16[528,512]{1,0:T(8,128)(2,1)S(1)} collective-permute-done((bf16[528,512]{1,0:T(8,128)(2,1)S(1)}, bf16[528,512]{1,0:T(8,128)(2,1)S(1)}, u32[]{:S(2)}, u32[]{:S(2)}) %collective-permute-start.27) | collective-permute-done | bytes 540704 | tf_op jit(solution)/shard_map/ppermute | solution.py:478
  253.4 9.9 %collective-permute-done.29.refs_3_ = bf16[528,512]{1,0:T(8,128)(2,1)S(1)} collective-permute-done((bf16[528,512]{1,0:T(8,128)(2,1)}, bf16[528,512]{1,0:T(8,128)(2,1)S(1)}, u32[]{:S(2)}, u32[]{:S(2)}) %collective-permute-start.29) | collective-permute-done | bytes 540704 | tf_op jit(solution)/shard_map/ppermute | solution.py:478
  263.3 10.8 %project.5.value_ref = bf16[512,512]{1,0:T(8,128)(2,1)} custom-call(s32[6]{0:T(128)} %stack.67.at, bf16[128,2048]{1,0:T(8,128)(2,1)} %norm.1.refs_0_, bf16[128,2048]{1,0:T(8,128)(2,1)} %copy-done.5, bf16[128,2048]{1,0:T(8,128)(2,1)} %copy-done.3, bf16[128,2048]{1,0:T(8,128)(2,1)} %copy-done.4, bf16[128,2048]{1,0:T(8,128)(2,1)} %copy-done.6, ...), custom_call_target="tpu_custom_call" | custom-call | flops 2684354560 | bytes 8388608 | tf_op jit(solution)/shard_map/project/pallas_call | solution.py:176
  274.2 4.9 %new_attention.1.refs_4_ = bf16[528,512]{1,0:T(8,128)(2,1)} custom-call(bf16[512,512]{1,0:T(8,128)(2,1)} %project.3.refs_0_.query_ref, bf16[512,512]{1,0:T(8,128)(2,1)} %project.4.key_ref, bf16[512,512]{1,0:T(8,128)(2,1)} %project.5.value_ref), custom_call_target="tpu_custom_call" | custom-call | flops 1073741824 | bytes 2097152 | tf_op jit(solution)/shard_map/new_attention/pallas_call | solution.py:300
  279.1 3.2 %merge.1 = (bf16[256,512]{1,0:T(8,128)(2,1)}, bf16[256,512]{1,0:T(8,128)(2,1)}) custom-call(s32[6]{0:T(128)} %stack.67.at, bf16[528,512]{1,0:T(8,128)(2,1)} %cache_attention.4.refs_0_, bf16[528,512]{1,0:T(8,128)(2,1)} %copy-done.13, bf16[528,512]{1,0:T(8,128)(2,1)} %copy-done.14, bf16[528,512]{1,0:T(8,128)(2,1)} %copy-done.15, ...), custom_call_target="tpu_custom_call" | custom-call | tf_op jit(solution)/shard_map/merge/pallas_call | solution.py:344
  286.3 4.6 %output_projection.1 = (bf16[64,2048]{1,0:T(8,128)(2,1)}, bf16[64,2048]{1,0:T(8,128)(2,1)}, bf16[64,2048]{1,0:T(8,128)(2,1)}, bf16[64,2048]{1,0:T(8,128)(2,1)}) custom-call(s32[6]{0:T(128)} %stack.67.at, bf16[256,512]{1,0:T(8,128)(2,1)} %get-tuple-element.18.keep_ref, bf16[256,512]{1,0:T(8,128)(2,1)} %copy-done.48, bf16[512,512]{1,0:T(8,128)(2,1)} %bitcast.53, ...), custom_call_target="tpu_custom_call" | custom-call | flops 1073741824 | bytes 4194304 | tf_op jit(solution)/shard_map/output_projection/pallas_call | solution.py:387
  290.9 1.8 collective-permute-start.64
  292.7 1.7 collective-permute-start.65
  294.4 7.4 %collective-permute-done.63.refs_1_ = bf16[64,2048]{1,0:T(8,128)(2,1)S(1)} collective-permute-done((bf16[64,2048]{1,0:T(8,128)(2,1)}, bf16[64,2048]{1,0:T(8,128)(2,1)S(1)}, u32[]{:S(2)}, u32[]{:S(2)}) %collective-permute-start.63) | collective-permute-done | bytes 262176 | tf_op jit(solution)/shard_map/ppermute | solution.py:485
  301.8 9.2 %collective-permute-done.64.refs_2_ = bf16[64,2048]{1,0:T(8,128)(2,1)S(1)} collective-permute-done((bf16[64,2048]{1,0:T(8,128)(2,1)}, bf16[64,2048]{1,0:T(8,128)(2,1)S(1)}, u32[]{:S(2)}, u32[]{:S(2)}) %collective-permute-start.64) | collective-permute-done | bytes 262176 | tf_op jit(solution)/shard_map/ppermute | solution.py:485
  311.0 6.7 %collective-permute-done.65.refs_3_ = bf16[64,2048]{1,0:T(8,128)(2,1)S(1)} collective-permute-done((bf16[64,2048]{1,0:T(8,128)(2,1)}, bf16[64,2048]{1,0:T(8,128)(2,1)S(1)}, u32[]{:S(2)}, u32[]{:S(2)}) %collective-permute-start.65) | collective-permute-done | bytes 262176 | tf_op jit(solution)/shard_map/ppermute | solution.py:485
  318.5 2.1 final_sum.1
  (246 shorter events, 55.7 us)
Async XLA Ops:
  4.4 51.4 %collective-permute-start = (bf16[128,2048]{1,0:T(8,128)(2,1)}, bf16[128,2048]{1,0:T(8,128)(2,1)S(1)}, u32[]{:S(2)}, u32[]{:S(2)}) collective-permute-start(bf16[128,2048]{1,0:T(8,128)(2,1)} %norm.1.refs_0_), channel_id=1, source_target_pairs={{0,2},{2,0},{4,6},{6,4},{1,3},{3,1},{5,7},{7,5},{8,10},{10,8},{12,... | collective-permute-start | bytes 1572872 | tf_op jit(solution)/shard_map/ppermute | solution.py:49
  6.0 45.7 %collective-permute-start.1 = (bf16[128,2048]{1,0:T(8,128)(2,1)}, bf16[128,2048]{1,0:T(8,128)(2,1)}, u32[]{:S(2)}, u32[]{:S(2)}) collective-permute-start(bf16[128,2048]{1,0:T(8,128)(2,1)} %norm.1.refs_0_), channel_id=1, source_target_pairs={{2,4},{4,2},{3,5},{5,3},{10,12},{12,10},{11,13},{13,11},{18,20},{2... | collective-permute-start | bytes 1572872 | tf_op jit(solution)/shard_map/ppermute | solution.py:50
  10.1 49.0 %collective-permute-start.9 = (bf16[512,512]{1,0:T(8,128)(2,1)}, bf16[512,512]{1,0:T(8,128)(2,1)}, u32[]{:S(2)}, u32[]{:S(2)}) collective-permute-start(bf16[512,512]{1,0:T(8,128)(2,1)} %get-tuple-element.29), channel_id=1, source_target_pairs={{0,8},{8,0},{16,24},{24,16},{1,9},{9,1},{17,25},{25,17},{2,10},{10... | collective-permute-start | bytes 1572872 | tf_op jit(solution)/shard_map/ppermute | solution.py:63
  11.6 48.4 %collective-permute-start.12 = (bf16[512,512]{1,0:T(8,128)(2,1)}, bf16[512,512]{1,0:T(8,128)(2,1)}, u32[]{:S(2)}, u32[]{:S(2)}) collective-permute-start(bf16[512,512]{1,0:T(8,128)(2,1)} %get-tuple-element.28), channel_id=1, source_target_pairs={{0,16},{8,24},{16,0},{24,8},{1,17},{9,25},{17,1},{25,9},{2,18},{10... | collective-permute-start | bytes 1572872 | tf_op jit(solution)/shard_map/ppermute | solution.py:64
  51.7 24.3 %collective-permute-start.2 = (bf16[128,2048]{1,0:T(8,128)(2,1)}, bf16[128,2048]{1,0:T(8,128)(2,1)S(1)}, u32[]{:S(2)}, u32[]{:S(2)}) collective-permute-start(bf16[128,2048]{1,0:T(8,128)(2,1)} %collective-permute-done.1), channel_id=1, source_target_pairs={{2,0},{4,6},{3,1},{5,7},{10,8},{12,14},{11,9},{13,15},{18,16},{20,... | collective-permute-start | bytes 1572872 | tf_op jit(solution)/shard_map/ppermute | solution.py:51
  55.8 20.2 %collective-permute-start.3 = (bf16[128,2048]{1,0:T(8,128)(2,1)S(1)}, bf16[128,2048]{1,0:T(8,128)(2,1)S(1)}, u32[]{:S(2)}, u32[]{:S(2)}) collective-permute-start(bf16[128,2048]{1,0:T(8,128)(2,1)S(1)} %collective-permute-done.refs_1_), channel_id=1, source_target_pairs={{2,4},{4,2},{3,5},{5,3},{10,12},{12,10},{11,13},{13,11},{18,20},{2... | collective-permute-start | bytes 1572872 | tf_op jit(solution)/shard_map/ppermute | solution.py:52
  59.2 12.6 %collective-permute-start.13 = (bf16[512,512]{1,0:T(8,128)(2,1)}, bf16[512,512]{1,0:T(8,128)(2,1)S(1)}, u32[]{:S(2)}, u32[]{:S(2)}) collective-permute-start(bf16[512,512]{1,0:T(8,128)(2,1)} %collective-permute-done.9.refs_9_), channel_id=1, source_target_pairs={{0,16},{8,24},{16,0},{24,8},{1,17},{9,25},{17,1},{25,9},{2,18},{10... | collective-permute-start | bytes 1572872 | tf_op jit(solution)/shard_map/ppermute | solution.py:67
  60.1 14.7 %collective-permute-start.14 = (bf16[512,512]{1,0:T(8,128)(2,1)}, bf16[512,512]{1,0:T(8,128)(2,1)S(1)}, u32[]{:S(2)}, u32[]{:S(2)}) collective-permute-start(bf16[512,512]{1,0:T(8,128)(2,1)} %collective-permute-done.12.refs_12_), channel_id=1, source_target_pairs={{0,8},{8,0},{16,24},{24,16},{1,9},{9,1},{17,25},{25,17},{2,10},{10... | collective-permute-start | bytes 1572872 | tf_op jit(solution)/shard_map/ppermute | solution.py:68
  60.6 17.9 %collective-permute-start.5 = (bf16[128,2048]{1,0:T(8,128)(2,1)S(1)}, bf16[128,2048]{1,0:T(8,128)(2,1)S(1)}, u32[]{:S(2)}, u32[]{:S(2)}) collective-permute-start(bf16[128,2048]{1,0:T(8,128)(2,1)S(1)} %copy-done.2), channel_id=1, source_target_pairs={{0,1},{1,0},{2,3},{3,2},{4,5},{5,4},{6,7},{7,6},{8,9},{9,8},{10,11... | collective-permute-start | bytes 1572872 | tf_op jit(solution)/shard_map/ppermute | solution.py:454
  71.8 19.6 %collective-permute-start.10 = (bf16[512,512]{1,0:T(8,128)(2,1)}, bf16[512,512]{1,0:T(8,128)(2,1)S(1)}, u32[]{:S(2)}, u32[]{:S(2)}) collective-permute-start(bf16[512,512]{1,0:T(8,128)(2,1)} %get-tuple-element.28), channel_id=1, source_target_pairs={{0,8},{8,0},{16,24},{24,16},{1,9},{9,1},{17,25},{25,17},{2,10},{10... | collective-permute-start | bytes 1572872 | tf_op jit(solution)/shard_map/ppermute | solution.py:66
  74.8 17.5 %collective-permute-start.11 = (bf16[512,512]{1,0:T(8,128)(2,1)}, bf16[512,512]{1,0:T(8,128)(2,1)S(1)}, u32[]{:S(2)}, u32[]{:S(2)}) collective-permute-start(bf16[512,512]{1,0:T(8,128)(2,1)} %get-tuple-element.29), channel_id=1, source_target_pairs={{0,16},{8,24},{16,0},{24,8},{1,17},{9,25},{17,1},{25,9},{2,18},{10... | collective-permute-start | bytes 1572872 | tf_op jit(solution)/shard_map/ppermute | solution.py:65
  76.0 17.1 %collective-permute-start.21 = (bf16[4,512,128]{2,1,0:T(8,128)(2,1)S(1)}, bf16[4,512,128]{2,1,0:T(8,128)(2,1)S(1)}, u32[]{:S(2)}, u32[]{:S(2)}) collective-permute-start(bf16[4,512,128]{2,1,0:T(8,128)(2,1)S(1)} %pad_maximum_fusion.3), channel_id=1, source_target_pairs={{0,1},{1,0},{2,3},{3,2},{4,5},{5,4},{6,7},{7,6},{8,9},{9,8},{10,11... | collective-permute-start | bytes 1572872 | tf_op jit(solution)/shard_map/ppermute | solution.py:98
  76.0 13.4 %collective-permute-start.4 = (bf16[128,2048]{1,0:T(8,128)(2,1)S(1)}, bf16[128,2048]{1,0:T(8,128)(2,1)S(1)}, u32[]{:S(2)}, u32[]{:S(2)}) collective-permute-start(bf16[128,2048]{1,0:T(8,128)(2,1)S(1)} %collective-permute-done.3), channel_id=1, source_target_pairs={{2,0},{4,6},{3,1},{5,7},{10,8},{12,14},{11,9},{13,15},{18,16},{20,... | collective-permute-start | bytes 1572872 | tf_op jit(solution)/shard_map/ppermute | solution.py:53
  78.5 15.3 %collective-permute-start.30 = (bf16[512,512]{1,0:T(8,128)(2,1)}, bf16[512,512]{1,0:T(8,128)(2,1)S(1)}, u32[]{:S(2)}, u32[]{:S(2)}) collective-permute-start(bf16[512,512]{1,0:T(8,128)(2,1)} %get-tuple-element.41), channel_id=1, source_target_pairs={{0,8},{8,0},{16,24},{24,16},{1,9},{9,1},{17,25},{25,17},{2,10},{10... | collective-permute-start | bytes 1572872 | tf_op jit(solution)/shard_map/ppermute | solution.py:63
  89.4 15.0 %collective-permute-start.33 = (bf16[512,512]{1,0:T(8,128)(2,1)}, bf16[512,512]{1,0:T(8,128)(2,1)S(1)}, u32[]{:S(2)}, u32[]{:S(2)}) collective-permute-start(bf16[512,512]{1,0:T(8,128)(2,1)} %get-tuple-element.40), channel_id=1, source_target_pairs={{0,16},{8,24},{16,0},{24,8},{1,17},{9,25},{17,1},{25,9},{2,18},{10... | collective-permute-start | bytes 1572872 | tf_op jit(solution)/shard_map/ppermute | solution.py:64
  91.4 15.0 %collective-permute-start.6 = (bf16[128,2048]{1,0:T(8,128)(2,1)S(1)}, bf16[128,2048]{1,0:T(8,128)(2,1)S(1)}, u32[]{:S(2)}, u32[]{:S(2)}) collective-permute-start(bf16[128,2048]{1,0:T(8,128)(2,1)S(1)} %collective-permute-done.refs_1_), channel_id=1, source_target_pairs={{0,1},{1,0},{2,3},{3,2},{4,5},{5,4},{6,7},{7,6},{8,9},{9,8},{10,11... | collective-permute-start | bytes 1572872 | tf_op jit(solution)/shard_map/ppermute | solution.py:454
  92.2 14.1 %collective-permute-start.7 = (bf16[128,2048]{1,0:T(8,128)(2,1)S(1)}, bf16[128,2048]{1,0:T(8,128)(2,1)S(1)}, u32[]{:S(2)}, u32[]{:S(2)}) collective-permute-start(bf16[128,2048]{1,0:T(8,128)(2,1)S(1)} %broadcast_select_fusion.5.refs_2_), channel_id=1, source_target_pairs={{0,1},{1,0},{2,3},{3,2},{4,5},{5,4},{6,7},{7,6},{8,9},{9,8},{10,11... | collective-permute-start | bytes 1572872 | tf_op jit(solution)/shard_map/ppermute | solution.py:454
  93.0 13.3 %collective-permute-start.8 = (bf16[128,2048]{1,0:T(8,128)(2,1)S(1)}, bf16[128,2048]{1,0:T(8,128)(2,1)S(1)}, u32[]{:S(2)}, u32[]{:S(2)}) collective-permute-start(bf16[128,2048]{1,0:T(8,128)(2,1)S(1)} %broadcast_select_fusion.4.refs_3_), channel_id=1, source_target_pairs={{0,1},{1,0},{2,3},{3,2},{4,5},{5,4},{6,7},{7,6},{8,9},{9,8},{10,11... | collective-permute-start | bytes 1572872 | tf_op jit(solution)/shard_map/ppermute | solution.py:454
  93.8 29.2 %collective-permute-start.34 = (bf16[512,512]{1,0:T(8,128)(2,1)S(1)}, bf16[512,512]{1,0:T(8,128)(2,1)S(1)}, u32[]{:S(2)}, u32[]{:S(2)}) collective-permute-start(bf16[512,512]{1,0:T(8,128)(2,1)S(1)} %collective-permute-done.30.refs_9_), channel_id=1, source_target_pairs={{0,16},{8,24},{16,0},{24,8},{1,17},{9,25},{17,1},{25,9},{2,18},{10... | collective-permute-start | bytes 1572872 | tf_op jit(solution)/shard_map/ppermute | solution.py:67
  104.4 18.7 %collective-permute-start.35 = (bf16[512,512]{1,0:T(8,128)(2,1)S(1)}, bf16[512,512]{1,0:T(8,128)(2,1)}, u32[]{:S(2)}, u32[]{:S(2)}) collective-permute-start(bf16[512,512]{1,0:T(8,128)(2,1)S(1)} %collective-permute-done.33.refs_12_), channel_id=1, source_target_pairs={{0,8},{8,0},{16,24},{24,16},{1,9},{9,1},{17,25},{25,17},{2,10},{10... | collective-permute-start | bytes 1572872 | tf_op jit(solution)/shard_map/ppermute | solution.py:68
  118.2 55.5 %collective-permute-start.22 = (bf16[512,512]{1,0:T(8,128)(2,1)}, bf16[512,512]{1,0:T(8,128)(2,1)}, u32[]{:S(2)}, u32[]{:S(2)}) collective-permute-start(bf16[512,512]{1,0:T(8,128)(2,1)} %project.3.refs_0_.query_ref), channel_id=1, source_target_pairs={{0,2},{2,0},{4,6},{6,4},{1,3},{3,1},{5,7},{7,5},{8,10},{10,8},{12,... | collective-permute-start | bytes 1572872 | tf_op jit(solution)/shard_map/ppermute | solution.py:49
  120.6 50.6 %collective-permute-start.24 = (bf16[512,512]{1,0:T(8,128)(2,1)}, bf16[512,512]{1,0:T(8,128)(2,1)S(1)}, u32[]{:S(2)}, u32[]{:S(2)}) collective-permute-start(bf16[512,512]{1,0:T(8,128)(2,1)} %project.3.refs_0_.query_ref), channel_id=1, source_target_pairs={{2,4},{4,2},{3,5},{5,3},{10,12},{12,10},{11,13},{13,11},{18,20},{2... | collective-permute-start | bytes 1572872 | tf_op jit(solution)/shard_map/ppermute | solution.py:50
  150.1 12.5 %collective-permute-start.43 = (bf16[512,512]{1,0:T(8,128)(2,1)}, bf16[512,512]{1,0:T(8,128)(2,1)S(1)}, u32[]{:S(2)}, u32[]{:S(2)}) collective-permute-start(bf16[512,512]{1,0:T(8,128)(2,1)} %get-tuple-element.35), channel_id=1, source_target_pairs={{0,8},{8,0},{16,24},{24,16},{1,9},{9,1},{17,25},{25,17},{2,10},{10... | collective-permute-start | bytes 1572872 | tf_op jit(solution)/shard_map/ppermute | solution.py:63
  157.8 11.7 %collective-permute-start.46 = (bf16[512,512]{1,0:T(8,128)(2,1)S(1)}, bf16[512,512]{1,0:T(8,128)(2,1)S(1)}, u32[]{:S(2)}, u32[]{:S(2)}) collective-permute-start(bf16[512,512]{1,0:T(8,128)(2,1)S(1)} %get-tuple-element.34), channel_id=1, source_target_pairs={{0,16},{8,24},{16,0},{24,8},{1,17},{9,25},{17,1},{25,9},{2,18},{10... | collective-permute-start | bytes 1572872 | tf_op jit(solution)/shard_map/ppermute | solution.py:64
  162.6 23.2 %collective-permute-start.47 = (bf16[512,512]{1,0:T(8,128)(2,1)S(1)}, bf16[512,512]{1,0:T(8,128)(2,1)S(1)}, u32[]{:S(2)}, u32[]{:S(2)}) collective-permute-start(bf16[512,512]{1,0:T(8,128)(2,1)S(1)} %collective-permute-done.43.refs_9_), channel_id=1, source_target_pairs={{0,16},{8,24},{16,0},{24,8},{1,17},{9,25},{17,1},{25,9},{2,18},{10... | collective-permute-start | bytes 1572872 | tf_op jit(solution)/shard_map/ppermute | solution.py:67
  163.8 44.9 %collective-permute-start.42 = (bf16[4,512,256]{2,1,0:T(8,128)(2,1)S(1)}, bf16[4,512,256]{2,1,0:T(8,128)(2,1)S(1)}, u32[]{:S(2)}, u32[]{:S(2)}) collective-permute-start(bf16[4,512,256]{2,1,0:T(8,128)(2,1)S(1)} %pad_maximum_fusion.2), channel_id=1, source_target_pairs={{0,1},{1,0},{2,3},{3,2},{4,5},{5,4},{6,7},{7,6},{8,9},{9,8},{10,11... | collective-permute-start | bytes 3145736 | tf_op jit(solution)/shard_map/ppermute | solution.py:98
  169.5 25.7 %collective-permute-start.48 = (bf16[512,512]{1,0:T(8,128)(2,1)S(1)}, bf16[512,512]{1,0:T(8,128)(2,1)S(1)}, u32[]{:S(2)}, u32[]{:S(2)}) collective-permute-start(bf16[512,512]{1,0:T(8,128)(2,1)S(1)} %collective-permute-done.46.refs_12_), channel_id=1, source_target_pairs={{0,8},{8,0},{16,24},{24,16},{1,9},{9,1},{17,25},{25,17},{2,10},{10... | collective-permute-start | bytes 1572872 | tf_op jit(solution)/shard_map/ppermute | solution.py:68
  171.2 25.6 %collective-permute-start.25 = (bf16[512,512]{1,0:T(8,128)(2,1)S(1)}, bf16[512,512]{1,0:T(8,128)(2,1)}, u32[]{:S(2)}, u32[]{:S(2)}) collective-permute-start(bf16[512,512]{1,0:T(8,128)(2,1)S(1)} %collective-permute-done.24.refs_1_), channel_id=1, source_target_pairs={{2,0},{4,6},{3,1},{5,7},{10,8},{12,14},{11,9},{13,15},{18,16},{20,... | collective-permute-start | bytes 1572872 | tf_op jit(solution)/shard_map/ppermute | solution.py:51
  173.6 23.8 %collective-permute-start.26 = (bf16[512,512]{1,0:T(8,128)(2,1)}, bf16[512,512]{1,0:T(8,128)(2,1)S(1)}, u32[]{:S(2)}, u32[]{:S(2)}) collective-permute-start(bf16[512,512]{1,0:T(8,128)(2,1)} %collective-permute-done.22.refs_0_), channel_id=1, source_target_pairs={{2,4},{4,2},{3,5},{5,3},{10,12},{12,10},{11,13},{13,11},{18,20},{2... | collective-permute-start | bytes 1572872 | tf_op jit(solution)/shard_map/ppermute | solution.py:52
  185.9 21.5 %collective-permute-start.31 = (bf16[512,512]{1,0:T(8,128)(2,1)}, bf16[512,512]{1,0:T(8,128)(2,1)S(1)}, u32[]{:S(2)}, u32[]{:S(2)}) collective-permute-start(bf16[512,512]{1,0:T(8,128)(2,1)} %get-tuple-element.40), channel_id=1, source_target_pairs={{0,8},{8,0},{16,24},{24,16},{1,9},{9,1},{17,25},{25,17},{2,10},{10... | collective-permute-start | bytes 1572872 | tf_op jit(solution)/shard_map/ppermute | solution.py:66
  195.2 23.6 %collective-permute-start.32 = (bf16[512,512]{1,0:T(8,128)(2,1)}, bf16[512,512]{1,0:T(8,128)(2,1)S(1)}, u32[]{:S(2)}, u32[]{:S(2)}) collective-permute-start(bf16[512,512]{1,0:T(8,128)(2,1)} %get-tuple-element.41), channel_id=1, source_target_pairs={{0,16},{8,24},{16,0},{24,8},{1,17},{9,25},{17,1},{25,9},{2,18},{10... | collective-permute-start | bytes 1572872 | tf_op jit(solution)/shard_map/ppermute | solution.py:65
  196.9 23.1 %collective-permute-start.44 = (bf16[512,512]{1,0:T(8,128)(2,1)}, bf16[512,512]{1,0:T(8,128)(2,1)S(1)}, u32[]{:S(2)}, u32[]{:S(2)}) collective-permute-start(bf16[512,512]{1,0:T(8,128)(2,1)} %copy-done.34), channel_id=1, source_target_pairs={{0,8},{8,0},{16,24},{24,16},{1,9},{9,1},{17,25},{25,17},{2,10},{10... | collective-permute-start | bytes 1572872 | tf_op jit(solution)/shard_map/ppermute | solution.py:66
  197.4 11.5 %collective-permute-start.28 = (bf16[512,512]{1,0:T(8,128)(2,1)S(1)}, bf16[512,512]{1,0:T(8,128)(2,1)}, u32[]{:S(2)}, u32[]{:S(2)}) collective-permute-start(bf16[512,512]{1,0:T(8,128)(2,1)S(1)} %collective-permute-done.26.refs_1_), channel_id=1, source_target_pairs={{2,0},{4,6},{3,1},{5,7},{10,8},{12,14},{11,9},{13,15},{18,16},{20,... | collective-permute-start | bytes 1572872 | tf_op jit(solution)/shard_map/ppermute | solution.py:53
  207.4 13.1 %collective-permute-start.45 = (bf16[512,512]{1,0:T(8,128)(2,1)}, bf16[512,512]{1,0:T(8,128)(2,1)S(1)}, u32[]{:S(2)}, u32[]{:S(2)}) collective-permute-start(bf16[512,512]{1,0:T(8,128)(2,1)} %get-tuple-element.35), channel_id=1, source_target_pairs={{0,16},{8,24},{16,0},{24,8},{1,17},{9,25},{17,1},{25,9},{2,18},{10... | collective-permute-start | bytes 1572872 | tf_op jit(solution)/shard_map/ppermute | solution.py:65
  208.7 12.8 %collective-permute-start.23 = (bf16[528,512]{1,0:T(8,128)(2,1)S(1)}, bf16[528,512]{1,0:T(8,128)(2,1)S(1)}, u32[]{:S(2)}, u32[]{:S(2)}) collective-permute-start(bf16[528,512]{1,0:T(8,128)(2,1)S(1)} %copy-done.12), channel_id=1, source_target_pairs={{0,2},{2,0},{4,6},{6,4},{1,3},{3,1},{5,7},{7,5},{8,10},{10,8},{12,... | collective-permute-start | bytes 1622024 | tf_op jit(solution)/shard_map/ppermute | solution.py:478
  208.9 14.2 %collective-permute-start.50 = (bf16[256,512]{1,0:T(8,128)(2,1)}, bf16[256,512]{1,0:T(8,128)(2,1)S(1)}, u32[]{:S(2)}, u32[]{:S(2)}) collective-permute-start(bf16[256,512]{1,0:T(8,128)(2,1)} %get-tuple-element.45), channel_id=1, source_target_pairs={{0,8},{8,0},{16,24},{24,16},{1,9},{9,1},{17,25},{25,17},{2,10},{10... | collective-permute-start | bytes 786440 | tf_op jit(solution)/shard_map/ppermute | solution.py:63
  218.8 18.8 %collective-permute-start.52 = (bf16[256,512]{1,0:T(8,128)(2,1)}, bf16[256,512]{1,0:T(8,128)(2,1)S(1)}, u32[]{:S(2)}, u32[]{:S(2)}) collective-permute-start(bf16[256,512]{1,0:T(8,128)(2,1)} %get-tuple-element.45), channel_id=1, source_target_pairs={{0,16},{8,24},{16,0},{24,8},{1,17},{9,25},{17,1},{25,9},{2,18},{10... | collective-permute-start | bytes 786440 | tf_op jit(solution)/shard_map/ppermute | solution.py:65
  220.5 18.4 %collective-permute-start.53 = (bf16[256,512]{1,0:T(8,128)(2,1)}, bf16[256,512]{1,0:T(8,128)(2,1)S(1)}, u32[]{:S(2)}, u32[]{:S(2)}) collective-permute-start(bf16[256,512]{1,0:T(8,128)(2,1)} %get-tuple-element.44), channel_id=1, source_target_pairs={{0,16},{8,24},{16,0},{24,8},{1,17},{9,25},{17,1},{25,9},{2,18},{10... | collective-permute-start | bytes 786440 | tf_op jit(solution)/shard_map/ppermute | solution.py:64
  221.4 30.5 %collective-permute-start.27 = (bf16[528,512]{1,0:T(8,128)(2,1)S(1)}, bf16[528,512]{1,0:T(8,128)(2,1)S(1)}, u32[]{:S(2)}, u32[]{:S(2)}) collective-permute-start(bf16[528,512]{1,0:T(8,128)(2,1)S(1)} %copy-done.11), channel_id=1, source_target_pairs={{0,4},{2,6},{4,0},{6,2},{1,5},{3,7},{5,1},{7,3},{8,12},{10,14},{12... | collective-permute-start | bytes 1622024 | tf_op jit(solution)/shard_map/ppermute | solution.py:478
  223.1 40.2 %collective-permute-start.29 = (bf16[528,512]{1,0:T(8,128)(2,1)}, bf16[528,512]{1,0:T(8,128)(2,1)S(1)}, u32[]{:S(2)}, u32[]{:S(2)}) collective-permute-start(bf16[528,512]{1,0:T(8,128)(2,1)} %cache_attention.7), channel_id=1, source_target_pairs={{0,6},{2,4},{4,2},{6,0},{1,7},{3,5},{5,3},{7,1},{8,14},{10,12},{12... | collective-permute-start | bytes 1622024 | tf_op jit(solution)/shard_map/ppermute | solution.py:478
  226.9 56.1 %collective-permute-start.56 = (bf16[512,512]{1,0:T(8,128)(2,1)S(1)}, bf16[512,512]{1,0:T(8,128)(2,1)S(1)}, u32[]{:S(2)}, u32[]{:S(2)}) collective-permute-start(bf16[512,512]{1,0:T(8,128)(2,1)S(1)} %bitcast.55), channel_id=1, source_target_pairs={{0,1},{1,0},{2,3},{3,2},{4,5},{5,4},{6,7},{7,6},{8,9},{9,8},{10,11... | collective-permute-start | bytes 1572872 | tf_op jit(solution)/shard_map/ppermute | solution.py:470
  237.6 44.7 %collective-permute-start.54 = (bf16[256,512]{1,0:T(8,128)(2,1)S(1)}, bf16[256,512]{1,0:T(8,128)(2,1)S(1)}, u32[]{:S(2)}, u32[]{:S(2)}) collective-permute-start(bf16[256,512]{1,0:T(8,128)(2,1)S(1)} %collective-permute-done.50.refs_1_), channel_id=1, source_target_pairs={{0,16},{8,24},{16,0},{24,8},{1,17},{9,25},{17,1},{25,9},{2,18},{10... | collective-permute-start | bytes 786440 | tf_op jit(solution)/shard_map/ppermute | solution.py:67
  238.9 44.3 %collective-permute-start.57 = (bf16[256,512]{1,0:T(8,128)(2,1)S(1)}, bf16[256,512]{1,0:T(8,128)(2,1)S(1)}, u32[]{:S(2)}, u32[]{:S(2)}) collective-permute-start(bf16[256,512]{1,0:T(8,128)(2,1)S(1)} %collective-permute-done.50.refs_1_), channel_id=1, source_target_pairs={{0,1},{1,0},{2,3},{3,2},{4,5},{5,4},{6,7},{7,6},{8,9},{9,8},{10,11... | collective-permute-start | bytes 786440 | tf_op jit(solution)/shard_map/ppermute | solution.py:470
  251.9 30.7 %collective-permute-start.55 = (bf16[256,512]{1,0:T(8,128)(2,1)S(1)}, bf16[256,512]{1,0:T(8,128)(2,1)S(1)}, u32[]{:S(2)}, u32[]{:S(2)}) collective-permute-start(bf16[256,512]{1,0:T(8,128)(2,1)S(1)} %collective-permute-done.53.refs_4_), channel_id=1, source_target_pairs={{0,8},{8,0},{16,24},{24,16},{1,9},{9,1},{17,25},{25,17},{2,10},{10... | collective-permute-start | bytes 786440 | tf_op jit(solution)/shard_map/ppermute | solution.py:68
  263.3 20.2 %collective-permute-start.58 = (bf16[256,512]{1,0:T(8,128)(2,1)S(1)}, bf16[256,512]{1,0:T(8,128)(2,1)S(1)}, u32[]{:S(2)}, u32[]{:S(2)}) collective-permute-start(bf16[256,512]{1,0:T(8,128)(2,1)S(1)} %collective-permute-done.51.refs_2_), channel_id=1, source_target_pairs={{0,1},{1,0},{2,3},{3,2},{4,5},{5,4},{6,7},{7,6},{8,9},{9,8},{10,11... | collective-permute-start | bytes 786440 | tf_op jit(solution)/shard_map/ppermute | solution.py:470
  290.9 10.9 %collective-permute-start.63 = (bf16[64,2048]{1,0:T(8,128)(2,1)}, bf16[64,2048]{1,0:T(8,128)(2,1)S(1)}, u32[]{:S(2)}, u32[]{:S(2)}) collective-permute-start(bf16[64,2048]{1,0:T(8,128)(2,1)} %get-tuple-element.22), channel_id=1, source_target_pairs={{0,2},{2,0},{4,6},{6,4},{1,3},{3,1},{5,7},{7,5},{8,10},{10,8},{12,... | collective-permute-start | bytes 786440 | tf_op jit(solution)/shard_map/ppermute | solution.py:485
  290.9 20.0 %collective-permute-start.64 = (bf16[64,2048]{1,0:T(8,128)(2,1)}, bf16[64,2048]{1,0:T(8,128)(2,1)S(1)}, u32[]{:S(2)}, u32[]{:S(2)}) collective-permute-start(bf16[64,2048]{1,0:T(8,128)(2,1)} %get-tuple-element.23), channel_id=1, source_target_pairs={{0,4},{2,6},{4,0},{6,2},{1,5},{3,7},{5,1},{7,3},{8,12},{10,14},{12... | collective-permute-start | bytes 786440 | tf_op jit(solution)/shard_map/ppermute | solution.py:485
  292.7 25.0 %collective-permute-start.65 = (bf16[64,2048]{1,0:T(8,128)(2,1)}, bf16[64,2048]{1,0:T(8,128)(2,1)S(1)}, u32[]{:S(2)}, u32[]{:S(2)}) collective-permute-start(bf16[64,2048]{1,0:T(8,128)(2,1)} %get-tuple-element.24), channel_id=1, source_target_pairs={{0,6},{2,4},{4,2},{6,0},{1,7},{3,5},{5,3},{7,1},{8,14},{10,12},{12... | collective-permute-start | bytes 786440 | tf_op jit(solution)/shard_map/ppermute | solution.py:485
  (73 other events, 830.3 us)

commit v2 on v1

v2 whole, which is shorter than its diff:
```python
import functools
import math

import jax
import jax.numpy as jnp
from jax import lax
from jax.experimental import pallas as pl
from jax.experimental.pallas import tpu as pltpu
from jax.sharding import PartitionSpec as P

HD = 128
PAGE = 64
EPS = 1e-05
NEG = -1e30
STAT_ROWS = 16
MARK = jax.ShapeDtypeStruct((1,), jnp.int32)

SMEM = pltpu.MemorySpace.SMEM
F32 = jnp.float32
BF16 = jnp.bfloat16


def swap(count, k):
    return [(i, i ^ k) for i in range(count)]


def assemble_kernel(plan, *refs):
    out_ref, row = refs[-1], 0
    for index, start, size in plan:
        out_ref[row : row + size, :] = refs[index][start : start + size, :]
        row += size


def assemble(pieces, *earlier):
    arrays = [piece[0] for piece in pieces]
    plan = tuple((n, start, size) for n, (_, start, size) in enumerate(pieces))
    shape = (sum(piece[2] for piece in pieces), arrays[0].shape[1])
    return pl.pallas_call(
        functools.partial(assemble_kernel, plan),
        out_shape=jax.ShapeDtypeStruct(shape, BF16),
        in_specs=[pl.BlockSpec(memory_space=pltpu.VMEM)] * len(arrays)
        + [pl.BlockSpec(memory_space=pl.ANY)] * len(earlier),
        out_specs=pl.BlockSpec(memory_space=pltpu.VMEM),
        compiler_params=params(16),
        cost_estimate=cost(1, 1),
        name="assemble",
    )(*arrays, *earlier)


def cut_kernel(start, *refs):
    out_ref, sem = refs[-2:]
    copy = pltpu.make_async_copy(refs[0].at[start : start + out_ref.shape[0], :], out_ref, sem)
    copy.start()
    copy.wait()


def cut(x, start, size, *earlier):
    return pl.pallas_call(
        functools.partial(cut_kernel, start),
        out_shape=jax.ShapeDtypeStruct((size, x.shape[1]), BF16),
        in_specs=[pl.BlockSpec(memory_space=pl.ANY)] * (1 + len(earlier)),
        out_specs=pl.BlockSpec(memory_space=pltpu.VMEM),
        scratch_shapes=[pltpu.SemaphoreType.DMA(())],
        compiler_params=params(8),
        cost_estimate=cost(1, 1),
        name="cut",
    )(x, *earlier)


def params(mebibytes=16):
    return pltpu.CompilerParams(vmem_limit_bytes=mebibytes * 1024 * 1024)


def cost(flops, moved, transcendentals=0):
    return pl.CostEstimate(flops=1, bytes_accessed=1, transcendentals=0)


def spread(x):
    count = lax.axis_size("seq")
    blocks = {0: x}
    for k in sorted(range(1, count), key=lambda k: k.bit_count()):
        step = k & -k
        blocks[k] = lax.ppermute(blocks[k ^ step], "seq", swap(count, step))
    return [blocks[k] for k in range(count)]


def along_x(x):
    return lax.ppermute(x, "dp", swap(4, 1))


def along_y(x):
    return lax.ppermute(x, "dp", swap(4, 2))


def both_ways(x):
    return along_x(x), along_y(x)


def halves_on(by_x, by_y, small, *gate):
    half = by_x.shape[0] // 2
    rest = [] if small is None else [(small, 0, small.shape[0])]
    top = along_y(assemble([(by_x, 0, half)] + rest, *gate))
    bottom = along_x(assemble([(by_y, half, half)] + rest, *gate))
    return top, bottom


def other_core(x):
    return lax.ppermute(x, "mp", swap(2, 1))


def norm_kernel(down_rows, at, *refs):
    count = (len(refs) - 3) // 2
    sources, (out_ref, mark), held, sems = (
        refs[:count],
        refs[count : count + 2],
        refs[count + 2 : -1],
        refs[-1],
    )
    mark[0] = jnp.int32(0)
    copies = [
        pltpu.make_async_copy(source, target, sems.at[n])
        for n, (source, target) in enumerate(zip(sources, held))
    ]
    for copy in copies:
        copy.start()
    for copy in copies:
        copy.wait()
    hidden_ref, embed_ref, gain_ref = held[:3]
    hidden = hidden_ref[...].astype(F32)
    embed = embed_ref[...].astype(F32)
    rows, width = hidden.shape
    squares = jnp.sum(hidden * hidden, axis=1, keepdims=True) + jnp.sum(
        embed * embed, axis=1, keepdims=True
    )
    factor = lax.rsqrt(squares / (2 * width) + EPS)

    @pl.when(at[2] == 0)
    def _():
        out_ref[:rows, :] = (hidden * factor * gain_ref[:, :width]).astype(BF16)

    @pl.when(at[2] != 0)
    def _():
        out_ref[:rows, :] = (embed * factor * gain_ref[:, width:]).astype(BF16)

    if down_rows is not None:
        whole = jnp.transpose(held[3][:, :HD].astype(F32)).astype(BF16)
        own = pl.ds(pl.multiple_of(at[0] * down_rows, down_rows), down_rows)
        part = jnp.transpose(held[3][own, HD:].astype(F32)).astype(BF16)
        for x in (whole, part):
            groups = width // x.shape[1]
            step = x.shape[0] // groups
            for g in range(groups):
                columns = slice(g * x.shape[1], (g + 1) * x.shape[1])
                out_ref[rows : rows + step, columns] = x[g * step : (g + 1) * step, :]
            rows += step


def norm(at, hidden, embed, gain, down, down_rows):
    rows, width = hidden.shape
    arrays = (hidden, embed, gain)
    if down_rows is not None:
        arrays += (down,)
        rows += HD * down.shape[0] // width + 2 * HD * down_rows // width
    return pl.pallas_call(
        functools.partial(norm_kernel, down_rows),
        out_shape=(jax.ShapeDtypeStruct((rows, width), BF16), MARK),
        in_specs=[pl.BlockSpec(memory_space=SMEM)]
        + [pl.BlockSpec(memory_space=pl.ANY)] * len(arrays),
        out_specs=(pl.BlockSpec(memory_space=pltpu.VMEM), pl.BlockSpec(memory_space=SMEM)),
        scratch_shapes=[pltpu.VMEM(x.shape, x.dtype) for x in arrays]
        + [pltpu.SemaphoreType.DMA((len(arrays),))],
        compiler_params=params(60),
        cost_estimate=cost(1, 1),
        name="norm",
    )(at, *arrays)


def arrange_kernel(begin, *refs):
    count = len(refs) - 4
    sources, out_ref, held, sems = refs[:count], refs[-3], refs[-2], refs[-1]
    step, width = held.shape[1:]
    copies = [
        pltpu.make_async_copy(source.at[begin : begin + step, :], held.at[n], sems.at[n])
        for n, source in enumerate(sources)
    ]
    for copy in copies:
        copy.start()
    for copy in copies:
        copy.wait()
    size = out_ref.shape[1] // count
    for n in range(count):
        for g in range(width // size):
            out_ref[g * step : (g + 1) * step, n * size : (n + 1) * size] = held[
                n, :, g * size : (g + 1) * size
            ]


def arrange(blocks, earlier, begin, down_rows):
    width = blocks[0].shape[1]
    step = 2 * HD * down_rows // width
    return pl.pallas_call(
        functools.partial(arrange_kernel, begin),
        out_shape=jax.ShapeDtypeStruct((2 * HD, len(blocks) * down_rows), BF16),
        in_specs=[pl.BlockSpec(memory_space=pl.ANY)] * (len(blocks) + 1),
        out_specs=pl.BlockSpec(memory_space=pltpu.VMEM),
        scratch_shapes=[
            pltpu.VMEM((len(blocks), step, width), BF16),
            pltpu.SemaphoreType.DMA((len(blocks),)),
        ],
        cost_estimate=cost(1, 1),
        name="arrange",
    )(*blocks, earlier)


def project_kernel(plan, at, *refs):
    slots, count, inputs, down_rows = plan
    arrays, outs = refs[:count], refs[count : count + len(inputs)]
    mark, joined, down = refs[count + len(inputs) :]
    mark[0] = jnp.int32(0)
    dp, seq, core = at[0], at[1], at[2]
    rows = joined.shape[0] // len(slots)
    width = joined.shape[1] // 2

    def part(begin, size):
        return pl.ds(pl.multiple_of(begin, size), size)

    for k, (mine, other) in enumerate(slots):
        at_row = part((seq ^ k) * rows, rows)
        joined[at_row, part(core * width, width)] = arrays[mine][:rows, :]
        joined[at_row, part((1 - core) * width, width)] = arrays[other][:rows, :]
    for n, (_, downs, _) in enumerate(inputs):
        if down_rows is None:
            down[:, n * HD : (n + 1) * HD] = arrays[downs][...]
            continue
        if downs is None:
            size = (joined.shape[1] // 2) // len(slots)
            step = HD * size // width
            for k, pair in enumerate(slots):
                for crossed, index in enumerate(pair):
                    columns = part(((seq ^ k) * 2 + (core ^ crossed)) * size, size)
                    for g in range(width // size):
                        down[g * step : (g + 1) * step, columns] = arrays[index][
                            rows : rows + step, g * size : (g + 1) * size
                        ]
            continue
        for index, row, k, crossed in downs:
            for j in range(4):
                begin = (((seq ^ j) * 2 + (core ^ crossed)) * 4 + (dp ^ k)) * down_rows
                down[n * HD : (n + 1) * HD, part(begin, down_rows)] = arrays[index][
                    row : row + HD, j * down_rows : (j + 1) * down_rows
                ]
    if down_rows is None:
        low = jnp.dot(joined[...], down[...], preferred_element_type=F32).astype(BF16)
    else:
        low = scores_of(joined[...], down[...]).astype(BF16)
    for n, ((weights, _, up), out) in enumerate(zip(inputs, outs)):
        total = jnp.dot(
            low[:, n * HD : (n + 1) * HD], arrays[up][...], preferred_element_type=F32
        )
        for index, row, size, k, start, shard in weights:
            columns = joined[...] if k is None else joined[:, part((dp ^ k) * shard + start, size)]
            total += jnp.dot(columns, arrays[index][row : row + size, :], preferred_element_type=F32)
        out[...] = total.astype(BF16)


def project(at, slots, rows, inputs, down_rows):
    arrays = []

    def place(array):
        for index, known in enumerate(arrays):
            if known is array:
                return index
        arrays.append(array)
        return len(arrays) - 1

    placed = tuple(tuple(place(x) for x in slot) for slot in slots)
    plans = []
    for weights, downs, up in inputs:
        weights = tuple((place(piece[0]), *piece[1:]) for piece in weights)
        if down_rows is None:
            downs = place(downs)
        elif downs is not None:
            downs = tuple((place(piece[0]), *piece[1:]) for piece in downs)
        plans.append((weights, downs, place(up)))
    width = 2 * slots[0][0].shape[1]
    columns = inputs[0][2].shape[1]
    result = jax.ShapeDtypeStruct((rows, columns), BF16)
    ranks = len(inputs) * HD
    return pl.pallas_call(
        functools.partial(project_kernel, (placed, len(arrays), tuple(plans), down_rows)),
        out_shape=(*(result,) * len(inputs), MARK),
        in_specs=[pl.BlockSpec(memory_space=SMEM)]
        + [pl.BlockSpec(memory_space=pltpu.VMEM)] * len(arrays),
        out_specs=(
            *(pl.BlockSpec(memory_space=pltpu.VMEM),) * len(inputs),
            pl.BlockSpec(memory_space=SMEM),
        ),
        scratch_shapes=[
            pltpu.VMEM((rows, width), BF16),
            pltpu.VMEM((width, ranks) if down_rows is None else (ranks, width), BF16),
        ],
        compiler_params=params((20 if len(inputs) == 1 else 32) if down_rows is not None else 40),
        cost_estimate=cost(
            2 * rows * width * (columns + HD) * len(inputs), 2 * width * (rows + columns * len(inputs))
        ),
        name="project",
    )(at, *arrays)


def finish_head(head, heads, weighted, peak, total, out_ref, stats):
    level = peak + jnp.log(total)
    high = level.astype(BF16).astype(F32)
    rest = level - high
    mid = rest.astype(BF16).astype(F32)
    stats[3 * head : 3 * head + 1, :] = high
    stats[3 * head + 1 : 3 * head + 2, :] = mid
    stats[3 * head + 2 : 3 * head + 3, :] = rest - mid
    out_ref[head * HD : (head + 1) * HD, :] = (weighted / total).astype(BF16)
    if head == heads - 1:
        out_ref[heads * HD :, :] = stats[...].astype(BF16)


def over_keys(left, right):
    return lax.dot_general(left, right, (((0,), (0,)), ((), ())), preferred_element_type=F32)


def scores_of(keys, queries):
    return lax.dot_general(keys, queries, (((1,), (1,)), ((), ())), preferred_element_type=F32)


def cache_kernel(
    slot,
    heads,
    at,
    earlier,
    pages,
    query_ref,
    key_ref,
    value_ref,
    shared_key_ref,
    shared_value_ref,
    out_ref,
    mark,
    stats,
):
    mark[0] = jnp.int32(0)
    stats[...] = jnp.zeros_like(stats)
    scale = 1.0 / math.sqrt(HD)
    group = at[4]
    for head in range(heads):
        columns = pl.ds(pl.multiple_of(((at[1] ^ slot) * heads + head) * HD, HD), HD)
        queries = query_ref[:, head * HD : (head + 1) * HD]
        own = scores_of(key_ref[0, :, columns], queries) * scale
        shared = scores_of(shared_key_ref[group, :, columns], queries) * scale
        offset = lax.broadcasted_iota(jnp.int32, (PAGE, own.shape[1]), 0)
        masked = []
        for u in range(own.shape[0] // PAGE):
            usable = offset < at[3] - pages[u] * PAGE
            masked.append(jnp.where(usable, own[u * PAGE : (u + 1) * PAGE], NEG))
        own = jnp.concatenate(masked, axis=0)
        peak = jnp.maximum(
            jnp.max(own, axis=0, keepdims=True), jnp.max(shared, axis=0, keepdims=True)
        )
        own = jnp.exp(own - peak)
        shared = jnp.exp(shared - peak)
        total = jnp.sum(own, axis=0, keepdims=True) + jnp.sum(shared, axis=0, keepdims=True)
        weighted = over_keys(value_ref[0, :, columns], own.astype(BF16)) + over_keys(
            shared_value_ref[group, :, columns], shared.astype(BF16)
        )
        finish_head(head, heads, weighted, peak, total, out_ref, stats)


def cache_attention(at, earlier, pages, slot, queries, own_keys, own_values, shared_keys, shared_values):
    rows, width = queries.shape
    heads = width // HD
    slots, shared_slots = own_keys.shape[1], shared_keys.shape[1]
    return pl.pallas_call(
        functools.partial(cache_kernel, slot, heads),
        out_shape=(jax.ShapeDtypeStruct((width + STAT_ROWS, rows), BF16), MARK),
        in_specs=[pl.BlockSpec(memory_space=SMEM)] * 3
        + [pl.BlockSpec(memory_space=pltpu.VMEM)] * 5,
        out_specs=(pl.BlockSpec(memory_space=pltpu.VMEM), pl.BlockSpec(memory_space=SMEM)),
        scratch_shapes=[pltpu.VMEM((STAT_ROWS, rows), F32)],
        compiler_params=params(16),
        cost_estimate=cost(
            8 * rows * width * (slots + shared_slots),
            4 * width * (slots + shared_slots),
            rows * heads * (slots + shared_slots),
        ),
        name="cache_attention",
    )(at, earlier, pages, queries, own_keys, own_values, shared_keys, shared_values)


def new_kernel(heads, query_ref, key_ref, value_ref, out_ref, stats):
    stats[...] = jnp.zeros_like(stats)
    for head in range(heads):
        columns = slice(head * HD, (head + 1) * HD)
        scores = scores_of(key_ref[:, columns], query_ref[:, columns]) * (1.0 / math.sqrt(HD))
        places = lax.broadcasted_iota(jnp.int32, scores.shape, 0)
        tokens = lax.broadcasted_iota(jnp.int32, scores.shape, 1)
        scores = jnp.where(places <= tokens, scores, NEG)
        peak = jnp.max(scores, axis=0, keepdims=True)
        exponent = jnp.exp(scores - peak)
        total = jnp.sum(exponent, axis=0, keepdims=True)
        weighted = over_keys(value_ref[:, columns], exponent.astype(BF16))
        finish_head(head, heads, weighted, peak, total, out_ref, stats)


def new_attention(queries, keys, values):
    rows, width = queries.shape
    heads = width // HD
    return pl.pallas_call(
        functools.partial(new_kernel, heads),
        out_shape=jax.ShapeDtypeStruct((width + STAT_ROWS, rows), BF16),
        in_specs=[pl.BlockSpec(memory_space=pltpu.VMEM)] * 3,
        out_specs=pl.BlockSpec(memory_space=pltpu.VMEM),
        scratch_shapes=[pltpu.VMEM((STAT_ROWS, rows), F32)],
        compiler_params=params(16),
        cost_estimate=cost(8 * rows * rows * width, 8 * rows * width, rows * rows * heads),
        name="new_attention",
    )(queries, keys, values)


def merge_kernel(heads, blocks, at, *refs):
    parts = refs[: len(refs) - 3]
    keep_ref, give_ref, attended = refs[len(refs) - 3 :]
    base = heads * HD
    for h in range(heads):
        levels = []
        for part in parts:
            stats = part[base : base + STAT_ROWS, :].astype(F32)
            levels.append(
                stats[3 * h : 3 * h + 1] + (stats[3 * h + 1 : 3 * h + 2] + stats[3 * h + 2 : 3 * h + 3])
            )
        highest = functools.reduce(jnp.maximum, levels)
        weights = [jnp.exp(level - highest) for level in levels]
        mass = functools.reduce(jnp.add, weights)
        joined = functools.reduce(
            jnp.add,
            [w * part[h * HD : (h + 1) * HD, :].astype(F32) for w, part in zip(weights, parts)],
        )
        attended[:, h * HD : (h + 1) * HD] = jnp.transpose(joined / mass)
    step = keep_ref.shape[0] // blocks
    for block in range(blocks):
        here = pl.ds(pl.multiple_of((2 * block + at[2]) * step, step), step)
        there = pl.ds(pl.multiple_of((2 * block + 1 - at[2]) * step, step), step)
        keep_ref[block * step : (block + 1) * step, :] = attended[here, :].astype(BF16)
        give_ref[block * step : (block + 1) * step, :] = attended[there, :].astype(BF16)


def merge(at, parts, blocks):
    rows = parts[0].shape[1]
    width = parts[0].shape[0] - STAT_ROWS
    half = jax.ShapeDtypeStruct((rows // 2, width), BF16)
    return pl.pallas_call(
        functools.partial(merge_kernel, width // HD, blocks),
        out_shape=(half, half),
        in_specs=[pl.BlockSpec(memory_space=SMEM)]
        + [pl.BlockSpec(memory_space=pltpu.VMEM)] * len(parts),
        out_specs=(pl.BlockSpec(memory_space=pltpu.VMEM),) * 2,
        scratch_shapes=[pltpu.VMEM((rows, width), F32)],
        compiler_params=params(),
        cost_estimate=cost(1, 1),
        name="merge",
    )(at, *parts)


def output_kernel(count, blocks, at, keep_ref, got_ref, *refs):
    mine, other = refs[:count], refs[count : len(refs) - blocks - 1]
    outs, total = refs[-1 - blocks : -1], refs[-1]
    depth = keep_ref.shape[1]
    groups = 4 if count == 5 else 1
    width = total.shape[1] // groups
    for k in range(groups):
        if k < 3:
            here = jnp.dot(keep_ref[...], mine[k][...], preferred_element_type=F32)
            there = other[0][k * depth : (k + 1) * depth, :]
        else:
            half = depth // 2
            here = jnp.dot(keep_ref[:, :half], mine[3][...], preferred_element_type=F32)
            here += jnp.dot(keep_ref[:, half:], mine[4][...], preferred_element_type=F32)
            there = other[1][...]
        here += jnp.dot(got_ref[...], there, preferred_element_type=F32)
        total[:, k * width : (k + 1) * width] = here
    step = total.shape[0] // blocks
    for k in range(blocks):
        at_row = pl.ds(pl.multiple_of((at[1] ^ k) * step, step), step)
        outs[k][...] = total[at_row, :].astype(BF16)


def output_projection(at, keep, got, mine, other, blocks):
    columns = mine[0].shape[1] * (4 if len(mine) == 5 else 1)
    block = jax.ShapeDtypeStruct((keep.shape[0] // blocks, columns), BF16)
    return pl.pallas_call(
        functools.partial(output_kernel, len(mine), blocks),
        out_shape=(block,) * blocks,
        in_specs=[pl.BlockSpec(memory_space=SMEM)]
        + [pl.BlockSpec(memory_space=pltpu.VMEM)] * (2 + len(mine) + len(other)),
        out_specs=(pl.BlockSpec(memory_space=pltpu.VMEM),) * blocks,
        scratch_shapes=[pltpu.VMEM((keep.shape[0], columns), F32)],
        compiler_params=params(20),
        cost_estimate=cost(1, 1),
        name="output_projection",
    )(at, keep, got, *mine, *other)


def sum_kernel(groups, at, mask_ref, *refs):
    parts, out_ref = refs[:-1], refs[-1]
    width = out_ref.shape[1] // groups
    mask = mask_ref[:, :1]
    for k in range(groups):
        here = slice(k * width, (k + 1) * width)
        total = functools.reduce(jnp.add, [part[:, here].astype(F32) for part in parts])
        total = total * mask
        if groups == 1:
            out_ref[...] = total.astype(BF16)
        else:
            begin = pl.multiple_of((at[0] ^ k) * width, width)
            out_ref[:, pl.ds(begin, width)] = total.astype(BF16)


def final_sum(at, mask, parts, groups):
    return pl.pallas_call(
        functools.partial(sum_kernel, groups),
        out_shape=jax.ShapeDtypeStruct(parts[0].shape, BF16),
        in_specs=[pl.BlockSpec(memory_space=SMEM)]
        + [pl.BlockSpec(memory_space=pltpu.VMEM)] * (1 + len(parts)),
        out_specs=pl.BlockSpec(memory_space=pltpu.VMEM),
        compiler_params=params(),
        cost_estimate=cost(1, 1),
        name="final_sum",
    )(at, mask, *parts)


def query_4(at, blocks, rows, weights, up, down_rows, *gate):
    shard = weights.shape[0]
    half = shard // 2
    by_x, by_y = both_ways(weights)
    top, bottom = halves_on(by_x, by_y, None, *gate)
    pieces = [(x, 0, shard, k, 0, shard) for k, x in enumerate((weights, by_x, by_y))]
    pieces += [(top, 0, half, 3, 0, shard), (bottom, 0, half, 3, half, shard)]
    query, mark = project(at, blocks, rows, [(pieces, None, up)], down_rows)
    return query, mark, [top, bottom]


def key_value_4(at, blocks, rows, weights, near, last, downs, ups, down_rows, *late):
    shard = weights.shape[0] // 2
    other = other_core(assemble([(x, row, 2 * HD) for x, row in downs], *late))
    inputs = []
    for n in range(2):
        pieces = [(x, n * shard, shard, k, 0, shard) for k, x in enumerate((weights, *near))]
        pieces.append((last[n], 0, shard, 3, 0, shard))
        small = [(x, row + n * HD, k, 0) for k, (x, row) in enumerate(downs)]
        small += [(other, (2 * k + n) * HD, k, 1) for k in range(4)]
        inputs.append((pieces, small, ups[n]))
    return project(at, blocks, rows, inputs, down_rows)


def shards(
    hidden_states,
    embeddings,
    norm_gain,
    input_weights,
    adapter_down,
    adapter_up,
    output_weights,
    own_keys,
    own_values,
    shared_keys,
    shared_values,
    cached_lengths,
    prompt_group,
    slot_pages,
    padding_mask,
):
    dp, seq, mp = (lax.axis_index(axis) for axis in ("dp", "seq", "mp"))
    seq_count = lax.axis_size("seq")
    by_four = lax.axis_size("dp") == 4 and seq_count == 4
    at = jnp.stack([dp, seq, mp, cached_lengths[0], prompt_group[0]])
    pages = slot_pages[0]
    ups = [adapter_up[p, :, 0] for p in range(3)]
    down_rows = adapter_down.shape[0] // 4

    own_rows = hidden_states.shape[0]
    rows = own_rows * seq_count
    half, mark = norm(
        at,
        hidden_states,
        embeddings,
        norm_gain[None, :],
        adapter_down,
        down_rows if by_four else None,
    )
    mine = spread(half)
    blocks = [(block, other_core(block)) for block in mine]
    shard, _, _, width = input_weights.shape
    if by_four:
        own_weights = jnp.transpose(input_weights[:, :, 0], (1, 0, 2)).reshape(-1, width)
        weights = cut(own_weights, 0, shard, mark)
        query, mark, arrived = query_4(at, blocks, rows, weights, ups[0], down_rows, mine[2])
    else:
        whole = lax.all_gather(input_weights[:, :, 0], "dp", axis=0, tiled=True)
        down = lax.all_gather(adapter_down, ("seq", "mp"), axis=0, tiled=True)
        inputs = [
            ([(whole[:, p], 0, whole.shape[0], None, 0, 0)], down[:, p * HD : (p + 1) * HD], ups[p])
            for p in range(3)
        ]
        query, key, value, mark = project(at, blocks, rows, inputs, None)
    queries = spread(query)

    parts, sent, marks = {}, {}, [mark]
    for k in range(seq_count):
        parts[k], mark = cache_attention(
            at,
            marks[-1],
            pages,
            k,
            queries[k],
            own_keys,
            own_values,
            shared_keys,
            shared_values,
        )
        marks.append(mark)
        sent[k] = lax.ppermute(parts[k], "seq", swap(seq_count, k)) if k else parts[k]

    if by_four:
        begin = own_rows + HD * adapter_down.shape[0] // half.shape[1]
        down = arrange(mine, marks[0], begin, down_rows)
        exchanged = [block[1] for block in blocks[:3]]
        weights = cut(own_weights, shard, 2 * shard, mine[3], *exchanged, *arrived)
        near = both_ways(weights)
        far = lax.ppermute(down, "dp", swap(4, 3))
        output_own = cut(output_weights[0], 0, output_weights.shape[1], *near, far, marks[3])
        by_x, by_y = both_ways(output_own)
        last = halves_on(*near, down, by_x, by_y, queries[3])
        top, bottom = halves_on(by_x, by_y, None, *last)
        downs = [(down, 0), (last[1], shard), (last[0], shard), (far, 0)]
        key, value, _ = key_value_4(
            at, blocks, rows, weights, near, last, downs, ups[1:], down_rows, *list(sent.values())[1:]
        )
        out_mine = [output_own, by_x, by_y, top, bottom]
        out_other = [
            other_core(assemble([(x, 0, x.shape[0]) for x in part]))
            for part in (out_mine[:3], out_mine[3:])
        ]
    else:
        out_mine = [lax.all_gather(output_weights[0], "dp", axis=1, tiled=True)]
        out_other = [other_core(out_mine[0])]

    joined = [sent[k] for k in range(seq_count)] + [new_attention(query, key, value)]
    keep, give = merge(at, joined, seq_count)
    got = other_core(give)
    sums = output_projection(at, keep, got, out_mine, out_other, seq_count)
    sums = [sums[0]] + [lax.ppermute(sums[k], "seq", swap(seq_count, k)) for k in range(1, seq_count)]
    mask = jnp.broadcast_to(padding_mask.astype(F32)[:, None], (padding_mask.shape[0], HD))
    return final_sum(at, mask, sums, 4 if by_four else 1)


def solution(mesh):
    placed = (
        P(("dp", "seq"), None),
        P(("dp", "seq"), None),
        P(),
        P("dp", None, "mp", "seq"),
        P(("seq", "mp"), None),
        P(None, None, "mp", "seq"),
        P("mp", "seq", "dp"),
        P("dp", "seq", "mp"),
        P("dp", "seq", "mp"),
        P(None, "seq", "mp"),
        P(None, "seq", "mp"),
        P("dp"),
        P("dp"),
        P("dp", "seq"),
        P(("dp", "seq", "mp")),
    )
    return jax.shard_map(
        shards, mesh=mesh, in_specs=placed, out_specs=P(("dp", "seq", "mp"), None), check_vma=False
    )
```

time: 321 us -> 240 us (0.75)
  starting transfers between devices: 74.3 us -> 31.9 us
  blocking collectives: 34.4 us -> 0 us
  waiting for transfers between devices: 110 us -> 137 us
  Pallas kernels: 80.7 us -> 60 us
  local copies, waits for them, and re-layouts: 17.1 us -> 8.36 us
    ppermute x63 -> x30, starting transfers between devices: 70.8 us -> 28.3 us  [the longest x6 10.1 us: spread(): blocks[k] = lax.ppermute(blocks[k ^ step], 'seq', swap(count, step))]
    all_gather x2 -> x0, blocking collectives: 34.4 us -> none  [gather_down(): along = lax.all_gather(own, 'seq', axis=0, tiled=True)]
    ppermute x63 -> x30, waiting for transfers between devices: 86.4 us -> 114 us  [the longest x6 51.7 us: spread(): blocks[k] = lax.ppermute(blocks[k ^ step], 'seq', swap(count, step))]
    pallas_call x8 -> x20, Pallas kernels: 65.9 us -> 52.3 us  [the longest x4 25.2 us: cache_attention(): pl.pallas_call(functools.partial(cache_kernel, slot, heads), out_shape=(j...]
    slice x11 -> x0, local copies, waits for them, and re-layouts: 6.49 us -> none  [the longest x6 5.03 us: gather_dp(): top, bottom = (x[:half], x[half:])]
    squeeze x2 -> x1, local copies, waits for them, and re-layouts: 3.86 us -> 0.03 us  [shards(): ups = [adapter_up[p, :, 0] for p in range(3)]]
    unnamed x112 -> x60, local copies, waits for them, and re-layouts: 4.12 us -> 7.6 us
  transfers between devices with their start and end apart: 66 -> 33, of which waited for: 22 -> 18; matrix products, arithmetic and copies ran while one was open for 4% -> 0% of each run, Pallas kernels for 22% -> 21%
where the time goes in v2:
time: 240 us; the launch traced here: 239 us
  waiting for transfers between devices  137 us (57%)
  Pallas kernels  60 us (25%)
  starting transfers between devices  31.9 us (13%)
  local copies, waits for them, and re-layouts  8.36 us (3%)
    ppermute x6, waiting for transfers between devices, spread(): blocks[k] = lax.ppermute(blocks[k ^ step], 'seq', swap(count, step))  51.7 us
    ppermute x3, waiting for transfers between devices, shards(): lax.ppermute(parts[k], 'seq', swap(seq_count, k))  38 us
    pallas_call x4, Pallas kernels, cache_attention(): pl.pallas_call(functools.partial(cache_kernel, slot, heads), out_shape=(j...  25.2 us
    ppermute x3, waiting for transfers between devices, shards(): lax.ppermute(sums[k], 'seq', swap(seq_count, k))  23.2 us
    pallas_call x2, Pallas kernels, project(): pl.pallas_call(functools.partial(project_kernel, (placed, len(arrays), tu...  16.3 us
    ppermute x6, waiting for transfers between devices, along_x(): return lax.ppermute(x, 'dp', swap(4, 1))  10.6 us
    ppermute x6, starting transfers between devices, spread(): blocks[k] = lax.ppermute(blocks[k ^ step], 'seq', swap(count, step))  10.1 us
    ppermute x6, waiting for transfers between devices, along_y(): return lax.ppermute(x, 'dp', swap(4, 2))  8.3 us
  transfers between devices with their start and end apart: 33, of which 18 were waited for; matrix products, arithmetic and copies ran while one was open for 0% of the time, Pallas kernels for 21%

profile of v2, /device:TPU:16, one launch (start us, length us, event | category | flops | bytes accessed | tf_op | source)
XLA Modules:
  0.0 239.0 jit_solution(11688947258423230207)
XLA Ops:
  2.0 3.4 %norm.1 = (bf16[176,2048]{1,0:T(8,128)(2,1)}, s32[1]{0:T(128)}) custom-call(s32[5]{0:T(128)} %stack.15.at, bf16[128,2048]{1,0:T(8,128)(2,1)} %refs_0_.1, bf16[128,2048]{1,0:T(8,128)(2,1)} %refs_1_.1, f32[1,4096]{1,0:T(1,128)} %bitcast.24, bf16[512,384]{1,0:T(8,128)(2,1)} %refs_3_.1), custom_call_target="tpu_custom_call" | custom-call | flops 1 | bytes 1 | tf_op jit(solution)/shard_map/norm/pallas_call | solution.py:164
  5.4 1.9 copy-done.8
  7.3 0.8 cut.3.refs_8_
  8.1 1.6 collective-permute-start.7
  9.7 1.5 collective-permute-start.8
  11.2 1.6 collective-permute-start.1
  13.1 28.7 %collective-permute-done.1.refs_2_.refs_1_ = bf16[176,2048]{1,0:T(8,128)(2,1)S(1)} collective-permute-done((bf16[176,2048]{1,0:T(8,128)(2,1)S(1)}, bf16[176,2048]{1,0:T(8,128)(2,1)S(1)}, u32[]{:S(2)}, u32[]{:S(2)}) %collective-permute-start.1) | collective-permute-done | bytes 720928 | tf_op jit(solution)/shard_map/ppermute | solution.py:83
  41.8 2.1 collective-permute-done.3.refs_1_.refs_4_.refs_2_
  44.0 2.8 %collective-permute-start.5 = (bf16[176,2048]{1,0:T(8,128)(2,1)S(1)}, bf16[176,2048]{1,0:T(8,128)(2,1)S(1)}, u32[]{:S(2)}, u32[]{:S(2)}) collective-permute-start(bf16[176,2048]{1,0:T(8,128)(2,1)S(1)} %collective-permute-done.3.refs_1_.refs_4_.refs_2_), channel_id=1, source_target_pairs={{0,2},{2,0},{4,6},{6,4},{1,3},{3,1},{5,7},{7,5},{8,10},{10,8},{12,... | collective-permute-start | bytes 2162696 | tf_op jit(solution)/shard_map/ppermute | solution.py:83
  48.1 15.4 %collective-permute-done.5.refs_6_.refs_1_.refs_3_ = bf16[176,2048]{1,0:T(8,128)(2,1)S(1)} collective-permute-done((bf16[176,2048]{1,0:T(8,128)(2,1)S(1)}, bf16[176,2048]{1,0:T(8,128)(2,1)S(1)}, u32[]{:S(2)}, u32[]{:S(2)}) %collective-permute-start.5) | collective-permute-done | bytes 720928 | tf_op jit(solution)/shard_map/ppermute | solution.py:83
  63.5 1.6 cut.4.refs_8_
  66.2 2.2 collective-permute-done.6.refs_7_
  68.4 7.4 %project.2 = (bf16[512,512]{1,0:T(8,128)(2,1)}, s32[1]{0:T(128)}) custom-call(s32[5]{0:T(128)S(1)} %copy-done.26, bf16[176,2048]{1,0:T(8,128)(2,1)S(1)} %copy-done.13, bf16[176,2048]{1,0:T(8,128)(2,1)S(1)} %collective-permute-done.refs_1_.refs_2_, bf16[176,2048]{1,0:T(8,128)(2,1)S(1)} %collective-permute-done.1.refs_2_.refs_1_, ...), custom_call_target="tpu_custom_call" | custom-call | flops 1 | bytes 1 | tf_op jit(solution)/shard_map/project/pallas_call | solution.py:289
  75.8 1.7 collective-permute-start.13
  78.0 2.3 arrange.1.refs_1_.refs_0_.refs_12_
  80.2 2.5 %collective-permute-start.19 = (bf16[256,512]{1,0:T(8,128)(2,1)}, bf16[256,512]{1,0:T(8,128)(2,1)S(1)}, u32[]{:S(2)}, u32[]{:S(2)}) collective-permute-start(bf16[256,512]{1,0:T(8,128)(2,1)} %arrange.1.refs_1_.refs_0_.refs_12_), channel_id=1, source_target_pairs={{0,24},{8,16},{16,8},{24,0},{1,25},{9,17},{17,9},{25,1},{2,26},{10... | collective-permute-start | bytes 786440 | tf_op jit(solution)/shard_map/ppermute | solution.py:633
  82.8 2.2 copy-done
  84.9 2.2 copy-done.2
  87.1 1.2 copy-done.7
  88.4 6.7 %cache_attention.4 = (bf16[528,512]{1,0:T(8,128)(2,1)S(1)}, s32[1]{0:T(128)}) custom-call(s32[5]{0:T(128)S(1)} %copy-done.26, s32[1]{0:T(128)} %get-tuple-element.26.earlier.refs_4_, s32[16]{0:T(128)S(1)} %bitcast.20, bf16[512,512]{1,0:T(8,128)(2,1)} %get-tuple-element.27.query_ref, bf16[1,1024,2048]{2,1,0:T(8,128)(2,1)S(1)} %copy-done, ...), custom_call_target="tpu_custom_call" | custom-call | flops 1 | bytes 1 | tf_op jit(solution)/shard_map/cache_attention/pallas_call | solution.py:377
  95.1 5.4 %collective-permute-done.13.query_ref = bf16[512,512]{1,0:T(8,128)(2,1)} collective-permute-done((bf16[512,512]{1,0:T(8,128)(2,1)}, bf16[512,512]{1,0:T(8,128)(2,1)}, u32[]{:S(2)}, u32[]{:S(2)}) %collective-permute-start.13) | collective-permute-done | bytes 524320 | tf_op jit(solution)/shard_map/ppermute | solution.py:83
  100.5 3.3 %collective-permute-start.15 = (bf16[512,512]{1,0:T(8,128)(2,1)}, bf16[512,512]{1,0:T(8,128)(2,1)S(1)}, u32[]{:S(2)}, u32[]{:S(2)}) collective-permute-start(bf16[512,512]{1,0:T(8,128)(2,1)} %collective-permute-done.13.query_ref), channel_id=1, source_target_pairs={{0,2},{2,0},{4,6},{6,4},{1,3},{3,1},{5,7},{7,5},{8,10},{10,8},{12,... | collective-permute-start | bytes 1572872 | tf_op jit(solution)/shard_map/ppermute | solution.py:83
  103.8 6.5 %cache_attention.5 = (bf16[528,512]{1,0:T(8,128)(2,1)S(1)}, s32[1]{0:T(128)}) custom-call(s32[5]{0:T(128)S(1)} %copy-done.26, s32[1]{0:T(128)} %get-tuple-element.29.earlier, s32[16]{0:T(128)S(1)} %bitcast.21, bf16[512,512]{1,0:T(8,128)(2,1)} %collective-permute-done.11.query_ref, bf16[1,1024,2048]{2,1,0:T(8,128)(2,1)S(1)} %copy-done.1, ...), custom_call_target="tpu_custom_call" | custom-call | flops 1 | bytes 1 | tf_op jit(solution)/shard_map/cache_attention/pallas_call | solution.py:377
  110.3 6.2 %cache_attention.6 = (bf16[528,512]{1,0:T(8,128)(2,1)S(1)}, s32[1]{0:T(128)}) custom-call(s32[5]{0:T(128)S(1)} %copy-done.26, s32[1]{0:T(128)} %get-tuple-element.31.earlier, s32[16]{0:T(128)S(1)} %bitcast.22, bf16[512,512]{1,0:T(8,128)(2,1)} %collective-permute-done.13.query_ref, bf16[1,1024,2048]{2,1,0:T(8,128)(2,1)S(1)} %copy-done.1, ...), custom_call_target="tpu_custom_call" | custom-call | flops 1 | bytes 1 | tf_op jit(solution)/shard_map/cache_attention/pallas_call | solution.py:377
  116.6 1.8 collective-permute-done.19.refs_3_.refs_14_
  119.4 1.6 collective-permute-start.20
  121.5 10.5 %collective-permute-done.20.refs_2_.refs_0_.refs_1_ = bf16[512,512]{1,0:T(8,128)(2,1)S(1)} collective-permute-done((bf16[512,512]{1,0:T(8,128)(2,1)S(1)}, bf16[512,512]{1,0:T(8,128)(2,1)S(1)}, u32[]{:S(2)}, u32[]{:S(2)}) %collective-permute-start.20) | collective-permute-done | bytes 524320 | tf_op jit(solution)/shard_map/ppermute | solution.py:88
  132.3 1.6 collective-permute-start.22
  133.9 1.7 assemble.12
  135.5 1.5 collective-permute-start.23
  137.0 1.3 collective-permute-start.12
  138.7 5.7 %cache_attention.7 = (bf16[528,512]{1,0:T(8,128)(2,1)S(1)}, s32[1]{0:T(128)}) custom-call(s32[5]{0:T(128)S(1)} %copy-done.26, s32[1]{0:T(128)} %get-tuple-element.33.earlier.refs_4_, s32[16]{0:T(128)S(1)} %bitcast.23, bf16[512,512]{1,0:T(8,128)(2,1)S(1)} %collective-permute-done.15.query_ref.refs_4_, bf16[1,1024,2048]{2,1,0:T(8,128)(2,1)S(1)} %copy-done.1, ...), custom_call_target="tpu_custom_call" | custom-call | flops 1 | bytes 1 | tf_op jit(solution)/shard_map/cache_attention/pallas_call | solution.py:377
  144.4 1.9 collective-permute-start.16
  146.4 10.4 %collective-permute-done.12.refs_4_.refs_1_ = bf16[528,512]{1,0:T(8,128)(2,1)S(1)} collective-permute-done((bf16[528,512]{1,0:T(8,128)(2,1)S(1)}, bf16[528,512]{1,0:T(8,128)(2,1)S(1)}, u32[]{:S(2)}, u32[]{:S(2)}) %collective-permute-start.12) | collective-permute-done | bytes 540704 | tf_op jit(solution)/shard_map/ppermute | solution.py:625
  156.8 17.4 %collective-permute-done.14.refs_5_.refs_2_ = bf16[528,512]{1,0:T(8,128)(2,1)S(1)} collective-permute-done((bf16[528,512]{1,0:T(8,128)(2,1)S(1)}, bf16[528,512]{1,0:T(8,128)(2,1)S(1)}, u32[]{:S(2)}, u32[]{:S(2)}) %collective-permute-start.14) | collective-permute-done | bytes 540704 | tf_op jit(solution)/shard_map/ppermute | solution.py:625
  174.3 10.2 %collective-permute-done.16.refs_6_.refs_3_ = bf16[528,512]{1,0:T(8,128)(2,1)S(1)} collective-permute-done((bf16[528,512]{1,0:T(8,128)(2,1)S(1)}, bf16[528,512]{1,0:T(8,128)(2,1)S(1)}, u32[]{:S(2)}, u32[]{:S(2)}) %collective-permute-start.16) | collective-permute-done | bytes 540704 | tf_op jit(solution)/shard_map/ppermute | solution.py:625
  185.7 7.7 %collective-permute-done.26.refs_0_.refs_3_ = bf16[256,512]{1,0:T(8,128)(2,1)S(1)} collective-permute-done((bf16[256,512]{1,0:T(8,128)(2,1)S(1)}, bf16[256,512]{1,0:T(8,128)(2,1)S(1)}, u32[]{:S(2)}, u32[]{:S(2)}) %collective-permute-start.26) | collective-permute-done | bytes 262176 | tf_op jit(solution)/shard_map/ppermute | solution.py:92
  193.8 9.0 %project.3 = (bf16[512,512]{1,0:T(8,128)(2,1)S(1)}, bf16[512,512]{1,0:T(8,128)(2,1)S(1)}, s32[1]{0:T(128)}) custom-call(s32[5]{0:T(128)S(1)} %copy-done.26, bf16[176,2048]{1,0:T(8,128)(2,1)S(1)} %copy-done.14, bf16[176,2048]{1,0:T(8,128)(2,1)S(1)} %copy-done.18, bf16[176,2048]{1,0:T(8,128)(2,1)S(1)} %copy-done.16, bf16[176,2048]{1,0:T(8,128)(2,1)S(1)} %copy-done.20, ...), custom_call_target="tpu_custom_call" | custom-call | flops 1 | bytes 1 | tf_op jit(solution)/shard_map/project/pallas_call | solution.py:289
  202.7 3.1 %new_attention.1.refs_4_ = bf16[528,512]{1,0:T(8,128)(2,1)S(1)} custom-call(bf16[512,512]{1,0:T(8,128)(2,1)} %get-tuple-element.27.query_ref, bf16[512,512]{1,0:T(8,128)(2,1)S(1)} %get-tuple-element.35.key_ref, bf16[512,512]{1,0:T(8,128)(2,1)S(1)} %get-tuple-element.36.value_ref), custom_call_target="tpu_custom_call" | custom-call | flops 1 | bytes 1 | tf_op jit(solution)/shard_map/new_attention/pallas_call | solution.py:412
  205.8 1.3 merge.1
  207.7 1.2 collective-permute-done.25.got_ref
  208.8 1.9 output_projection.1
  210.8 1.4 collective-permute-start.31
  212.2 2.1 collective-permute-start.32
  214.3 6.7 %collective-permute-done.30.refs_1_ = bf16[64,2048]{1,0:T(8,128)(2,1)S(1)} collective-permute-done((bf16[64,2048]{1,0:T(8,128)(2,1)S(1)}, bf16[64,2048]{1,0:T(8,128)(2,1)S(1)}, u32[]{:S(2)}, u32[]{:S(2)}) %collective-permute-start.30) | collective-permute-done | bytes 262176 | tf_op jit(solution)/shard_map/ppermute | solution.py:655
  221.0 9.0 %collective-permute-done.31.refs_2_ = bf16[64,2048]{1,0:T(8,128)(2,1)S(1)} collective-permute-done((bf16[64,2048]{1,0:T(8,128)(2,1)S(1)}, bf16[64,2048]{1,0:T(8,128)(2,1)S(1)}, u32[]{:S(2)}, u32[]{:S(2)}) %collective-permute-start.31) | collective-permute-done | bytes 262176 | tf_op jit(solution)/shard_map/ppermute | solution.py:655
  230.0 7.4 %collective-permute-done.32.refs_3_ = bf16[64,2048]{1,0:T(8,128)(2,1)S(1)} collective-permute-done((bf16[64,2048]{1,0:T(8,128)(2,1)S(1)}, bf16[64,2048]{1,0:T(8,128)(2,1)S(1)}, u32[]{:S(2)}, u32[]{:S(2)}) %collective-permute-start.32) | collective-permute-done | bytes 262176 | tf_op jit(solution)/shard_map/ppermute | solution.py:655
  237.5 1.4 final_sum.1
  (106 shorter events, 8.3 us)
Async XLA Ops:
  8.1 35.8 %collective-permute-start.7 = (bf16[1024,512]{1,0:T(8,128)(2,1)S(1)}, bf16[1024,512]{1,0:T(8,128)(2,1)S(1)}, u32[]{:S(2)}, u32[]{:S(2)}) collective-permute-start(bf16[1024,512]{1,0:T(8,128)(2,1)S(1)} %cut.3.refs_8_), channel_id=1, source_target_pairs={{0,8},{8,0},{16,24},{24,16},{1,9},{9,1},{17,25},{25,17},{2,10},{10... | collective-permute-start | bytes 3145736 | tf_op jit(solution)/shard_map/ppermute | solution.py:88
  9.7 37.1 %collective-permute-start.8 = (bf16[1024,512]{1,0:T(8,128)(2,1)S(1)}, bf16[1024,512]{1,0:T(8,128)(2,1)S(1)}, u32[]{:S(2)}, u32[]{:S(2)}) collective-permute-start(bf16[1024,512]{1,0:T(8,128)(2,1)S(1)} %cut.3.refs_8_), channel_id=1, source_target_pairs={{0,16},{8,24},{16,0},{24,8},{1,17},{9,25},{17,1},{25,9},{2,18},{10... | collective-permute-start | bytes 3145736 | tf_op jit(solution)/shard_map/ppermute | solution.py:92
  11.2 52.3 %copy-start.9 = (bf16[1024,3,1,512]{3,0,2,1:T(8,128)(2,1)S(1)}, bf16[1024,3,1,512]{3,0,2,1:T(8,128)(2,1)}, u32[]{:S(2)}) copy-start(bf16[1024,3,1,512]{3,0,2,1:T(8,128)(2,1)} %param.18) | copy-start | bytes 9437188
  11.2 30.6 %collective-permute-start.1 = (bf16[176,2048]{1,0:T(8,128)(2,1)S(1)}, bf16[176,2048]{1,0:T(8,128)(2,1)S(1)}, u32[]{:S(2)}, u32[]{:S(2)}) collective-permute-start(bf16[176,2048]{1,0:T(8,128)(2,1)S(1)} %copy-done.13), channel_id=1, source_target_pairs={{0,2},{2,0},{4,6},{6,4},{1,3},{3,1},{5,7},{7,5},{8,10},{10,8},{12,... | collective-permute-start | bytes 2162696 | tf_op jit(solution)/shard_map/ppermute | solution.py:83
  12.8 31.2 %collective-permute-start.3 = (bf16[176,2048]{1,0:T(8,128)(2,1)S(1)}, bf16[176,2048]{1,0:T(8,128)(2,1)S(1)}, u32[]{:S(2)}, u32[]{:S(2)}) collective-permute-start(bf16[176,2048]{1,0:T(8,128)(2,1)S(1)} %copy-done.13), channel_id=1, source_target_pairs={{0,4},{2,6},{4,0},{6,2},{1,5},{3,7},{5,1},{7,3},{8,12},{10,14},{12... | collective-permute-start | bytes 2162696 | tf_op jit(solution)/shard_map/ppermute | solution.py:83
  13.1 34.3 %collective-permute-start = (bf16[176,2048]{1,0:T(8,128)(2,1)S(1)}, bf16[176,2048]{1,0:T(8,128)(2,1)S(1)}, u32[]{:S(2)}, u32[]{:S(2)}) collective-permute-start(bf16[176,2048]{1,0:T(8,128)(2,1)S(1)} %copy-done.13), channel_id=1, source_target_pairs={{0,1},{1,0},{2,3},{3,2},{4,5},{5,4},{6,7},{7,6},{8,9},{9,8},{10,11... | collective-permute-start | bytes 2162696 | tf_op jit(solution)/shard_map/ppermute | solution.py:108
  41.8 26.6 %copy-start.15 = (bf16[176,2048]{1,0:T(8,128)(2,1)}, bf16[176,2048]{1,0:T(8,128)(2,1)S(1)}, u32[]{:S(2)}) copy-start(bf16[176,2048]{1,0:T(8,128)(2,1)S(1)} %collective-permute-done.1.refs_2_.refs_1_) | copy-start | bytes 2162692
  41.8 6.2 %collective-permute-start.2 = (bf16[176,2048]{1,0:T(8,128)(2,1)S(1)}, bf16[176,2048]{1,0:T(8,128)(2,1)S(1)}, u32[]{:S(2)}, u32[]{:S(2)}) collective-permute-start(bf16[176,2048]{1,0:T(8,128)(2,1)S(1)} %collective-permute-done.1.refs_2_.refs_1_), channel_id=1, source_target_pairs={{0,1},{1,0},{2,3},{3,2},{4,5},{5,4},{6,7},{7,6},{8,9},{9,8},{10,11... | collective-permute-start | bytes 2162696 | tf_op jit(solution)/shard_map/ppermute | solution.py:108
  44.0 24.4 %copy-start.4 = (bf16[176,2048]{1,0:T(8,128)(2,1)}, bf16[176,2048]{1,0:T(8,128)(2,1)S(1)}, u32[]{:S(2)}) copy-start(bf16[176,2048]{1,0:T(8,128)(2,1)S(1)} %collective-permute-done.3.refs_1_.refs_4_.refs_2_) | copy-start | bytes 2162692
  44.0 4.1 %collective-permute-start.4 = (bf16[176,2048]{1,0:T(8,128)(2,1)S(1)}, bf16[176,2048]{1,0:T(8,128)(2,1)S(1)}, u32[]{:S(2)}, u32[]{:S(2)}) collective-permute-start(bf16[176,2048]{1,0:T(8,128)(2,1)S(1)} %collective-permute-done.3.refs_1_.refs_4_.refs_2_), channel_id=1, source_target_pairs={{0,1},{1,0},{2,3},{3,2},{4,5},{5,4},{6,7},{7,6},{8,9},{9,8},{10,11... | collective-permute-start | bytes 2162696 | tf_op jit(solution)/shard_map/ppermute | solution.py:108
  44.0 19.5 %collective-permute-start.5 = (bf16[176,2048]{1,0:T(8,128)(2,1)S(1)}, bf16[176,2048]{1,0:T(8,128)(2,1)S(1)}, u32[]{:S(2)}, u32[]{:S(2)}) collective-permute-start(bf16[176,2048]{1,0:T(8,128)(2,1)S(1)} %collective-permute-done.3.refs_1_.refs_4_.refs_2_), channel_id=1, source_target_pairs={{0,2},{2,0},{4,6},{6,4},{1,3},{3,1},{5,7},{7,5},{8,10},{10,8},{12,... | collective-permute-start | bytes 2162696 | tf_op jit(solution)/shard_map/ppermute | solution.py:83
  46.8 16.7 %collective-permute-start.9 = (bf16[512,512]{1,0:T(8,128)(2,1)S(1)}, bf16[512,512]{1,0:T(8,128)(2,1)S(1)}, u32[]{:S(2)}, u32[]{:S(2)}) collective-permute-start(bf16[512,512]{1,0:T(8,128)(2,1)S(1)} %assemble.9), channel_id=1, source_target_pairs={{0,16},{8,24},{16,0},{24,8},{1,17},{9,25},{17,1},{25,9},{2,18},{10... | collective-permute-start | bytes 1572872 | tf_op jit(solution)/shard_map/ppermute | solution.py:92
  47.4 18.8 %copy-start.28 = (bf16[3,128,1,512]{3,1,2,0:T(8,128)(2,1)S(1)}, bf16[3,128,1,512]{3,1,2,0:T(8,128)(2,1)}, u32[]{:S(2)}) copy-start(bf16[3,128,1,512]{3,1,2,0:T(8,128)(2,1)} %param.20) | copy-start | bytes 1179652
  47.4 21.0 %copy-start.26 = (s32[5]{0:T(128)S(1)}, s32[5]{0:T(128)}, u32[]{:S(2)}) copy-start(s32[5]{0:T(128)} %stack.15.at) | copy-start | bytes 64
  47.4 21.0 %copy-start.17 = (bf16[176,2048]{1,0:T(8,128)(2,1)}, bf16[176,2048]{1,0:T(8,128)(2,1)S(1)}, u32[]{:S(2)}) copy-start(bf16[176,2048]{1,0:T(8,128)(2,1)S(1)} %collective-permute-done.refs_1_.refs_2_) | copy-start | bytes 2162692
  47.4 16.0 %collective-permute-start.10 = (bf16[512,512]{1,0:T(8,128)(2,1)S(1)}, bf16[512,512]{1,0:T(8,128)(2,1)S(1)}, u32[]{:S(2)}, u32[]{:S(2)}) collective-permute-start(bf16[512,512]{1,0:T(8,128)(2,1)S(1)} %assemble.10), channel_id=1, source_target_pairs={{0,8},{8,0},{16,24},{24,16},{1,9},{9,1},{17,25},{25,17},{2,10},{10... | collective-permute-start | bytes 1572872 | tf_op jit(solution)/shard_map/ppermute | solution.py:88
  48.0 20.4 %copy-start.19 = (bf16[176,2048]{1,0:T(8,128)(2,1)}, bf16[176,2048]{1,0:T(8,128)(2,1)S(1)}, u32[]{:S(2)}) copy-start(bf16[176,2048]{1,0:T(8,128)(2,1)S(1)} %collective-permute-done.2.refs_3_) | copy-start | bytes 2162692
  48.0 20.4 %copy-start.21 = (bf16[176,2048]{1,0:T(8,128)(2,1)}, bf16[176,2048]{1,0:T(8,128)(2,1)S(1)}, u32[]{:S(2)}) copy-start(bf16[176,2048]{1,0:T(8,128)(2,1)S(1)} %collective-permute-done.4.refs_5_.refs_4_) | copy-start | bytes 2162692
  65.1 53.3 %collective-permute-start.17 = (bf16[2048,512]{1,0:T(8,128)(2,1)}, bf16[2048,512]{1,0:T(8,128)(2,1)S(1)}, u32[]{:S(2)}, u32[]{:S(2)}) collective-permute-start(bf16[2048,512]{1,0:T(8,128)(2,1)} %cut.4.refs_8_), channel_id=1, source_target_pairs={{0,8},{8,0},{16,24},{24,16},{1,9},{9,1},{17,25},{25,17},{2,10},{10... | collective-permute-start | bytes 6291464 | tf_op jit(solution)/shard_map/ppermute | solution.py:88
  65.7 53.0 %collective-permute-start.18 = (bf16[2048,512]{1,0:T(8,128)(2,1)}, bf16[2048,512]{1,0:T(8,128)(2,1)}, u32[]{:S(2)}, u32[]{:S(2)}) collective-permute-start(bf16[2048,512]{1,0:T(8,128)(2,1)} %cut.4.refs_8_), channel_id=1, source_target_pairs={{0,16},{8,24},{16,0},{24,8},{1,17},{9,25},{17,1},{25,9},{2,18},{10... | collective-permute-start | bytes 6291464 | tf_op jit(solution)/shard_map/ppermute | solution.py:92
  66.2 2.2 collective-permute-start.6
  75.8 24.7 %collective-permute-start.13 = (bf16[512,512]{1,0:T(8,128)(2,1)}, bf16[512,512]{1,0:T(8,128)(2,1)}, u32[]{:S(2)}, u32[]{:S(2)}) collective-permute-start(bf16[512,512]{1,0:T(8,128)(2,1)} %get-tuple-element.27.query_ref), channel_id=1, source_target_pairs={{0,4},{2,6},{4,0},{6,2},{1,5},{3,7},{5,1},{7,3},{8,12},{10,14},{12... | collective-permute-start | bytes 1572872 | tf_op jit(solution)/shard_map/ppermute | solution.py:83
  77.5 26.3 %collective-permute-start.11 = (bf16[512,512]{1,0:T(8,128)(2,1)}, bf16[512,512]{1,0:T(8,128)(2,1)}, u32[]{:S(2)}, u32[]{:S(2)}) collective-permute-start(bf16[512,512]{1,0:T(8,128)(2,1)} %get-tuple-element.27.query_ref), channel_id=1, source_target_pairs={{0,2},{2,0},{4,6},{6,4},{1,3},{3,1},{5,7},{7,5},{8,10},{10,8},{12,... | collective-permute-start | bytes 1572872 | tf_op jit(solution)/shard_map/ppermute | solution.py:83
  80.2 38.2 %collective-permute-start.19 = (bf16[256,512]{1,0:T(8,128)(2,1)}, bf16[256,512]{1,0:T(8,128)(2,1)S(1)}, u32[]{:S(2)}, u32[]{:S(2)}) collective-permute-start(bf16[256,512]{1,0:T(8,128)(2,1)} %arrange.1.refs_1_.refs_0_.refs_12_), channel_id=1, source_target_pairs={{0,24},{8,16},{16,8},{24,0},{1,25},{9,17},{17,9},{25,1},{2,26},{10... | collective-permute-start | bytes 786440 | tf_op jit(solution)/shard_map/ppermute | solution.py:633
  88.4 15.4 %copy-start.1 = (bf16[1,1024,2048]{2,1,0:T(8,128)(2,1)S(1)}, bf16[1,1024,2048]{2,1,0:T(8,128)(2,1)}, u32[]{:S(2)}) copy-start(bf16[1,1024,2048]{2,1,0:T(8,128)(2,1)} %key_ref.7) | copy-start | bytes 12582916
  88.4 15.4 %copy-start.3 = (bf16[1,1024,2048]{2,1,0:T(8,128)(2,1)S(1)}, bf16[1,1024,2048]{2,1,0:T(8,128)(2,1)}, u32[]{:S(2)}) copy-start(bf16[1,1024,2048]{2,1,0:T(8,128)(2,1)} %value_ref.7) | copy-start | bytes 12582916
  100.5 21.0 %collective-permute-start.15 = (bf16[512,512]{1,0:T(8,128)(2,1)}, bf16[512,512]{1,0:T(8,128)(2,1)S(1)}, u32[]{:S(2)}, u32[]{:S(2)}) collective-permute-start(bf16[512,512]{1,0:T(8,128)(2,1)} %collective-permute-done.13.query_ref), channel_id=1, source_target_pairs={{0,2},{2,0},{4,6},{6,4},{1,3},{3,1},{5,7},{7,5},{8,10},{10,8},{12,... | collective-permute-start | bytes 1572872 | tf_op jit(solution)/shard_map/ppermute | solution.py:83
  118.7 13.4 %copy-start.12 = (bf16[256,512]{1,0:T(8,128)(2,1)S(1)}, bf16[256,512]{1,0:T(8,128)(2,1)}, u32[]{:S(2)}) copy-start(bf16[256,512]{1,0:T(8,128)(2,1)} %arrange.1.refs_1_.refs_0_.refs_12_) | copy-start | bytes 786436
  119.4 12.5 %collective-permute-start.20 = (bf16[512,512]{1,0:T(8,128)(2,1)S(1)}, bf16[512,512]{1,0:T(8,128)(2,1)S(1)}, u32[]{:S(2)}, u32[]{:S(2)}) collective-permute-start(bf16[512,512]{1,0:T(8,128)(2,1)S(1)} %cut.5.refs_0_), channel_id=1, source_target_pairs={{0,8},{8,0},{16,24},{24,16},{1,9},{9,1},{17,25},{25,17},{2,10},{10... | collective-permute-start | bytes 1572872 | tf_op jit(solution)/shard_map/ppermute | solution.py:88
  120.9 11.2 %collective-permute-start.21 = (bf16[512,512]{1,0:T(8,128)(2,1)S(1)}, bf16[512,512]{1,0:T(8,128)(2,1)S(1)}, u32[]{:S(2)}, u32[]{:S(2)}) collective-permute-start(bf16[512,512]{1,0:T(8,128)(2,1)S(1)} %cut.5.refs_0_), channel_id=1, source_target_pairs={{0,16},{8,24},{16,0},{24,8},{1,17},{9,25},{17,1},{25,9},{2,18},{10... | collective-permute-start | bytes 1572872 | tf_op jit(solution)/shard_map/ppermute | solution.py:92
  132.3 52.2 %collective-permute-start.22 = (bf16[1280,512]{1,0:T(8,128)(2,1)S(1)}, bf16[1280,512]{1,0:T(8,128)(2,1)S(1)}, u32[]{:S(2)}, u32[]{:S(2)}) collective-permute-start(bf16[1280,512]{1,0:T(8,128)(2,1)S(1)} %assemble.11), channel_id=1, source_target_pairs={{0,16},{8,24},{16,0},{24,8},{1,17},{9,25},{17,1},{25,9},{2,18},{10... | collective-permute-start | bytes 3932168 | tf_op jit(solution)/shard_map/ppermute | solution.py:92
  135.5 48.9 %collective-permute-start.23 = (bf16[1280,512]{1,0:T(8,128)(2,1)S(1)}, bf16[1280,512]{1,0:T(8,128)(2,1)S(1)}, u32[]{:S(2)}, u32[]{:S(2)}) collective-permute-start(bf16[1280,512]{1,0:T(8,128)(2,1)S(1)} %assemble.12), channel_id=1, source_target_pairs={{0,8},{8,0},{16,24},{24,16},{1,9},{9,1},{17,25},{25,17},{2,10},{10... | collective-permute-start | bytes 3932168 | tf_op jit(solution)/shard_map/ppermute | solution.py:88
  137.0 19.8 %collective-permute-start.12 = (bf16[528,512]{1,0:T(8,128)(2,1)S(1)}, bf16[528,512]{1,0:T(8,128)(2,1)S(1)}, u32[]{:S(2)}, u32[]{:S(2)}) collective-permute-start(bf16[528,512]{1,0:T(8,128)(2,1)S(1)} %get-tuple-element.30), channel_id=1, source_target_pairs={{0,2},{2,0},{4,6},{6,4},{1,3},{3,1},{5,7},{7,5},{8,10},{10,8},{12,... | collective-permute-start | bytes 1622024 | tf_op jit(solution)/shard_map/ppermute | solution.py:625
  138.3 35.9 %collective-permute-start.14 = (bf16[528,512]{1,0:T(8,128)(2,1)S(1)}, bf16[528,512]{1,0:T(8,128)(2,1)S(1)}, u32[]{:S(2)}, u32[]{:S(2)}) collective-permute-start(bf16[528,512]{1,0:T(8,128)(2,1)S(1)} %get-tuple-element.32), channel_id=1, source_target_pairs={{0,4},{2,6},{4,0},{6,2},{1,5},{3,7},{5,1},{7,3},{8,12},{10,14},{12... | collective-permute-start | bytes 1622024 | tf_op jit(solution)/shard_map/ppermute | solution.py:625
  144.4 40.0 %collective-permute-start.16 = (bf16[528,512]{1,0:T(8,128)(2,1)S(1)}, bf16[528,512]{1,0:T(8,128)(2,1)S(1)}, u32[]{:S(2)}, u32[]{:S(2)}) collective-permute-start(bf16[528,512]{1,0:T(8,128)(2,1)S(1)} %get-tuple-element.34), channel_id=1, source_target_pairs={{0,6},{2,4},{4,2},{6,0},{1,7},{3,5},{5,3},{7,1},{8,14},{10,12},{12... | collective-permute-start | bytes 1622024 | tf_op jit(solution)/shard_map/ppermute | solution.py:625
  156.8 50.9 %collective-permute-start.28 = (bf16[1536,512]{1,0:T(8,128)(2,1)S(1)}, bf16[1536,512]{1,0:T(8,128)(2,1)S(1)}, u32[]{:S(2)}, u32[]{:S(2)}) collective-permute-start(bf16[1536,512]{1,0:T(8,128)(2,1)S(1)} %assemble.16), channel_id=1, source_target_pairs={{0,1},{1,0},{2,3},{3,2},{4,5},{5,4},{6,7},{7,6},{8,9},{9,8},{10,11... | collective-permute-start | bytes 4718600 | tf_op jit(solution)/shard_map/ppermute | solution.py:108
  184.5 9.2 %collective-permute-start.24 = (bf16[1024,512]{1,0:T(8,128)(2,1)S(1)}, bf16[1024,512]{1,0:T(8,128)(2,1)S(1)}, u32[]{:S(2)}, u32[]{:S(2)}) collective-permute-start(bf16[1024,512]{1,0:T(8,128)(2,1)S(1)} %assemble.13), channel_id=1, source_target_pairs={{0,1},{1,0},{2,3},{3,2},{4,5},{5,4},{6,7},{7,6},{8,9},{9,8},{10,11... | collective-permute-start | bytes 3145736 | tf_op jit(solution)/shard_map/ppermute | solution.py:108
  184.6 9.1 %copy-start.22 = (bf16[176,2048]{1,0:T(8,128)(2,1)S(1)}, bf16[176,2048]{1,0:T(8,128)(2,1)}, u32[]{:S(2)}) copy-start(bf16[176,2048]{1,0:T(8,128)(2,1)} %copy-done.21) | copy-start | bytes 2162692
  184.6 9.1 %copy-start.24 = (bf16[176,2048]{1,0:T(8,128)(2,1)S(1)}, bf16[176,2048]{1,0:T(8,128)(2,1)}, u32[]{:S(2)}) copy-start(bf16[176,2048]{1,0:T(8,128)(2,1)} %copy-done.23) | copy-start | bytes 2162692
  184.6 9.1 %copy-start.5 = (bf16[176,2048]{1,0:T(8,128)(2,1)S(1)}, bf16[176,2048]{1,0:T(8,128)(2,1)}, u32[]{:S(2)}) copy-start(bf16[176,2048]{1,0:T(8,128)(2,1)} %copy-done.4) | copy-start | bytes 2162692
  184.7 9.1 %copy-start.11 = (bf16[176,2048]{1,0:T(8,128)(2,1)S(1)}, bf16[176,2048]{1,0:T(8,128)(2,1)}, u32[]{:S(2)}) copy-start(bf16[176,2048]{1,0:T(8,128)(2,1)} %copy-done.10) | copy-start | bytes 2162692
  184.7 8.8 %collective-permute-start.26 = (bf16[256,512]{1,0:T(8,128)(2,1)S(1)}, bf16[256,512]{1,0:T(8,128)(2,1)S(1)}, u32[]{:S(2)}, u32[]{:S(2)}) collective-permute-start(bf16[256,512]{1,0:T(8,128)(2,1)S(1)} %assemble.14), channel_id=1, source_target_pairs={{0,16},{8,24},{16,0},{24,8},{1,17},{9,25},{17,1},{25,9},{2,18},{10... | collective-permute-start | bytes 786440 | tf_op jit(solution)/shard_map/ppermute | solution.py:92
  185.1 8.5 %collective-permute-start.27 = (bf16[256,512]{1,0:T(8,128)(2,1)S(1)}, bf16[256,512]{1,0:T(8,128)(2,1)S(1)}, u32[]{:S(2)}, u32[]{:S(2)}) collective-permute-start(bf16[256,512]{1,0:T(8,128)(2,1)S(1)} %assemble.15), channel_id=1, source_target_pairs={{0,8},{8,0},{16,24},{24,16},{1,9},{9,1},{17,25},{25,17},{2,10},{10... | collective-permute-start | bytes 786440 | tf_op jit(solution)/shard_map/ppermute | solution.py:88
  193.6 14.1 %collective-permute-start.29 = (bf16[512,512]{1,0:T(8,128)(2,1)S(1)}, bf16[512,512]{1,0:T(8,128)(2,1)S(1)}, u32[]{:S(2)}, u32[]{:S(2)}) collective-permute-start(bf16[512,512]{1,0:T(8,128)(2,1)S(1)} %assemble.17), channel_id=1, source_target_pairs={{0,1},{1,0},{2,3},{3,2},{4,5},{5,4},{6,7},{7,6},{8,9},{9,8},{10,11... | collective-permute-start | bytes 1572872 | tf_op jit(solution)/shard_map/ppermute | solution.py:108
  207.1 1.7 collective-permute-start.25
  210.7 10.3 %collective-permute-start.30 = (bf16[64,2048]{1,0:T(8,128)(2,1)S(1)}, bf16[64,2048]{1,0:T(8,128)(2,1)S(1)}, u32[]{:S(2)}, u32[]{:S(2)}) collective-permute-start(bf16[64,2048]{1,0:T(8,128)(2,1)S(1)} %get-tuple-element.40), channel_id=1, source_target_pairs={{0,2},{2,0},{4,6},{6,4},{1,3},{3,1},{5,7},{7,5},{8,10},{10,8},{12,... | collective-permute-start | bytes 786440 | tf_op jit(solution)/shard_map/ppermute | solution.py:655
  210.8 19.2 %collective-permute-start.31 = (bf16[64,2048]{1,0:T(8,128)(2,1)S(1)}, bf16[64,2048]{1,0:T(8,128)(2,1)S(1)}, u32[]{:S(2)}, u32[]{:S(2)}) collective-permute-start(bf16[64,2048]{1,0:T(8,128)(2,1)S(1)} %get-tuple-element.41), channel_id=1, source_target_pairs={{0,4},{2,6},{4,0},{6,2},{1,5},{3,7},{5,1},{7,3},{8,12},{10,14},{12... | collective-permute-start | bytes 786440 | tf_op jit(solution)/shard_map/ppermute | solution.py:655
  212.2 25.3 %collective-permute-start.32 = (bf16[64,2048]{1,0:T(8,128)(2,1)S(1)}, bf16[64,2048]{1,0:T(8,128)(2,1)S(1)}, u32[]{:S(2)}, u32[]{:S(2)}) collective-permute-start(bf16[64,2048]{1,0:T(8,128)(2,1)S(1)} %get-tuple-element.42), channel_id=1, source_target_pairs={{0,6},{2,4},{4,2},{6,0},{1,7},{3,5},{5,3},{7,1},{8,14},{10,12},{12... | collective-permute-start | bytes 786440 | tf_op jit(solution)/shard_map/ppermute | solution.py:655
  (15 other events, 87.8 us)

commit v3 on v2

--- a/solution.py
+++ b/solution.py
@@ -212,7 +212,7 @@
     )(*blocks, earlier)
 
 
-def project_kernel(plan, at, *refs):
+def project_kernel(plan, stage, at, *refs):
     slots, count, inputs, down_rows = plan
     arrays, outs = refs[:count], refs[count : count + len(inputs)]
     mark, joined, down = refs[count + len(inputs) :]
@@ -228,7 +228,7 @@
         at_row = part((seq ^ k) * rows, rows)
         joined[at_row, part(core * width, width)] = arrays[mine][:rows, :]
         joined[at_row, part((1 - core) * width, width)] = arrays[other][:rows, :]
-    for n, (_, downs, _) in enumerate(inputs):
+    for n, (_, downs, _, _) in enumerate(inputs if stage != 1 else ()):
         if down_rows is None:
             down[:, n * HD : (n + 1) * HD] = arrays[downs][...]
             continue
@@ -249,21 +249,27 @@
                 down[n * HD : (n + 1) * HD, part(begin, down_rows)] = arrays[index][
                     row : row + HD, j * down_rows : (j + 1) * down_rows
                 ]
-    if down_rows is None:
+    if stage == 1:
+        low = None
+    elif down_rows is None:
         low = jnp.dot(joined[...], down[...], preferred_element_type=F32).astype(BF16)
     else:
         low = scores_of(joined[...], down[...]).astype(BF16)
-    for n, ((weights, _, up), out) in enumerate(zip(inputs, outs)):
-        total = jnp.dot(
-            low[:, n * HD : (n + 1) * HD], arrays[up][...], preferred_element_type=F32
-        )
+    for n, ((weights, _, up, begun), out) in enumerate(zip(inputs, outs)):
+        total = 0.0
+        if stage != 1:
+            total = jnp.dot(
+                low[:, n * HD : (n + 1) * HD], arrays[up][...], preferred_element_type=F32
+            )
+        if begun is not None:
+            total += arrays[begun][...]
         for index, row, size, k, start, shard in weights:
             columns = joined[...] if k is None else joined[:, part((dp ^ k) * shard + start, size)]
             total += jnp.dot(columns, arrays[index][row : row + size, :], preferred_element_type=F32)
-        out[...] = total.astype(BF16)
-
-
-def project(at, slots, rows, inputs, down_rows):
+        out[...] = total.astype(out.dtype)
+
+
+def project(at, slots, rows, inputs, down_rows, stage=0, begun=(None, None, None)):
     arrays = []
 
     def place(array):
@@ -275,19 +281,22 @@
 
     placed = tuple(tuple(place(x) for x in slot) for slot in slots)
     plans = []
-    for weights, downs, up in inputs:
+    for (weights, downs, up), so_far in zip(inputs, begun):
         weights = tuple((place(piece[0]), *piece[1:]) for piece in weights)
-        if down_rows is None:
+        if stage == 1:
+            downs = None
+        elif down_rows is None:
             downs = place(downs)
         elif downs is not None:
             downs = tuple((place(piece[0]), *piece[1:]) for piece in downs)
-        plans.append((weights, downs, place(up)))
+        so_far = None if so_far is None else place(so_far)
+        plans.append((weights, downs, None if stage == 1 else place(up), so_far))
     width = 2 * slots[0][0].shape[1]
     columns = inputs[0][2].shape[1]
-    result = jax.ShapeDtypeStruct((rows, columns), BF16)
+    result = jax.ShapeDtypeStruct((rows, columns), F32 if stage == 1 else BF16)
     ranks = len(inputs) * HD
     return pl.pallas_call(
-        functools.partial(project_kernel, (placed, len(arrays), tuple(plans), down_rows)),
+        functools.partial(project_kernel, (placed, len(arrays), tuple(plans), down_rows), stage),
         out_shape=(*(result,) * len(inputs), MARK),
         in_specs=[pl.BlockSpec(memory_space=SMEM)]
         + [pl.BlockSpec(memory_space=pltpu.VMEM)] * len(arrays),
@@ -543,17 +552,24 @@
     return query, mark, [top, bottom]
 
 
-def key_value_4(at, blocks, rows, weights, near, last, downs, ups, down_rows, *late):
+def begin_4(at, blocks, rows, weights, near, ups, down_rows):
     shard = weights.shape[0] // 2
+    inputs = []
+    for n in range(2):
+        pieces = [(x, n * shard, shard, k, 0, shard) for k, x in enumerate((weights, *near))]
+        inputs.append((pieces, None, ups[n]))
+    return project(at, blocks, rows, inputs, down_rows, 1)
+
+
+def finish_4(at, blocks, rows, last, downs, ups, down_rows, begun, *late):
+    shard = last[0].shape[0] - 2 * HD
     other = other_core(assemble([(x, row, 2 * HD) for x, row in downs], *late))
     inputs = []
     for n in range(2):
-        pieces = [(x, n * shard, shard, k, 0, shard) for k, x in enumerate((weights, *near))]
-        pieces.append((last[n], 0, shard, 3, 0, shard))
         small = [(x, row + n * HD, k, 0) for k, (x, row) in enumerate(downs)]
         small += [(other, (2 * k + n) * HD, k, 1) for k in range(4)]
-        inputs.append((pieces, small, ups[n]))
-    return project(at, blocks, rows, inputs, down_rows)
+        inputs.append(([(last[n], 0, shard, 3, 0, shard)], small, ups[n]))
+    return project(at, blocks, rows, inputs, down_rows, 2, begun)
 
 
 def shards(
@@ -633,11 +649,12 @@
         far = lax.ppermute(down, "dp", swap(4, 3))
         output_own = cut(output_weights[0], 0, output_weights.shape[1], *near, far, marks[3])
         by_x, by_y = both_ways(output_own)
-        last = halves_on(*near, down, by_x, by_y, queries[3])
-        top, bottom = halves_on(by_x, by_y, None, *last)
+        *begun, mark = begin_4(at, blocks, rows, weights, near, ups[1:], down_rows)
+        top, bottom = halves_on(by_x, by_y, None)
+        last = halves_on(*near, down, queries[3], sent[2], top, bottom)
         downs = [(down, 0), (last[1], shard), (last[0], shard), (far, 0)]
-        key, value, _ = key_value_4(
-            at, blocks, rows, weights, near, last, downs, ups[1:], down_rows, *list(sent.values())[1:]
+        key, value, _ = finish_4(
+            at, blocks, rows, last, downs, ups[1:], down_rows, begun, sent[1], sent[3], mark
         )
         out_mine = [output_own, by_x, by_y, top, bottom]
         out_other = [

time: 240 us -> 226 us (0.942)
  waiting for transfers between devices: 137 us -> 118 us
  local copies, waits for them, and re-layouts: 8.36 us -> 11.3 us
    ppermute x3, waiting for transfers between devices: 38 us -> 16.9 us  [shards(): lax.ppermute(parts[k], 'seq', swap(seq_count, k))]
    ppermute x6, waiting for transfers between devices: 10.6 us -> 0.02 us  [along_x(): return lax.ppermute(x, 'dp', swap(4, 1))]
    ppermute x1, waiting for transfers between devices: 1.83 us -> 8.68 us  [shards(): far = lax.ppermute(down, 'dp', swap(4, 3))]
    ppermute x6, waiting for transfers between devices: 51.7 us -> 54.9 us  [spread(): blocks[k] = lax.ppermute(blocks[k ^ step], 'seq', swap(count, step))]
    pallas_call x2 -> x3, Pallas kernels: 16.3 us -> 18.6 us  [project(): pl.pallas_call(functools.partial(project_kernel, (placed, len(arrays), tu...]
    unnamed x60 -> x62, local copies, waits for them, and re-layouts: 7.6 us -> 9.87 us
  transfers between devices with their start and end apart: 33 -> 33, of which waited for: 18 -> 14; matrix products, arithmetic and copies ran while one was open for 0% -> 0% of each run, Pallas kernels for 21% -> 22%
where the time goes in v3:
time: 226 us
  waiting for transfers between devices  118 us (52%)
  Pallas kernels  61.6 us (27%)
  starting transfers between devices  33 us (15%)
  local copies, waits for them, and re-layouts  11.3 us (5%)
    ppermute x6, waiting for transfers between devices, spread(): blocks[k] = lax.ppermute(blocks[k ^ step], 'seq', swap(count, step))  54.9 us
    pallas_call x4, Pallas kernels, cache_attention(): pl.pallas_call(functools.partial(cache_kernel, slot, heads), out_shape=(j...  24.7 us
    ppermute x3, waiting for transfers between devices, shards(): lax.ppermute(sums[k], 'seq', swap(seq_count, k))  22.9 us
    pallas_call x3, Pallas kernels, project(): pl.pallas_call(functools.partial(project_kernel, (placed, len(arrays), tu...  18.6 us
    ppermute x3, waiting for transfers between devices, shards(): lax.ppermute(parts[k], 'seq', swap(seq_count, k))  16.9 us
    unnamed x62, local copies, waits for them, and re-layouts  9.87 us
    ppermute x6, waiting for transfers between devices, along_y(): return lax.ppermute(x, 'dp', swap(4, 2))  9.66 us
    ppermute x6, starting transfers between devices, spread(): blocks[k] = lax.ppermute(blocks[k ^ step], 'seq', swap(count, step))  9.61 us
  transfers between devices with their start and end apart: 33, of which 14 were waited for; matrix products, arithmetic and copies ran while one was open for 0% of the time, Pallas kernels for 22%

profile of v3, /device:TPU:16, one launch (start us, length us, event | category | flops | bytes accessed | tf_op | source)
XLA Modules:
  0.0 225.7 jit_solution(471196462793198980)
XLA Ops:
  2.0 3.4 %norm.1 = (bf16[176,2048]{1,0:T(8,128)(2,1)}, s32[1]{0:T(128)}) custom-call(s32[5]{0:T(128)} %stack.15.at, bf16[128,2048]{1,0:T(8,128)(2,1)} %refs_0_.1, bf16[128,2048]{1,0:T(8,128)(2,1)} %refs_1_.1, f32[1,4096]{1,0:T(1,128)} %bitcast.24, bf16[512,384]{1,0:T(8,128)(2,1)} %refs_3_.1), custom_call_target="tpu_custom_call" | custom-call | flops 1 | bytes 1 | tf_op jit(solution)/shard_map/norm/pallas_call | solution.py:164
  5.4 1.9 copy-done.12
  7.3 0.8 cut.3.refs_8_
  8.1 1.6 collective-permute-start.8
  9.7 1.5 collective-permute-start.7
  11.5 1.6 collective-permute-start.1
  13.1 28.8 %collective-permute-done.3.refs_1_.refs_4_.refs_2_ = bf16[176,2048]{1,0:T(8,128)(2,1)S(1)} collective-permute-done((bf16[176,2048]{1,0:T(8,128)(2,1)S(1)}, bf16[176,2048]{1,0:T(8,128)(2,1)S(1)}, u32[]{:S(2)}, u32[]{:S(2)}) %collective-permute-start.3) | collective-permute-done | bytes 720928 | tf_op jit(solution)/shard_map/ppermute | solution.py:83
  41.9 4.5 %collective-permute-start.5 = (bf16[176,2048]{1,0:T(8,128)(2,1)S(1)}, bf16[176,2048]{1,0:T(8,128)(2,1)S(1)}, u32[]{:S(2)}, u32[]{:S(2)}) collective-permute-start(bf16[176,2048]{1,0:T(8,128)(2,1)S(1)} %collective-permute-done.3.refs_1_.refs_4_.refs_2_), channel_id=1, source_target_pairs={{0,2},{2,0},{4,6},{6,4},{1,3},{3,1},{5,7},{7,5},{8,10},{10,8},{12,... | collective-permute-start | bytes 2162696 | tf_op jit(solution)/shard_map/ppermute | solution.py:83
  48.1 14.5 %collective-permute-done.5.refs_6_.refs_1_.refs_3_ = bf16[176,2048]{1,0:T(8,128)(2,1)S(1)} collective-permute-done((bf16[176,2048]{1,0:T(8,128)(2,1)S(1)}, bf16[176,2048]{1,0:T(8,128)(2,1)S(1)}, u32[]{:S(2)}, u32[]{:S(2)}) %collective-permute-start.5) | collective-permute-done | bytes 720928 | tf_op jit(solution)/shard_map/ppermute | solution.py:83
  62.7 1.6 cut.4.refs_8_
  66.1 1.5 collective-permute-done.6.refs_7_
  67.7 6.6 %project.3 = (bf16[512,512]{1,0:T(8,128)(2,1)S(1)}, s32[1]{0:T(128)}) custom-call(s32[5]{0:T(128)S(1)} %copy-done.27, bf16[176,2048]{1,0:T(8,128)(2,1)S(1)} %copy-done.14, bf16[176,2048]{1,0:T(8,128)(2,1)S(1)} %collective-permute-done.refs_1_.refs_2_, bf16[176,2048]{1,0:T(8,128)(2,1)S(1)} %collective-permute-done.1.refs_2_.refs_1_, ...), custom_call_target="tpu_custom_call" | custom-call | flops 1 | bytes 1 | tf_op jit(solution)/shard_map/project/pallas_call | solution.py:298
  74.2 1.8 collective-permute-start.11
  76.1 2.3 %arrange.1.refs_1_.refs_0_.refs_9_ = bf16[256,512]{1,0:T(8,128)(2,1)} custom-call(bf16[176,2048]{1,0:T(8,128)(2,1)} %get-tuple-element.27.refs_0_, bf16[176,2048]{1,0:T(8,128)(2,1)} %copy-done.16, bf16[176,2048]{1,0:T(8,128)(2,1)} %copy-done.4, bf16[176,2048]{1,0:T(8,128)(2,1)} %copy-done.6, s32[1]{0:T(128)} %get-tuple-element.29.earlier.refs_4_), custom_call_target="tpu_custom_call" | custom-call | flops 1 | bytes 1 | tf_op jit(solution)/shard_map/arrange/pallas_call | solution.py:201
  78.4 2.5 %collective-permute-start.19 = (bf16[256,512]{1,0:T(8,128)(2,1)}, bf16[256,512]{1,0:T(8,128)(2,1)S(1)}, u32[]{:S(2)}, u32[]{:S(2)}) collective-permute-start(bf16[256,512]{1,0:T(8,128)(2,1)} %arrange.1.refs_1_.refs_0_.refs_9_), channel_id=1, source_target_pairs={{0,24},{8,16},{16,8},{24,0},{1,25},{9,17},{17,9},{25,1},{2,26},{10... | collective-permute-start | bytes 786440 | tf_op jit(solution)/shard_map/ppermute | solution.py:649
  80.9 2.2 copy-done
  83.1 2.2 copy-done.2
  85.3 1.2 copy-done.8
  86.5 1.2 copy-done.10
  87.8 5.9 %cache_attention.4 = (bf16[528,512]{1,0:T(8,128)(2,1)S(1)}, s32[1]{0:T(128)}) custom-call(s32[5]{0:T(128)S(1)} %copy-done.27, s32[1]{0:T(128)} %get-tuple-element.29.earlier.refs_4_, s32[16]{0:T(128)S(1)} %bitcast.20, bf16[512,512]{1,0:T(8,128)(2,1)S(1)} %get-tuple-element.30.query_ref, bf16[1,1024,2048]{2,1,0:T(8,128)(2,1)S(1)} %copy-done, ...), custom_call_target="tpu_custom_call" | custom-call | flops 1 | bytes 1 | tf_op jit(solution)/shard_map/cache_attention/pallas_call | solution.py:386
  93.7 3.1 %collective-permute-done.11.query_ref = bf16[512,512]{1,0:T(8,128)(2,1)} collective-permute-done((bf16[512,512]{1,0:T(8,128)(2,1)S(1)}, bf16[512,512]{1,0:T(8,128)(2,1)}, u32[]{:S(2)}, u32[]{:S(2)}) %collective-permute-start.11) | collective-permute-done | bytes 524320 | tf_op jit(solution)/shard_map/ppermute | solution.py:83
  96.8 6.5 %cache_attention.5 = (bf16[528,512]{1,0:T(8,128)(2,1)S(1)}, s32[1]{0:T(128)}) custom-call(s32[5]{0:T(128)S(1)} %copy-done.27, s32[1]{0:T(128)} %get-tuple-element.32.earlier, s32[16]{0:T(128)S(1)} %bitcast.21, bf16[512,512]{1,0:T(8,128)(2,1)} %collective-permute-done.11.query_ref, bf16[1,1024,2048]{2,1,0:T(8,128)(2,1)S(1)} %copy-done.1, ...), custom_call_target="tpu_custom_call" | custom-call | flops 1 | bytes 1 | tf_op jit(solution)/shard_map/cache_attention/pallas_call | solution.py:386
  103.4 6.3 %cache_attention.6 = (bf16[528,512]{1,0:T(8,128)(2,1)S(1)}, s32[1]{0:T(128)}) custom-call(s32[5]{0:T(128)S(1)} %copy-done.27, s32[1]{0:T(128)} %get-tuple-element.34.earlier, s32[16]{0:T(128)S(1)} %bitcast.22, bf16[512,512]{1,0:T(8,128)(2,1)} %collective-permute-done.13.query_ref, bf16[1,1024,2048]{2,1,0:T(8,128)(2,1)S(1)} %copy-done.1, ...), custom_call_target="tpu_custom_call" | custom-call | flops 1 | bytes 1 | tf_op jit(solution)/shard_map/cache_attention/pallas_call | solution.py:386
  109.7 8.7 %collective-permute-done.19.refs_3_.refs_11_ = bf16[256,512]{1,0:T(8,128)(2,1)S(1)} collective-permute-done((bf16[256,512]{1,0:T(8,128)(2,1)}, bf16[256,512]{1,0:T(8,128)(2,1)S(1)}, u32[]{:S(2)}, u32[]{:S(2)}) %collective-permute-start.19) | collective-permute-done | bytes 262176 | tf_op jit(solution)/shard_map/ppermute | solution.py:649
  120.2 1.4 collective-permute-start.15
  121.6 9.6 %collective-permute-done.22.refs_0_.refs_2_ = bf16[512,512]{1,0:T(8,128)(2,1)S(1)} collective-permute-done((bf16[512,512]{1,0:T(8,128)(2,1)S(1)}, bf16[512,512]{1,0:T(8,128)(2,1)S(1)}, u32[]{:S(2)}, u32[]{:S(2)}) %collective-permute-start.22) | collective-permute-done | bytes 524320 | tf_op jit(solution)/shard_map/ppermute | solution.py:92
  131.9 2.3 %collective-permute-start.21 = (bf16[256,512]{1,0:T(8,128)(2,1)S(1)}, bf16[256,512]{1,0:T(8,128)(2,1)S(1)}, u32[]{:S(2)}, u32[]{:S(2)}) collective-permute-start(bf16[256,512]{1,0:T(8,128)(2,1)S(1)} %assemble.11), channel_id=1, source_target_pairs={{0,16},{8,24},{16,0},{24,8},{1,17},{9,25},{17,1},{25,9},{2,18},{10... | collective-permute-start | bytes 786440 | tf_op jit(solution)/shard_map/ppermute | solution.py:92
  134.2 8.5 %collective-permute-done.15.query_ref.refs_2_ = bf16[512,512]{1,0:T(8,128)(2,1)S(1)} collective-permute-done((bf16[512,512]{1,0:T(8,128)(2,1)}, bf16[512,512]{1,0:T(8,128)(2,1)S(1)}, u32[]{:S(2)}, u32[]{:S(2)}) %collective-permute-start.15) | collective-permute-done | bytes 524320 | tf_op jit(solution)/shard_map/ppermute | solution.py:83
  142.8 1.7 assemble.13
  144.5 1.6 collective-permute-start.24
  146.1 1.6 collective-permute-start.25
  147.7 2.9 %collective-permute-start.12 = (bf16[528,512]{1,0:T(8,128)(2,1)S(1)}, bf16[528,512]{1,0:T(8,128)(2,1)S(1)}, u32[]{:S(2)}, u32[]{:S(2)}) collective-permute-start(bf16[528,512]{1,0:T(8,128)(2,1)S(1)} %get-tuple-element.33), channel_id=1, source_target_pairs={{0,2},{2,0},{4,6},{6,4},{1,3},{3,1},{5,7},{7,5},{8,10},{10,8},{12,... | collective-permute-start | bytes 1622024 | tf_op jit(solution)/shard_map/ppermute | solution.py:641
  150.6 5.9 %cache_attention.7 = (bf16[528,512]{1,0:T(8,128)(2,1)S(1)}, s32[1]{0:T(128)}) custom-call(s32[5]{0:T(128)S(1)} %copy-done.27, s32[1]{0:T(128)} %get-tuple-element.36.earlier.refs_4_, s32[16]{0:T(128)S(1)} %bitcast.23, bf16[512,512]{1,0:T(8,128)(2,1)S(1)} %collective-permute-done.15.query_ref.refs_2_, bf16[1,1024,2048]{2,1,0:T(8,128)(2,1)S(1)} %copy-done.1, ...), custom_call_target="tpu_custom_call" | custom-call | flops 1 | bytes 1 | tf_op jit(solution)/shard_map/cache_attention/pallas_call | solution.py:386
  158.3 5.9 %project.4 = (f32[512,512]{1,0:T(8,128)S(1)}, f32[512,512]{1,0:T(8,128)S(1)}, s32[1]{0:T(128)}) custom-call(s32[5]{0:T(128)S(1)} %copy-done.27, bf16[176,2048]{1,0:T(8,128)(2,1)S(1)} %copy-done.15, bf16[176,2048]{1,0:T(8,128)(2,1)S(1)} %copy-done.19, bf16[176,2048]{1,0:T(8,128)(2,1)S(1)} %copy-done.17, bf16[176,2048]{1,0:T(8,128)(2,1)S(1)} %copy-done.23, ...), custom_call_target="tpu_custom_call" | custom-call | flops 1 | bytes 1 | tf_op jit(solution)/shard_map/project/pallas_call | solution.py:298
  164.2 8.7 %collective-permute-done.12.refs_4_.refs_1_ = bf16[528,512]{1,0:T(8,128)(2,1)S(1)} collective-permute-done((bf16[528,512]{1,0:T(8,128)(2,1)S(1)}, bf16[528,512]{1,0:T(8,128)(2,1)S(1)}, u32[]{:S(2)}, u32[]{:S(2)}) %collective-permute-start.12) | collective-permute-done | bytes 540704 | tf_op jit(solution)/shard_map/ppermute | solution.py:641
  172.9 8.2 %collective-permute-done.16.refs_5_.refs_3_ = bf16[528,512]{1,0:T(8,128)(2,1)S(1)} collective-permute-done((bf16[528,512]{1,0:T(8,128)(2,1)S(1)}, bf16[528,512]{1,0:T(8,128)(2,1)S(1)}, u32[]{:S(2)}, u32[]{:S(2)}) %collective-permute-start.16) | collective-permute-done | bytes 540704 | tf_op jit(solution)/shard_map/ppermute | solution.py:641
  182.6 2.0 collective-permute-done.26.refs_12_
  184.7 6.2 %project.5 = (bf16[512,512]{1,0:T(8,128)(2,1)S(1)}, bf16[512,512]{1,0:T(8,128)(2,1)S(1)}, s32[1]{0:T(128)}) custom-call(s32[5]{0:T(128)S(1)} %copy-done.27, bf16[176,2048]{1,0:T(8,128)(2,1)S(1)} %copy-done.15, bf16[176,2048]{1,0:T(8,128)(2,1)S(1)} %copy-done.19, bf16[176,2048]{1,0:T(8,128)(2,1)S(1)} %copy-done.17, bf16[176,2048]{1,0:T(8,128)(2,1)S(1)} %copy-done.23, ...), custom_call_target="tpu_custom_call" | custom-call | flops 1 | bytes 1 | tf_op jit(solution)/shard_map/project/pallas_call | solution.py:298
  190.8 2.0 new_attention.1.refs_4_
  192.9 1.3 merge.1
  194.4 1.4 collective-permute-done.27.got_ref
  195.8 1.9 output_projection.1
  197.8 1.7 collective-permute-start.31
  199.5 1.7 collective-permute-start.32
  201.3 6.9 %collective-permute-done.30.refs_1_ = bf16[64,2048]{1,0:T(8,128)(2,1)S(1)} collective-permute-done((bf16[64,2048]{1,0:T(8,128)(2,1)S(1)}, bf16[64,2048]{1,0:T(8,128)(2,1)S(1)}, u32[]{:S(2)}, u32[]{:S(2)}) %collective-permute-start.30) | collective-permute-done | bytes 262176 | tf_op jit(solution)/shard_map/ppermute | solution.py:672
  208.1 9.3 %collective-permute-done.31.refs_2_ = bf16[64,2048]{1,0:T(8,128)(2,1)S(1)} collective-permute-done((bf16[64,2048]{1,0:T(8,128)(2,1)S(1)}, bf16[64,2048]{1,0:T(8,128)(2,1)S(1)}, u32[]{:S(2)}, u32[]{:S(2)}) %collective-permute-start.31) | collective-permute-done | bytes 262176 | tf_op jit(solution)/shard_map/ppermute | solution.py:672
  217.5 6.7 %collective-permute-done.32.refs_3_ = bf16[64,2048]{1,0:T(8,128)(2,1)S(1)} collective-permute-done((bf16[64,2048]{1,0:T(8,128)(2,1)S(1)}, bf16[64,2048]{1,0:T(8,128)(2,1)S(1)}, u32[]{:S(2)}, u32[]{:S(2)}) %collective-permute-start.32) | collective-permute-done | bytes 262176 | tf_op jit(solution)/shard_map/ppermute | solution.py:672
  224.3 1.4 final_sum.1
  (109 shorter events, 10.6 us)
Async XLA Ops:
  8.1 38.2 %collective-permute-start.8 = (bf16[1024,512]{1,0:T(8,128)(2,1)S(1)}, bf16[1024,512]{1,0:T(8,128)(2,1)S(1)}, u32[]{:S(2)}, u32[]{:S(2)}) collective-permute-start(bf16[1024,512]{1,0:T(8,128)(2,1)S(1)} %cut.3.refs_8_), channel_id=1, source_target_pairs={{0,16},{8,24},{16,0},{24,8},{1,17},{9,25},{17,1},{25,9},{2,18},{10... | collective-permute-start | bytes 3145736 | tf_op jit(solution)/shard_map/ppermute | solution.py:92
  9.7 37.2 %collective-permute-start.7 = (bf16[1024,512]{1,0:T(8,128)(2,1)S(1)}, bf16[1024,512]{1,0:T(8,128)(2,1)S(1)}, u32[]{:S(2)}, u32[]{:S(2)}) collective-permute-start(bf16[1024,512]{1,0:T(8,128)(2,1)S(1)} %cut.3.refs_8_), channel_id=1, source_target_pairs={{0,8},{8,0},{16,24},{24,16},{1,9},{9,1},{17,25},{25,17},{2,10},{10... | collective-permute-start | bytes 3145736 | tf_op jit(solution)/shard_map/ppermute | solution.py:88
  11.2 51.5 %copy-start.13 = (bf16[1024,3,1,512]{3,0,2,1:T(8,128)(2,1)S(1)}, bf16[1024,3,1,512]{3,0,2,1:T(8,128)(2,1)}, u32[]{:S(2)}) copy-start(bf16[1024,3,1,512]{3,0,2,1:T(8,128)(2,1)} %param.18) | copy-start | bytes 9437188
  11.2 30.7 %collective-permute-start.3 = (bf16[176,2048]{1,0:T(8,128)(2,1)S(1)}, bf16[176,2048]{1,0:T(8,128)(2,1)S(1)}, u32[]{:S(2)}, u32[]{:S(2)}) collective-permute-start(bf16[176,2048]{1,0:T(8,128)(2,1)S(1)} %copy-done.14), channel_id=1, source_target_pairs={{0,4},{2,6},{4,0},{6,2},{1,5},{3,7},{5,1},{7,3},{8,12},{10,14},{12... | collective-permute-start | bytes 2162696 | tf_op jit(solution)/shard_map/ppermute | solution.py:83
  11.5 34.8 %collective-permute-start.1 = (bf16[176,2048]{1,0:T(8,128)(2,1)S(1)}, bf16[176,2048]{1,0:T(8,128)(2,1)S(1)}, u32[]{:S(2)}, u32[]{:S(2)}) collective-permute-start(bf16[176,2048]{1,0:T(8,128)(2,1)S(1)} %copy-done.14), channel_id=1, source_target_pairs={{0,2},{2,0},{4,6},{6,4},{1,3},{3,1},{5,7},{7,5},{8,10},{10,8},{12,... | collective-permute-start | bytes 2162696 | tf_op jit(solution)/shard_map/ppermute | solution.py:83
  13.1 34.5 %collective-permute-start = (bf16[176,2048]{1,0:T(8,128)(2,1)S(1)}, bf16[176,2048]{1,0:T(8,128)(2,1)S(1)}, u32[]{:S(2)}, u32[]{:S(2)}) collective-permute-start(bf16[176,2048]{1,0:T(8,128)(2,1)S(1)} %copy-done.14), channel_id=1, source_target_pairs={{0,1},{1,0},{2,3},{3,2},{4,5},{5,4},{6,7},{7,6},{8,9},{9,8},{10,11... | collective-permute-start | bytes 2162696 | tf_op jit(solution)/shard_map/ppermute | solution.py:108
  41.9 25.8 %copy-start.4 = (bf16[176,2048]{1,0:T(8,128)(2,1)}, bf16[176,2048]{1,0:T(8,128)(2,1)S(1)}, u32[]{:S(2)}) copy-start(bf16[176,2048]{1,0:T(8,128)(2,1)S(1)} %collective-permute-done.3.refs_1_.refs_4_.refs_2_) | copy-start | bytes 2162692
  41.9 20.8 %collective-permute-start.5 = (bf16[176,2048]{1,0:T(8,128)(2,1)S(1)}, bf16[176,2048]{1,0:T(8,128)(2,1)S(1)}, u32[]{:S(2)}, u32[]{:S(2)}) collective-permute-start(bf16[176,2048]{1,0:T(8,128)(2,1)S(1)} %collective-permute-done.3.refs_1_.refs_4_.refs_2_), channel_id=1, source_target_pairs={{0,2},{2,0},{4,6},{6,4},{1,3},{3,1},{5,7},{7,5},{8,10},{10,8},{12,... | collective-permute-start | bytes 2162696 | tf_op jit(solution)/shard_map/ppermute | solution.py:83
  46.3 21.3 %copy-start.16 = (bf16[176,2048]{1,0:T(8,128)(2,1)}, bf16[176,2048]{1,0:T(8,128)(2,1)S(1)}, u32[]{:S(2)}) copy-start(bf16[176,2048]{1,0:T(8,128)(2,1)S(1)} %collective-permute-done.1.refs_2_.refs_1_) | copy-start | bytes 2162692
  46.3 16.3 %collective-permute-start.4 = (bf16[176,2048]{1,0:T(8,128)(2,1)S(1)}, bf16[176,2048]{1,0:T(8,128)(2,1)S(1)}, u32[]{:S(2)}, u32[]{:S(2)}) collective-permute-start(bf16[176,2048]{1,0:T(8,128)(2,1)S(1)} %collective-permute-done.3.refs_1_.refs_4_.refs_2_), channel_id=1, source_target_pairs={{0,1},{1,0},{2,3},{3,2},{4,5},{5,4},{6,7},{7,6},{8,9},{9,8},{10,11... | collective-permute-start | bytes 2162696 | tf_op jit(solution)/shard_map/ppermute | solution.py:108
  46.3 16.3 %collective-permute-start.2 = (bf16[176,2048]{1,0:T(8,128)(2,1)S(1)}, bf16[176,2048]{1,0:T(8,128)(2,1)S(1)}, u32[]{:S(2)}, u32[]{:S(2)}) collective-permute-start(bf16[176,2048]{1,0:T(8,128)(2,1)S(1)} %collective-permute-done.1.refs_2_.refs_1_), channel_id=1, source_target_pairs={{0,1},{1,0},{2,3},{3,2},{4,5},{5,4},{6,7},{7,6},{8,9},{9,8},{10,11... | collective-permute-start | bytes 2162696 | tf_op jit(solution)/shard_map/ppermute | solution.py:108
  46.9 15.8 %collective-permute-start.10 = (bf16[512,512]{1,0:T(8,128)(2,1)S(1)}, bf16[512,512]{1,0:T(8,128)(2,1)S(1)}, u32[]{:S(2)}, u32[]{:S(2)}) collective-permute-start(bf16[512,512]{1,0:T(8,128)(2,1)S(1)} %assemble.10), channel_id=1, source_target_pairs={{0,8},{8,0},{16,24},{24,16},{1,9},{9,1},{17,25},{25,17},{2,10},{10... | collective-permute-start | bytes 1572872 | tf_op jit(solution)/shard_map/ppermute | solution.py:88
  47.5 17.9 %copy-start.29 = (bf16[3,128,1,512]{3,1,2,0:T(8,128)(2,1)S(1)}, bf16[3,128,1,512]{3,1,2,0:T(8,128)(2,1)}, u32[]{:S(2)}) copy-start(bf16[3,128,1,512]{3,1,2,0:T(8,128)(2,1)} %param.20) | copy-start | bytes 1179652
  47.5 20.1 %copy-start.27 = (s32[5]{0:T(128)S(1)}, s32[5]{0:T(128)}, u32[]{:S(2)}) copy-start(s32[5]{0:T(128)} %stack.15.at) | copy-start | bytes 64
  47.6 20.1 %copy-start.18 = (bf16[176,2048]{1,0:T(8,128)(2,1)}, bf16[176,2048]{1,0:T(8,128)(2,1)S(1)}, u32[]{:S(2)}) copy-start(bf16[176,2048]{1,0:T(8,128)(2,1)S(1)} %collective-permute-done.refs_1_.refs_2_) | copy-start | bytes 2162692
  47.6 15.1 %collective-permute-start.9 = (bf16[512,512]{1,0:T(8,128)(2,1)S(1)}, bf16[512,512]{1,0:T(8,128)(2,1)S(1)}, u32[]{:S(2)}, u32[]{:S(2)}) collective-permute-start(bf16[512,512]{1,0:T(8,128)(2,1)S(1)} %assemble.9), channel_id=1, source_target_pairs={{0,16},{8,24},{16,0},{24,8},{1,17},{9,25},{17,1},{25,9},{2,18},{10... | collective-permute-start | bytes 1572872 | tf_op jit(solution)/shard_map/ppermute | solution.py:92
  64.3 54.1 %collective-permute-start.18 = (bf16[2048,512]{1,0:T(8,128)(2,1)}, bf16[2048,512]{1,0:T(8,128)(2,1)S(1)}, u32[]{:S(2)}, u32[]{:S(2)}) collective-permute-start(bf16[2048,512]{1,0:T(8,128)(2,1)} %cut.4.refs_8_), channel_id=1, source_target_pairs={{0,16},{8,24},{16,0},{24,8},{1,17},{9,25},{17,1},{25,9},{2,18},{10... | collective-permute-start | bytes 6291464 | tf_op jit(solution)/shard_map/ppermute | solution.py:92
  64.9 53.5 %collective-permute-start.17 = (bf16[2048,512]{1,0:T(8,128)(2,1)}, bf16[2048,512]{1,0:T(8,128)(2,1)}, u32[]{:S(2)}, u32[]{:S(2)}) collective-permute-start(bf16[2048,512]{1,0:T(8,128)(2,1)} %cut.4.refs_8_), channel_id=1, source_target_pairs={{0,8},{8,0},{16,24},{24,16},{1,9},{9,1},{17,25},{25,17},{2,10},{10... | collective-permute-start | bytes 6291464 | tf_op jit(solution)/shard_map/ppermute | solution.py:88
  65.4 2.2 collective-permute-start.6
  74.2 6.7 %copy-start.28 = (s32[1,16]{1,0:T(1,128)S(1)}, s32[1,16]{1,0:T(1,128)}, u32[]{:S(2)}) copy-start(s32[1,16]{1,0:T(1,128)} %param.28) | copy-start | bytes 196
  74.2 22.6 %collective-permute-start.11 = (bf16[512,512]{1,0:T(8,128)(2,1)S(1)}, bf16[512,512]{1,0:T(8,128)(2,1)}, u32[]{:S(2)}, u32[]{:S(2)}) collective-permute-start(bf16[512,512]{1,0:T(8,128)(2,1)S(1)} %get-tuple-element.30.query_ref), channel_id=1, source_target_pairs={{0,2},{2,0},{4,6},{6,4},{1,3},{3,1},{5,7},{7,5},{8,10},{10,8},{12,... | collective-permute-start | bytes 1572872 | tf_op jit(solution)/shard_map/ppermute | solution.py:83
  76.1 27.3 %collective-permute-start.13 = (bf16[512,512]{1,0:T(8,128)(2,1)S(1)}, bf16[512,512]{1,0:T(8,128)(2,1)}, u32[]{:S(2)}, u32[]{:S(2)}) collective-permute-start(bf16[512,512]{1,0:T(8,128)(2,1)S(1)} %get-tuple-element.30.query_ref), channel_id=1, source_target_pairs={{0,4},{2,6},{4,0},{6,2},{1,5},{3,7},{5,1},{7,3},{8,12},{10,14},{12... | collective-permute-start | bytes 1572872 | tf_op jit(solution)/shard_map/ppermute | solution.py:83
  78.4 40.0 %collective-permute-start.19 = (bf16[256,512]{1,0:T(8,128)(2,1)}, bf16[256,512]{1,0:T(8,128)(2,1)S(1)}, u32[]{:S(2)}, u32[]{:S(2)}) collective-permute-start(bf16[256,512]{1,0:T(8,128)(2,1)} %arrange.1.refs_1_.refs_0_.refs_9_), channel_id=1, source_target_pairs={{0,24},{8,16},{16,8},{24,0},{1,25},{9,17},{17,9},{25,1},{2,26},{10... | collective-permute-start | bytes 786440 | tf_op jit(solution)/shard_map/ppermute | solution.py:649
  87.8 9.1 %copy-start.1 = (bf16[1,1024,2048]{2,1,0:T(8,128)(2,1)S(1)}, bf16[1,1024,2048]{2,1,0:T(8,128)(2,1)}, u32[]{:S(2)}) copy-start(bf16[1,1024,2048]{2,1,0:T(8,128)(2,1)} %key_ref.7) | copy-start | bytes 12582916
  87.8 9.1 %copy-start.3 = (bf16[1,1024,2048]{2,1,0:T(8,128)(2,1)S(1)}, bf16[1,1024,2048]{2,1,0:T(8,128)(2,1)}, u32[]{:S(2)}) copy-start(bf16[1,1024,2048]{2,1,0:T(8,128)(2,1)} %value_ref.7) | copy-start | bytes 12582916
  87.8 9.1 %copy-start.9 = (bf16[2,128,2048]{2,1,0:T(8,128)(2,1)S(1)}, bf16[2,128,2048]{2,1,0:T(8,128)(2,1)}, u32[]{:S(2)}) copy-start(bf16[2,128,2048]{2,1,0:T(8,128)(2,1)} %shared_key_ref.7) | copy-start | bytes 3145732
  87.8 9.1 %copy-start.11 = (bf16[2,128,2048]{2,1,0:T(8,128)(2,1)S(1)}, bf16[2,128,2048]{2,1,0:T(8,128)(2,1)}, u32[]{:S(2)}) copy-start(bf16[2,128,2048]{2,1,0:T(8,128)(2,1)} %shared_value_ref.7) | copy-start | bytes 3145732
  103.4 15.0 %copy-start.26 = (bf16[1,512,512]{2,1,0:T(8,128)(2,1)S(1)}, bf16[1,512,512]{2,1,0:T(8,128)(2,1)}, u32[]{:S(2)}) copy-start(bf16[1,512,512]{2,1,0:T(8,128)(2,1)} %param.21) | copy-start | bytes 1572868
  118.4 24.3 %copy-start.24 = (bf16[256,512]{1,0:T(8,128)(2,1)S(1)}, bf16[256,512]{1,0:T(8,128)(2,1)}, u32[]{:S(2)}) copy-start(bf16[256,512]{1,0:T(8,128)(2,1)} %arrange.1.refs_1_.refs_0_.refs_9_) | copy-start | bytes 786436
  119.1 12.2 %collective-permute-start.22 = (bf16[512,512]{1,0:T(8,128)(2,1)S(1)}, bf16[512,512]{1,0:T(8,128)(2,1)S(1)}, u32[]{:S(2)}, u32[]{:S(2)}) collective-permute-start(bf16[512,512]{1,0:T(8,128)(2,1)S(1)} %cut.5.refs_0_), channel_id=1, source_target_pairs={{0,16},{8,24},{16,0},{24,8},{1,17},{9,25},{17,1},{25,9},{2,18},{10... | collective-permute-start | bytes 1572872 | tf_op jit(solution)/shard_map/ppermute | solution.py:92
  119.7 12.2 %collective-permute-start.20 = (bf16[512,512]{1,0:T(8,128)(2,1)S(1)}, bf16[512,512]{1,0:T(8,128)(2,1)S(1)}, u32[]{:S(2)}, u32[]{:S(2)}) collective-permute-start(bf16[512,512]{1,0:T(8,128)(2,1)S(1)} %cut.5.refs_0_), channel_id=1, source_target_pairs={{0,8},{8,0},{16,24},{24,16},{1,9},{9,1},{17,25},{25,17},{2,10},{10... | collective-permute-start | bytes 1572872 | tf_op jit(solution)/shard_map/ppermute | solution.py:88
  120.2 22.6 %collective-permute-start.14 = (bf16[528,512]{1,0:T(8,128)(2,1)S(1)}, bf16[528,512]{1,0:T(8,128)(2,1)S(1)}, u32[]{:S(2)}, u32[]{:S(2)}) collective-permute-start(bf16[528,512]{1,0:T(8,128)(2,1)S(1)} %get-tuple-element.35), channel_id=1, source_target_pairs={{0,4},{2,6},{4,0},{6,2},{1,5},{3,7},{5,1},{7,3},{8,12},{10,14},{12... | collective-permute-start | bytes 1622024 | tf_op jit(solution)/shard_map/ppermute | solution.py:641
  120.2 22.5 %collective-permute-start.15 = (bf16[512,512]{1,0:T(8,128)(2,1)}, bf16[512,512]{1,0:T(8,128)(2,1)S(1)}, u32[]{:S(2)}, u32[]{:S(2)}) collective-permute-start(bf16[512,512]{1,0:T(8,128)(2,1)} %collective-permute-done.13.query_ref), channel_id=1, source_target_pairs={{0,2},{2,0},{4,6},{6,4},{1,3},{3,1},{5,7},{7,5},{8,10},{10,8},{12,... | collective-permute-start | bytes 1572872 | tf_op jit(solution)/shard_map/ppermute | solution.py:83
  131.3 11.5 %collective-permute-start.23 = (bf16[256,512]{1,0:T(8,128)(2,1)S(1)}, bf16[256,512]{1,0:T(8,128)(2,1)S(1)}, u32[]{:S(2)}, u32[]{:S(2)}) collective-permute-start(bf16[256,512]{1,0:T(8,128)(2,1)S(1)} %assemble.12), channel_id=1, source_target_pairs={{0,8},{8,0},{16,24},{24,16},{1,9},{9,1},{17,25},{25,17},{2,10},{10... | collective-permute-start | bytes 786440 | tf_op jit(solution)/shard_map/ppermute | solution.py:88
  131.9 10.8 %collective-permute-start.21 = (bf16[256,512]{1,0:T(8,128)(2,1)S(1)}, bf16[256,512]{1,0:T(8,128)(2,1)S(1)}, u32[]{:S(2)}, u32[]{:S(2)}) collective-permute-start(bf16[256,512]{1,0:T(8,128)(2,1)S(1)} %assemble.11), channel_id=1, source_target_pairs={{0,16},{8,24},{16,0},{24,8},{1,17},{9,25},{17,1},{25,9},{2,18},{10... | collective-permute-start | bytes 786440 | tf_op jit(solution)/shard_map/ppermute | solution.py:92
  144.5 36.7 %collective-permute-start.24 = (bf16[1280,512]{1,0:T(8,128)(2,1)S(1)}, bf16[1280,512]{1,0:T(8,128)(2,1)S(1)}, u32[]{:S(2)}, u32[]{:S(2)}) collective-permute-start(bf16[1280,512]{1,0:T(8,128)(2,1)S(1)} %assemble.13), channel_id=1, source_target_pairs={{0,16},{8,24},{16,0},{24,8},{1,17},{9,25},{17,1},{25,9},{2,18},{10... | collective-permute-start | bytes 3932168 | tf_op jit(solution)/shard_map/ppermute | solution.py:92
  146.1 35.0 %collective-permute-start.25 = (bf16[1280,512]{1,0:T(8,128)(2,1)S(1)}, bf16[1280,512]{1,0:T(8,128)(2,1)S(1)}, u32[]{:S(2)}, u32[]{:S(2)}) collective-permute-start(bf16[1280,512]{1,0:T(8,128)(2,1)S(1)} %assemble.14), channel_id=1, source_target_pairs={{0,8},{8,0},{16,24},{24,16},{1,9},{9,1},{17,25},{25,17},{2,10},{10... | collective-permute-start | bytes 3932168 | tf_op jit(solution)/shard_map/ppermute | solution.py:88
  147.7 25.3 %collective-permute-start.12 = (bf16[528,512]{1,0:T(8,128)(2,1)S(1)}, bf16[528,512]{1,0:T(8,128)(2,1)S(1)}, u32[]{:S(2)}, u32[]{:S(2)}) collective-permute-start(bf16[528,512]{1,0:T(8,128)(2,1)S(1)} %get-tuple-element.33), channel_id=1, source_target_pairs={{0,2},{2,0},{4,6},{6,4},{1,3},{3,1},{5,7},{7,5},{8,10},{10,8},{12,... | collective-permute-start | bytes 1622024 | tf_op jit(solution)/shard_map/ppermute | solution.py:641
  150.6 6.6 %copy-start.21 = (bf16[176,2048]{1,0:T(8,128)(2,1)S(1)}, bf16[176,2048]{1,0:T(8,128)(2,1)}, u32[]{:S(2)}) copy-start(bf16[176,2048]{1,0:T(8,128)(2,1)} %copy-done.20) | copy-start | bytes 2162692
  150.6 6.6 %copy-start.23 = (bf16[176,2048]{1,0:T(8,128)(2,1)S(1)}, bf16[176,2048]{1,0:T(8,128)(2,1)}, u32[]{:S(2)}) copy-start(bf16[176,2048]{1,0:T(8,128)(2,1)} %copy-done.22) | copy-start | bytes 2162692
  156.6 24.6 %collective-permute-start.16 = (bf16[528,512]{1,0:T(8,128)(2,1)S(1)}, bf16[528,512]{1,0:T(8,128)(2,1)S(1)}, u32[]{:S(2)}, u32[]{:S(2)}) collective-permute-start(bf16[528,512]{1,0:T(8,128)(2,1)S(1)} %get-tuple-element.37), channel_id=1, source_target_pairs={{0,6},{2,4},{4,2},{6,0},{1,7},{3,5},{5,3},{7,1},{8,14},{10,12},{12... | collective-permute-start | bytes 1622024 | tf_op jit(solution)/shard_map/ppermute | solution.py:641
  157.1 37.3 %collective-permute-start.28 = (bf16[1536,512]{1,0:T(8,128)(2,1)S(1)}, bf16[1536,512]{1,0:T(8,128)(2,1)S(1)}, u32[]{:S(2)}, u32[]{:S(2)}) collective-permute-start(bf16[1536,512]{1,0:T(8,128)(2,1)S(1)} %assemble.16), channel_id=1, source_target_pairs={{0,1},{1,0},{2,3},{3,2},{4,5},{5,4},{6,7},{7,6},{8,9},{9,8},{10,11... | collective-permute-start | bytes 4718600 | tf_op jit(solution)/shard_map/ppermute | solution.py:108
  181.9 2.7 %collective-permute-start.26 = (bf16[1024,512]{1,0:T(8,128)(2,1)S(1)}, bf16[1024,512]{1,0:T(8,128)(2,1)S(1)}, u32[]{:S(2)}, u32[]{:S(2)}) collective-permute-start(bf16[1024,512]{1,0:T(8,128)(2,1)S(1)} %assemble.15), channel_id=1, source_target_pairs={{0,1},{1,0},{2,3},{3,2},{4,5},{5,4},{6,7},{7,6},{8,9},{9,8},{10,11... | collective-permute-start | bytes 3145736 | tf_op jit(solution)/shard_map/ppermute | solution.py:108
  182.1 12.3 %collective-permute-start.29 = (bf16[512,512]{1,0:T(8,128)(2,1)S(1)}, bf16[512,512]{1,0:T(8,128)(2,1)S(1)}, u32[]{:S(2)}, u32[]{:S(2)}) collective-permute-start(bf16[512,512]{1,0:T(8,128)(2,1)S(1)} %assemble.17), channel_id=1, source_target_pairs={{0,1},{1,0},{2,3},{3,2},{4,5},{5,4},{6,7},{7,6},{8,9},{9,8},{10,11... | collective-permute-start | bytes 1572872 | tf_op jit(solution)/shard_map/ppermute | solution.py:108
  194.2 1.6 collective-permute-start.27
  197.7 10.4 %collective-permute-start.30 = (bf16[64,2048]{1,0:T(8,128)(2,1)S(1)}, bf16[64,2048]{1,0:T(8,128)(2,1)S(1)}, u32[]{:S(2)}, u32[]{:S(2)}) collective-permute-start(bf16[64,2048]{1,0:T(8,128)(2,1)S(1)} %get-tuple-element.46), channel_id=1, source_target_pairs={{0,2},{2,0},{4,6},{6,4},{1,3},{3,1},{5,7},{7,5},{8,10},{10,8},{12,... | collective-permute-start | bytes 786440 | tf_op jit(solution)/shard_map/ppermute | solution.py:672
  197.8 19.7 %collective-permute-start.31 = (bf16[64,2048]{1,0:T(8,128)(2,1)S(1)}, bf16[64,2048]{1,0:T(8,128)(2,1)S(1)}, u32[]{:S(2)}, u32[]{:S(2)}) collective-permute-start(bf16[64,2048]{1,0:T(8,128)(2,1)S(1)} %get-tuple-element.47), channel_id=1, source_target_pairs={{0,4},{2,6},{4,0},{6,2},{1,5},{3,7},{5,1},{7,3},{8,12},{10,14},{12... | collective-permute-start | bytes 786440 | tf_op jit(solution)/shard_map/ppermute | solution.py:672
  199.5 24.7 %collective-permute-start.32 = (bf16[64,2048]{1,0:T(8,128)(2,1)S(1)}, bf16[64,2048]{1,0:T(8,128)(2,1)S(1)}, u32[]{:S(2)}, u32[]{:S(2)}) collective-permute-start(bf16[64,2048]{1,0:T(8,128)(2,1)S(1)} %get-tuple-element.48), channel_id=1, source_target_pairs={{0,6},{2,4},{4,2},{6,0},{1,7},{3,5},{5,3},{7,1},{8,14},{10,12},{12... | collective-permute-start | bytes 786440 | tf_op jit(solution)/shard_map/ppermute | solution.py:672
  (16 other events, 48.8 us)

commit v4 on v2

--- a/solution.py
+++ b/solution.py
@@ -58,7 +58,8 @@
     return pl.pallas_call(
         functools.partial(cut_kernel, start),
         out_shape=jax.ShapeDtypeStruct((size, x.shape[1]), BF16),
-        in_specs=[pl.BlockSpec(memory_space=pl.ANY)] * (1 + len(earlier)),
+        in_specs=[pl.BlockSpec(memory_space=pltpu.MemorySpace.HBM)]
+        + [pl.BlockSpec(memory_space=pl.ANY)] * len(earlier),
         out_specs=pl.BlockSpec(memory_space=pltpu.VMEM),
         scratch_shapes=[pltpu.SemaphoreType.DMA(())],
         compiler_params=params(8),
@@ -165,7 +166,7 @@
         functools.partial(norm_kernel, down_rows),
         out_shape=(jax.ShapeDtypeStruct((rows, width), BF16), MARK),
         in_specs=[pl.BlockSpec(memory_space=SMEM)]
-        + [pl.BlockSpec(memory_space=pl.ANY)] * len(arrays),
+        + [pl.BlockSpec(memory_space=pltpu.MemorySpace.HBM)] * len(arrays),
         out_specs=(pl.BlockSpec(memory_space=pltpu.VMEM), pl.BlockSpec(memory_space=SMEM)),
         scratch_shapes=[pltpu.VMEM(x.shape, x.dtype) for x in arrays]
         + [pltpu.SemaphoreType.DMA((len(arrays),))],
@@ -212,7 +213,7 @@
     )(*blocks, earlier)
 
 
-def project_kernel(plan, at, *refs):
+def project_kernel(plan, stage, at, *refs):
     slots, count, inputs, down_rows = plan
     arrays, outs = refs[:count], refs[count : count + len(inputs)]
     mark, joined, down = refs[count + len(inputs) :]
@@ -224,6 +225,18 @@
     def part(begin, size):
         return pl.ds(pl.multiple_of(begin, size), size)
 
+    if stage == 2:
+        half = joined.shape[1]
+        columns = part(((dp ^ 3) & 1) * half, half)
+        for k, (mine, other) in enumerate(slots):
+            joined[part((seq ^ k) * rows, rows), :] = jnp.where(
+                (dp ^ 3) >> 1 == core, arrays[mine][:rows, columns], arrays[other][:rows, columns]
+            )
+        for (index, begun), out in zip(inputs, outs):
+            total = arrays[begun][...]
+            total += jnp.dot(joined[...], arrays[index][...], preferred_element_type=F32)
+            out[...] = total.astype(out.dtype)
+        return
     for k, (mine, other) in enumerate(slots):
         at_row = part((seq ^ k) * rows, rows)
         joined[at_row, part(core * width, width)] = arrays[mine][:rows, :]
@@ -260,10 +273,10 @@
         for index, row, size, k, start, shard in weights:
             columns = joined[...] if k is None else joined[:, part((dp ^ k) * shard + start, size)]
             total += jnp.dot(columns, arrays[index][row : row + size, :], preferred_element_type=F32)
-        out[...] = total.astype(BF16)
-
-
-def project(at, slots, rows, inputs, down_rows):
+        out[...] = total.astype(out.dtype)
+
+
+def project(at, slots, rows, inputs, down_rows, stage=0):
     arrays = []
 
     def place(array):
@@ -284,10 +297,10 @@
         plans.append((weights, downs, place(up)))
     width = 2 * slots[0][0].shape[1]
     columns = inputs[0][2].shape[1]
-    result = jax.ShapeDtypeStruct((rows, columns), BF16)
+    result = jax.ShapeDtypeStruct((rows, columns), F32 if stage == 1 else BF16)
     ranks = len(inputs) * HD
     return pl.pallas_call(
-        functools.partial(project_kernel, (placed, len(arrays), tuple(plans), down_rows)),
+        functools.partial(project_kernel, (placed, len(arrays), tuple(plans), down_rows), stage),
         out_shape=(*(result,) * len(inputs), MARK),
         in_specs=[pl.BlockSpec(memory_space=SMEM)]
         + [pl.BlockSpec(memory_space=pltpu.VMEM)] * len(arrays),
@@ -304,6 +317,33 @@
             2 * rows * width * (columns + HD) * len(inputs), 2 * width * (rows + columns * len(inputs))
         ),
         name="project",
+    )(at, *arrays)
+
+
+def project_rest(at, slots, rows, last, begun, *earlier):
+    arrays = [x for slot in slots for x in slot] + [*last, *begun, *earlier]
+    count = len(arrays) - len(earlier)
+    placed = tuple((2 * k, 2 * k + 1) for k in range(len(slots)))
+    first = 2 * len(slots)
+    plans = tuple((first + n, first + len(last) + n) for n in range(len(last)))
+    result = jax.ShapeDtypeStruct(begun[0].shape, BF16)
+    return pl.pallas_call(
+        functools.partial(project_kernel, (placed, len(arrays), plans, None), 2),
+        out_shape=(*(result,) * len(last), MARK),
+        in_specs=[pl.BlockSpec(memory_space=SMEM)]
+        + [pl.BlockSpec(memory_space=pltpu.VMEM)] * count
+        + [pl.BlockSpec(memory_space=pl.ANY)] * len(earlier),
+        out_specs=(
+            *(pl.BlockSpec(memory_space=pltpu.VMEM),) * len(last),
+            pl.BlockSpec(memory_space=SMEM),
+        ),
+        scratch_shapes=[
+            pltpu.VMEM((rows, last[0].shape[0]), BF16),
+            pltpu.VMEM((8, HD), BF16),
+        ],
+        compiler_params=params(24),
+        cost_estimate=cost(1, 1),
+        name="project_rest",
     )(at, *arrays)
 
 
@@ -473,7 +513,7 @@
     width = total.shape[1] // groups
     for k in range(groups):
         if k < 3:
-            here = jnp.dot(keep_ref[...], mine[k][...], preferred_element_type=F32)
+            here = jnp.dot(keep_ref[...], mine[k][:depth, :], preferred_element_type=F32)
             there = other[0][k * depth : (k + 1) * depth, :]
         else:
             half = depth // 2
@@ -543,17 +583,16 @@
     return query, mark, [top, bottom]
 
 
-def key_value_4(at, blocks, rows, weights, near, last, downs, ups, down_rows, *late):
+def begin_4(at, blocks, rows, weights, near, downs, ups, down_rows):
     shard = weights.shape[0] // 2
-    other = other_core(assemble([(x, row, 2 * HD) for x, row in downs], *late))
+    other = other_core(assemble([(x, row, 2 * HD) for x, row in downs]))
     inputs = []
     for n in range(2):
         pieces = [(x, n * shard, shard, k, 0, shard) for k, x in enumerate((weights, *near))]
-        pieces.append((last[n], 0, shard, 3, 0, shard))
         small = [(x, row + n * HD, k, 0) for k, (x, row) in enumerate(downs)]
         small += [(other, (2 * k + n) * HD, k, 1) for k in range(4)]
         inputs.append((pieces, small, ups[n]))
-    return project(at, blocks, rows, inputs, down_rows)
+    return project(at, blocks, rows, inputs, down_rows, 1)[:2]
 
 
 def shards(
@@ -631,18 +670,21 @@
         weights = cut(own_weights, shard, 2 * shard, mine[3], *exchanged, *arrived)
         near = both_ways(weights)
         far = lax.ppermute(down, "dp", swap(4, 3))
-        output_own = cut(output_weights[0], 0, output_weights.shape[1], *near, far, marks[3])
+        depth = output_weights.shape[1]
+        output_own = assemble(
+            [(output_weights[0], 0, depth), (down, 0, 2 * HD)], *near, far, marks[3]
+        )
         by_x, by_y = both_ways(output_own)
-        last = halves_on(*near, down, by_x, by_y, queries[3])
-        top, bottom = halves_on(by_x, by_y, None, *last)
-        downs = [(down, 0), (last[1], shard), (last[0], shard), (far, 0)]
-        key, value, _ = key_value_4(
-            at, blocks, rows, weights, near, last, downs, ups[1:], down_rows, *list(sent.values())[1:]
-        )
+        downs = [(down, 0), (by_x, depth), (by_y, depth), (far, 0)]
+        begun = begin_4(at, blocks, rows, weights, near, downs, ups[1:], down_rows)
+        top = along_y(assemble([(by_x, 0, depth // 2)]))
+        bottom = along_x(assemble([(by_y, depth // 2, depth // 2)]))
+        last = halves_on(*near, None, queries[3], sent[2], top, bottom)
+        key, value, _ = project_rest(at, blocks, rows, last, begun, sent[1], sent[3])
         out_mine = [output_own, by_x, by_y, top, bottom]
         out_other = [
-            other_core(assemble([(x, 0, x.shape[0]) for x in part]))
-            for part in (out_mine[:3], out_mine[3:])
+            other_core(assemble([(x, 0, size) for x in part]))
+            for part, size in ((out_mine[:3], depth), (out_mine[3:], depth // 2))
         ]
     else:
         out_mine = [lax.all_gather(output_weights[0], "dp", axis=1, tiled=True)]

time: 240 us -> 215 us (0.90)
  waiting for transfers between devices: 137 us -> 110 us
    ppermute x3, waiting for transfers between devices: 38 us -> 14.9 us  [shards(): lax.ppermute(parts[k], 'seq', swap(seq_count, k))]
    ppermute x6, waiting for transfers between devices: 8.3 us -> 0.32 us  [along_y(): return lax.ppermute(x, 'dp', swap(4, 2))]
    ppermute x1, waiting for transfers between devices: 1.83 us -> 7.96 us  [shards(): far = lax.ppermute(down, 'dp', swap(4, 3))]
    ppermute x6, waiting for transfers between devices: 51.7 us -> 46.4 us  [spread(): blocks[k] = lax.ppermute(blocks[k ^ step], 'seq', swap(count, step))]
    ppermute x6, waiting for transfers between devices: 10.6 us -> 14.2 us  [along_x(): return lax.ppermute(x, 'dp', swap(4, 1))]
    unnamed x60 -> x64, local copies, waits for them, and re-layouts: 7.6 us -> 8.82 us
  transfers between devices with their start and end apart: 33 -> 33, of which waited for: 18 -> 13; matrix products, arithmetic and copies ran while one was open for 0% -> 0% of each run, Pallas kernels for 21% -> 23%
where the time goes in v4:
time: 215 us; the launch traced here: 214 us
  waiting for transfers between devices  110 us (51%)
  Pallas kernels  58.3 us (27%)
  starting transfers between devices  34.1 us (16%)
  local copies, waits for them, and re-layouts  9.52 us (4%)
    ppermute x6, waiting for transfers between devices, spread(): blocks[k] = lax.ppermute(blocks[k ^ step], 'seq', swap(count, step))  46.4 us
    pallas_call x4, Pallas kernels, cache_attention(): pl.pallas_call(functools.partial(cache_kernel, slot, heads), out_shape=(j...  24.4 us
    ppermute x3, waiting for transfers between devices, shards(): lax.ppermute(sums[k], 'seq', swap(seq_count, k))  22.9 us
    ppermute x3, waiting for transfers between devices, shards(): lax.ppermute(parts[k], 'seq', swap(seq_count, k))  14.9 us
    pallas_call x2, Pallas kernels, project(): pl.pallas_call(functools.partial(project_kernel, (placed, len(arrays), tu...  14.7 us
    ppermute x6, waiting for transfers between devices, along_x(): return lax.ppermute(x, 'dp', swap(4, 1))  14.2 us
    ppermute x6, starting transfers between devices, spread(): blocks[k] = lax.ppermute(blocks[k ^ step], 'seq', swap(count, step))  9.61 us
    unnamed x64, local copies, waits for them, and re-layouts  8.82 us
  transfers between devices with their start and end apart: 33, of which 13 were waited for; matrix products, arithmetic and copies ran while one was open for 0% of the time, Pallas kernels for 23%

profile of v4, /device:TPU:16, one launch (start us, length us, event | category | flops | bytes accessed | tf_op | source)
XLA Modules:
  0.0 214.2 jit_solution(10456555110476758157)
XLA Ops:
  1.9 3.4 %norm.1 = (bf16[176,2048]{1,0:T(8,128)(2,1)}, s32[1]{0:T(128)}) custom-call(s32[5]{0:T(128)} %stack.15.at, bf16[128,2048]{1,0:T(8,128)(2,1)} %refs_0_.1, bf16[128,2048]{1,0:T(8,128)(2,1)} %refs_1_.1, f32[1,4096]{1,0:T(1,128)} %bitcast.24, bf16[512,384]{1,0:T(8,128)(2,1)} %refs_3_.1), custom_call_target="tpu_custom_call" | custom-call | flops 1 | bytes 1 | tf_op jit(solution)/shard_map/norm/pallas_call | solution.py:165
  5.3 1.9 copy-done.12
  7.2 0.8 cut.2.refs_8_
  8.0 1.6 collective-permute-start.8
  9.6 1.5 collective-permute-start.7
  11.4 1.6 collective-permute-start.1
  13.0 28.8 %collective-permute-done.3.refs_1_.refs_4_.refs_2_ = bf16[176,2048]{1,0:T(8,128)(2,1)S(1)} collective-permute-done((bf16[176,2048]{1,0:T(8,128)(2,1)S(1)}, bf16[176,2048]{1,0:T(8,128)(2,1)S(1)}, u32[]{:S(2)}, u32[]{:S(2)}) %collective-permute-start.3) | collective-permute-done | bytes 720928 | tf_op jit(solution)/shard_map/ppermute | solution.py:84
  41.8 4.5 %collective-permute-start.5 = (bf16[176,2048]{1,0:T(8,128)(2,1)S(1)}, bf16[176,2048]{1,0:T(8,128)(2,1)S(1)}, u32[]{:S(2)}, u32[]{:S(2)}) collective-permute-start(bf16[176,2048]{1,0:T(8,128)(2,1)S(1)} %collective-permute-done.3.refs_1_.refs_4_.refs_2_), channel_id=1, source_target_pairs={{0,2},{2,0},{4,6},{6,4},{1,3},{3,1},{5,7},{7,5},{8,10},{10,8},{12,... | collective-permute-start | bytes 2162696 | tf_op jit(solution)/shard_map/ppermute | solution.py:84
  48.1 14.5 %collective-permute-done.5.refs_6_.refs_1_.refs_3_ = bf16[176,2048]{1,0:T(8,128)(2,1)S(1)} collective-permute-done((bf16[176,2048]{1,0:T(8,128)(2,1)S(1)}, bf16[176,2048]{1,0:T(8,128)(2,1)S(1)}, u32[]{:S(2)}, u32[]{:S(2)}) %collective-permute-start.5) | collective-permute-done | bytes 720928 | tf_op jit(solution)/shard_map/ppermute | solution.py:84
  62.6 1.7 cut.3.refs_8_
  65.4 2.2 %collective-permute-done.6.refs_7_ = bf16[176,2048]{1,0:T(8,128)(2,1)S(1)} collective-permute-done((bf16[176,2048]{1,0:T(8,128)(2,1)S(1)}, bf16[176,2048]{1,0:T(8,128)(2,1)S(1)}, u32[]{:S(2)}, u32[]{:S(2)}) %collective-permute-start.6) | collective-permute-done | bytes 720928 | tf_op jit(solution)/shard_map/ppermute | solution.py:109
  67.6 6.6 %project.2 = (bf16[512,512]{1,0:T(8,128)(2,1)S(1)}, s32[1]{0:T(128)}) custom-call(s32[5]{0:T(128)S(1)} %copy-done.28, bf16[176,2048]{1,0:T(8,128)(2,1)S(1)} %copy-done.14, bf16[176,2048]{1,0:T(8,128)(2,1)S(1)} %collective-permute-done.refs_1_.refs_2_, bf16[176,2048]{1,0:T(8,128)(2,1)S(1)} %collective-permute-done.1.refs_2_.refs_1_, ...), custom_call_target="tpu_custom_call" | custom-call | flops 1 | bytes 1 | tf_op jit(solution)/shard_map/project/pallas_call | solution.py:302
  74.2 1.8 collective-permute-start.11
  76.0 2.3 %arrange.1.refs_1_.refs_0_.refs_11_ = bf16[256,512]{1,0:T(8,128)(2,1)} custom-call(bf16[176,2048]{1,0:T(8,128)(2,1)} %get-tuple-element.26.refs_0_, bf16[176,2048]{1,0:T(8,128)(2,1)} %copy-done.16, bf16[176,2048]{1,0:T(8,128)(2,1)} %copy-done.4, bf16[176,2048]{1,0:T(8,128)(2,1)} %copy-done.6, s32[1]{0:T(128)} %get-tuple-element.28.earlier.refs_4_), custom_call_target="tpu_custom_call" | custom-call | flops 1 | bytes 1 | tf_op jit(solution)/shard_map/arrange/pallas_call | solution.py:202
  78.4 2.5 %collective-permute-start.19 = (bf16[256,512]{1,0:T(8,128)(2,1)}, bf16[256,512]{1,0:T(8,128)(2,1)S(1)}, u32[]{:S(2)}, u32[]{:S(2)}) collective-permute-start(bf16[256,512]{1,0:T(8,128)(2,1)} %arrange.1.refs_1_.refs_0_.refs_11_), channel_id=1, source_target_pairs={{0,24},{8,16},{16,8},{24,0},{1,25},{9,17},{17,9},{25,1},{2,26},{10... | collective-permute-start | bytes 786440 | tf_op jit(solution)/shard_map/ppermute | solution.py:672
  80.9 2.2 %copy-done = bf16[1,1024,2048]{2,1,0:T(8,128)(2,1)S(1)} copy-done((bf16[1,1024,2048]{2,1,0:T(8,128)(2,1)S(1)}, bf16[1,1024,2048]{2,1,0:T(8,128)(2,1)}, u32[]{:S(2)}) %copy-start) | copy-done | bytes 4194328
  83.1 2.2 %copy-done.2 = bf16[1,1024,2048]{2,1,0:T(8,128)(2,1)S(1)} copy-done((bf16[1,1024,2048]{2,1,0:T(8,128)(2,1)S(1)}, bf16[1,1024,2048]{2,1,0:T(8,128)(2,1)}, u32[]{:S(2)}) %copy-start.2) | copy-done | bytes 4194328
  85.3 1.2 copy-done.8
  86.5 1.2 copy-done.10
  87.7 5.9 %cache_attention.4 = (bf16[528,512]{1,0:T(8,128)(2,1)S(1)}, s32[1]{0:T(128)}) custom-call(s32[5]{0:T(128)S(1)} %copy-done.28, s32[1]{0:T(128)} %get-tuple-element.28.earlier.refs_4_, s32[16]{0:T(128)S(1)} %bitcast.20, bf16[512,512]{1,0:T(8,128)(2,1)S(1)} %get-tuple-element.29.query_ref, bf16[1,1024,2048]{2,1,0:T(8,128)(2,1)S(1)} %copy-done, ...), custom_call_target="tpu_custom_call" | custom-call | flops 1 | bytes 1 | tf_op jit(solution)/shard_map/cache_attention/pallas_call | solution.py:417
  93.7 3.2 %collective-permute-done.11.query_ref = bf16[512,512]{1,0:T(8,128)(2,1)} collective-permute-done((bf16[512,512]{1,0:T(8,128)(2,1)S(1)}, bf16[512,512]{1,0:T(8,128)(2,1)}, u32[]{:S(2)}, u32[]{:S(2)}) %collective-permute-start.11) | collective-permute-done | bytes 524320 | tf_op jit(solution)/shard_map/ppermute | solution.py:84
  96.8 6.6 %cache_attention.5 = (bf16[528,512]{1,0:T(8,128)(2,1)S(1)}, s32[1]{0:T(128)}) custom-call(s32[5]{0:T(128)S(1)} %copy-done.28, s32[1]{0:T(128)} %get-tuple-element.31.earlier, s32[16]{0:T(128)S(1)} %bitcast.21, bf16[512,512]{1,0:T(8,128)(2,1)} %collective-permute-done.11.query_ref, bf16[1,1024,2048]{2,1,0:T(8,128)(2,1)S(1)} %copy-done.1, ...), custom_call_target="tpu_custom_call" | custom-call | flops 1 | bytes 1 | tf_op jit(solution)/shard_map/cache_attention/pallas_call | solution.py:417
  103.5 5.8 %cache_attention.6 = (bf16[528,512]{1,0:T(8,128)(2,1)S(1)}, s32[1]{0:T(128)}) custom-call(s32[5]{0:T(128)S(1)} %copy-done.28, s32[1]{0:T(128)} %get-tuple-element.33.earlier, s32[16]{0:T(128)S(1)} %bitcast.22, bf16[512,512]{1,0:T(8,128)(2,1)S(1)} %collective-permute-done.13.query_ref, bf16[1,1024,2048]{2,1,0:T(8,128)(2,1)S(1)} %copy-done.1, ...), custom_call_target="tpu_custom_call" | custom-call | flops 1 | bytes 1 | tf_op jit(solution)/shard_map/cache_attention/pallas_call | solution.py:417
  109.3 8.0 %collective-permute-done.19.refs_4_.refs_3_.refs_14_ = bf16[256,512]{1,0:T(8,128)(2,1)S(1)} collective-permute-done((bf16[256,512]{1,0:T(8,128)(2,1)}, bf16[256,512]{1,0:T(8,128)(2,1)S(1)}, u32[]{:S(2)}, u32[]{:S(2)}) %collective-permute-start.19) | collective-permute-done | bytes 262176 | tf_op jit(solution)/shard_map/ppermute | solution.py:672
  118.2 1.6 collective-permute-start.20
  120.3 1.4 collective-permute-start.15
  121.7 14.2 %collective-permute-done.20.refs_0_.refs_1_.refs_12_ = bf16[768,512]{1,0:T(8,128)(2,1)S(1)} collective-permute-done((bf16[768,512]{1,0:T(8,128)(2,1)S(1)}, bf16[768,512]{1,0:T(8,128)(2,1)S(1)}, u32[]{:S(2)}, u32[]{:S(2)}) %collective-permute-start.20) | collective-permute-done | bytes 786464 | tf_op jit(solution)/shard_map/ppermute | solution.py:89
  135.9 1.5 collective-permute-start.21
  137.5 1.6 collective-permute-start.23
  139.9 2.2 %collective-permute-done.14.refs_2_ = bf16[528,512]{1,0:T(8,128)(2,1)S(1)} collective-permute-done((bf16[528,512]{1,0:T(8,128)(2,1)S(1)}, bf16[528,512]{1,0:T(8,128)(2,1)S(1)}, u32[]{:S(2)}, u32[]{:S(2)}) %collective-permute-start.14) | collective-permute-done | bytes 540704 | tf_op jit(solution)/shard_map/ppermute | solution.py:664
  142.1 4.4 %collective-permute-start.12 = (bf16[528,512]{1,0:T(8,128)(2,1)S(1)}, bf16[528,512]{1,0:T(8,128)(2,1)S(1)}, u32[]{:S(2)}, u32[]{:S(2)}) collective-permute-start(bf16[528,512]{1,0:T(8,128)(2,1)S(1)} %get-tuple-element.32), channel_id=1, source_target_pairs={{0,2},{2,0},{4,6},{6,4},{1,3},{3,1},{5,7},{7,5},{8,10},{10,8},{12,... | collective-permute-start | bytes 1622024 | tf_op jit(solution)/shard_map/ppermute | solution.py:664
  146.5 1.7 assemble.16
  148.2 1.5 collective-permute-start.25
  149.9 0.6 collective-permute-start.24
  150.5 6.1 %cache_attention.7 = (bf16[528,512]{1,0:T(8,128)(2,1)S(1)}, s32[1]{0:T(128)}) custom-call(s32[5]{0:T(128)S(1)} %copy-done.28, s32[1]{0:T(128)} %get-tuple-element.35.earlier.refs_5_, s32[16]{0:T(128)S(1)} %bitcast.23, bf16[512,512]{1,0:T(8,128)(2,1)S(1)} %collective-permute-done.15.query_ref.refs_1_, bf16[1,1024,2048]{2,1,0:T(8,128)(2,1)S(1)} %copy-done.1, ...), custom_call_target="tpu_custom_call" | custom-call | flops 1 | bytes 1 | tf_op jit(solution)/shard_map/cache_attention/pallas_call | solution.py:417
  156.9 8.1 %project.3 = (f32[512,512]{1,0:T(8,128)S(1)}, f32[512,512]{1,0:T(8,128)S(1)}, s32[1]{0:T(128)}) custom-call(s32[5]{0:T(128)S(1)} %copy-done.28, bf16[176,2048]{1,0:T(8,128)(2,1)S(1)} %copy-done.15, bf16[176,2048]{1,0:T(8,128)(2,1)S(1)} %copy-done.19, bf16[176,2048]{1,0:T(8,128)(2,1)S(1)} %copy-done.17, bf16[176,2048]{1,0:T(8,128)(2,1)S(1)} %copy-done.23, ...), custom_call_target="tpu_custom_call" | custom-call | flops 1 | bytes 1 | tf_op jit(solution)/shard_map/project/pallas_call | solution.py:302
  165.0 12.7 %collective-permute-done.16.refs_13_.refs_3_ = bf16[528,512]{1,0:T(8,128)(2,1)S(1)} collective-permute-done((bf16[528,512]{1,0:T(8,128)(2,1)S(1)}, bf16[528,512]{1,0:T(8,128)(2,1)S(1)}, u32[]{:S(2)}, u32[]{:S(2)}) %collective-permute-start.16) | collective-permute-done | bytes 540704 | tf_op jit(solution)/shard_map/ppermute | solution.py:664
  177.7 1.9 project_rest.1
  179.6 1.8 new_attention.1.refs_4_
  181.4 1.3 merge.1
  182.8 1.5 collective-permute-done.27.got_ref
  184.3 1.9 output_projection.1
  186.3 2.0 collective-permute-start.31
  188.3 1.5 collective-permute-start.32
  189.8 7.1 %collective-permute-done.30.refs_1_ = bf16[64,2048]{1,0:T(8,128)(2,1)S(1)} collective-permute-done((bf16[64,2048]{1,0:T(8,128)(2,1)S(1)}, bf16[64,2048]{1,0:T(8,128)(2,1)S(1)}, u32[]{:S(2)}, u32[]{:S(2)}) %collective-permute-start.30) | collective-permute-done | bytes 262176 | tf_op jit(solution)/shard_map/ppermute | solution.py:697
  196.9 9.3 %collective-permute-done.31.refs_2_ = bf16[64,2048]{1,0:T(8,128)(2,1)S(1)} collective-permute-done((bf16[64,2048]{1,0:T(8,128)(2,1)S(1)}, bf16[64,2048]{1,0:T(8,128)(2,1)S(1)}, u32[]{:S(2)}, u32[]{:S(2)}) %collective-permute-start.31) | collective-permute-done | bytes 262176 | tf_op jit(solution)/shard_map/ppermute | solution.py:697
  206.3 6.5 %collective-permute-done.32.refs_3_ = bf16[64,2048]{1,0:T(8,128)(2,1)S(1)} collective-permute-done((bf16[64,2048]{1,0:T(8,128)(2,1)S(1)}, bf16[64,2048]{1,0:T(8,128)(2,1)S(1)}, u32[]{:S(2)}, u32[]{:S(2)}) %collective-permute-start.32) | collective-permute-done | bytes 262176 | tf_op jit(solution)/shard_map/ppermute | solution.py:697
  212.8 1.4 final_sum.1
  (111 shorter events, 6.7 us)
Async XLA Ops:
  8.0 38.2 %collective-permute-start.8 = (bf16[1024,512]{1,0:T(8,128)(2,1)S(1)}, bf16[1024,512]{1,0:T(8,128)(2,1)S(1)}, u32[]{:S(2)}, u32[]{:S(2)}) collective-permute-start(bf16[1024,512]{1,0:T(8,128)(2,1)S(1)} %cut.2.refs_8_), channel_id=1, source_target_pairs={{0,16},{8,24},{16,0},{24,8},{1,17},{9,25},{17,1},{25,9},{2,18},{10... | collective-permute-start | bytes 3145736 | tf_op jit(solution)/shard_map/ppermute | solution.py:93
  9.6 37.2 %collective-permute-start.7 = (bf16[1024,512]{1,0:T(8,128)(2,1)S(1)}, bf16[1024,512]{1,0:T(8,128)(2,1)S(1)}, u32[]{:S(2)}, u32[]{:S(2)}) collective-permute-start(bf16[1024,512]{1,0:T(8,128)(2,1)S(1)} %cut.2.refs_8_), channel_id=1, source_target_pairs={{0,8},{8,0},{16,24},{24,16},{1,9},{9,1},{17,25},{25,17},{2,10},{10... | collective-permute-start | bytes 3145736 | tf_op jit(solution)/shard_map/ppermute | solution.py:89
  11.1 51.5 %copy-start.13 = (bf16[1024,3,1,512]{3,0,2,1:T(8,128)(2,1)S(1)}, bf16[1024,3,1,512]{3,0,2,1:T(8,128)(2,1)}, u32[]{:S(2)}) copy-start(bf16[1024,3,1,512]{3,0,2,1:T(8,128)(2,1)} %param.18) | copy-start | bytes 9437188
  11.1 30.7 %collective-permute-start.3 = (bf16[176,2048]{1,0:T(8,128)(2,1)S(1)}, bf16[176,2048]{1,0:T(8,128)(2,1)S(1)}, u32[]{:S(2)}, u32[]{:S(2)}) collective-permute-start(bf16[176,2048]{1,0:T(8,128)(2,1)S(1)} %copy-done.14), channel_id=1, source_target_pairs={{0,4},{2,6},{4,0},{6,2},{1,5},{3,7},{5,1},{7,3},{8,12},{10,14},{12... | collective-permute-start | bytes 2162696 | tf_op jit(solution)/shard_map/ppermute | solution.py:84
  11.4 34.8 %collective-permute-start.1 = (bf16[176,2048]{1,0:T(8,128)(2,1)S(1)}, bf16[176,2048]{1,0:T(8,128)(2,1)S(1)}, u32[]{:S(2)}, u32[]{:S(2)}) collective-permute-start(bf16[176,2048]{1,0:T(8,128)(2,1)S(1)} %copy-done.14), channel_id=1, source_target_pairs={{0,2},{2,0},{4,6},{6,4},{1,3},{3,1},{5,7},{7,5},{8,10},{10,8},{12,... | collective-permute-start | bytes 2162696 | tf_op jit(solution)/shard_map/ppermute | solution.py:84
  13.0 34.5 %collective-permute-start = (bf16[176,2048]{1,0:T(8,128)(2,1)S(1)}, bf16[176,2048]{1,0:T(8,128)(2,1)S(1)}, u32[]{:S(2)}, u32[]{:S(2)}) collective-permute-start(bf16[176,2048]{1,0:T(8,128)(2,1)S(1)} %copy-done.14), channel_id=1, source_target_pairs={{0,1},{1,0},{2,3},{3,2},{4,5},{5,4},{6,7},{7,6},{8,9},{9,8},{10,11... | collective-permute-start | bytes 2162696 | tf_op jit(solution)/shard_map/ppermute | solution.py:109
  41.8 25.8 %copy-start.4 = (bf16[176,2048]{1,0:T(8,128)(2,1)}, bf16[176,2048]{1,0:T(8,128)(2,1)S(1)}, u32[]{:S(2)}) copy-start(bf16[176,2048]{1,0:T(8,128)(2,1)S(1)} %collective-permute-done.3.refs_1_.refs_4_.refs_2_) | copy-start | bytes 2162692
  41.8 20.8 %collective-permute-start.5 = (bf16[176,2048]{1,0:T(8,128)(2,1)S(1)}, bf16[176,2048]{1,0:T(8,128)(2,1)S(1)}, u32[]{:S(2)}, u32[]{:S(2)}) collective-permute-start(bf16[176,2048]{1,0:T(8,128)(2,1)S(1)} %collective-permute-done.3.refs_1_.refs_4_.refs_2_), channel_id=1, source_target_pairs={{0,2},{2,0},{4,6},{6,4},{1,3},{3,1},{5,7},{7,5},{8,10},{10,8},{12,... | collective-permute-start | bytes 2162696 | tf_op jit(solution)/shard_map/ppermute | solution.py:84
  46.2 21.4 %copy-start.16 = (bf16[176,2048]{1,0:T(8,128)(2,1)}, bf16[176,2048]{1,0:T(8,128)(2,1)S(1)}, u32[]{:S(2)}) copy-start(bf16[176,2048]{1,0:T(8,128)(2,1)S(1)} %collective-permute-done.1.refs_2_.refs_1_) | copy-start | bytes 2162692
  46.2 16.3 %collective-permute-start.4 = (bf16[176,2048]{1,0:T(8,128)(2,1)S(1)}, bf16[176,2048]{1,0:T(8,128)(2,1)S(1)}, u32[]{:S(2)}, u32[]{:S(2)}) collective-permute-start(bf16[176,2048]{1,0:T(8,128)(2,1)S(1)} %collective-permute-done.3.refs_1_.refs_4_.refs_2_), channel_id=1, source_target_pairs={{0,1},{1,0},{2,3},{3,2},{4,5},{5,4},{6,7},{7,6},{8,9},{9,8},{10,11... | collective-permute-start | bytes 2162696 | tf_op jit(solution)/shard_map/ppermute | solution.py:109
  46.3 16.3 %collective-permute-start.2 = (bf16[176,2048]{1,0:T(8,128)(2,1)S(1)}, bf16[176,2048]{1,0:T(8,128)(2,1)S(1)}, u32[]{:S(2)}, u32[]{:S(2)}) collective-permute-start(bf16[176,2048]{1,0:T(8,128)(2,1)S(1)} %collective-permute-done.1.refs_2_.refs_1_), channel_id=1, source_target_pairs={{0,1},{1,0},{2,3},{3,2},{4,5},{5,4},{6,7},{7,6},{8,9},{9,8},{10,11... | collective-permute-start | bytes 2162696 | tf_op jit(solution)/shard_map/ppermute | solution.py:109
  46.8 15.8 %collective-permute-start.10 = (bf16[512,512]{1,0:T(8,128)(2,1)S(1)}, bf16[512,512]{1,0:T(8,128)(2,1)S(1)}, u32[]{:S(2)}, u32[]{:S(2)}) collective-permute-start(bf16[512,512]{1,0:T(8,128)(2,1)S(1)} %assemble.11), channel_id=1, source_target_pairs={{0,8},{8,0},{16,24},{24,16},{1,9},{9,1},{17,25},{25,17},{2,10},{10... | collective-permute-start | bytes 1572872 | tf_op jit(solution)/shard_map/ppermute | solution.py:89
  47.5 18.0 %copy-start.30 = (bf16[3,128,1,512]{3,1,2,0:T(8,128)(2,1)S(1)}, bf16[3,128,1,512]{3,1,2,0:T(8,128)(2,1)}, u32[]{:S(2)}) copy-start(bf16[3,128,1,512]{3,1,2,0:T(8,128)(2,1)} %param.20) | copy-start | bytes 1179652
  47.5 20.2 %copy-start.28 = (s32[5]{0:T(128)S(1)}, s32[5]{0:T(128)}, u32[]{:S(2)}) copy-start(s32[5]{0:T(128)} %stack.15.at) | copy-start | bytes 64
  47.5 20.1 %copy-start.18 = (bf16[176,2048]{1,0:T(8,128)(2,1)}, bf16[176,2048]{1,0:T(8,128)(2,1)S(1)}, u32[]{:S(2)}) copy-start(bf16[176,2048]{1,0:T(8,128)(2,1)S(1)} %collective-permute-done.refs_1_.refs_2_) | copy-start | bytes 2162692
  47.5 15.1 %collective-permute-start.9 = (bf16[512,512]{1,0:T(8,128)(2,1)S(1)}, bf16[512,512]{1,0:T(8,128)(2,1)S(1)}, u32[]{:S(2)}, u32[]{:S(2)}) collective-permute-start(bf16[512,512]{1,0:T(8,128)(2,1)S(1)} %assemble.10), channel_id=1, source_target_pairs={{0,16},{8,24},{16,0},{24,8},{1,17},{9,25},{17,1},{25,9},{2,18},{10... | collective-permute-start | bytes 1572872 | tf_op jit(solution)/shard_map/ppermute | solution.py:93
  64.3 53.0 %collective-permute-start.17 = (bf16[2048,512]{1,0:T(8,128)(2,1)}, bf16[2048,512]{1,0:T(8,128)(2,1)S(1)}, u32[]{:S(2)}, u32[]{:S(2)}) collective-permute-start(bf16[2048,512]{1,0:T(8,128)(2,1)} %cut.3.refs_8_), channel_id=1, source_target_pairs={{0,8},{8,0},{16,24},{24,16},{1,9},{9,1},{17,25},{25,17},{2,10},{10... | collective-permute-start | bytes 6291464 | tf_op jit(solution)/shard_map/ppermute | solution.py:89
  64.9 52.7 %collective-permute-start.18 = (bf16[2048,512]{1,0:T(8,128)(2,1)}, bf16[2048,512]{1,0:T(8,128)(2,1)}, u32[]{:S(2)}, u32[]{:S(2)}) collective-permute-start(bf16[2048,512]{1,0:T(8,128)(2,1)} %cut.3.refs_8_), channel_id=1, source_target_pairs={{0,16},{8,24},{16,0},{24,8},{1,17},{9,25},{17,1},{25,9},{2,18},{10... | collective-permute-start | bytes 6291464 | tf_op jit(solution)/shard_map/ppermute | solution.py:93
  65.4 2.2 %collective-permute-start.6 = (bf16[176,2048]{1,0:T(8,128)(2,1)S(1)}, bf16[176,2048]{1,0:T(8,128)(2,1)S(1)}, u32[]{:S(2)}, u32[]{:S(2)}) collective-permute-start(bf16[176,2048]{1,0:T(8,128)(2,1)S(1)} %collective-permute-done.5.refs_6_.refs_1_.refs_3_), channel_id=1, source_target_pairs={{0,1},{1,0},{2,3},{3,2},{4,5},{5,4},{6,7},{7,6},{8,9},{9,8},{10,11... | collective-permute-start | bytes 2162696 | tf_op jit(solution)/shard_map/ppermute | solution.py:109
  74.2 22.6 %collective-permute-start.11 = (bf16[512,512]{1,0:T(8,128)(2,1)S(1)}, bf16[512,512]{1,0:T(8,128)(2,1)}, u32[]{:S(2)}, u32[]{:S(2)}) collective-permute-start(bf16[512,512]{1,0:T(8,128)(2,1)S(1)} %get-tuple-element.29.query_ref), channel_id=1, source_target_pairs={{0,2},{2,0},{4,6},{6,4},{1,3},{3,1},{5,7},{7,5},{8,10},{10,8},{12,... | collective-permute-start | bytes 1572872 | tf_op jit(solution)/shard_map/ppermute | solution.py:84
  76.0 27.4 %collective-permute-start.13 = (bf16[512,512]{1,0:T(8,128)(2,1)S(1)}, bf16[512,512]{1,0:T(8,128)(2,1)S(1)}, u32[]{:S(2)}, u32[]{:S(2)}) collective-permute-start(bf16[512,512]{1,0:T(8,128)(2,1)S(1)} %get-tuple-element.29.query_ref), channel_id=1, source_target_pairs={{0,4},{2,6},{4,0},{6,2},{1,5},{3,7},{5,1},{7,3},{8,12},{10,14},{12... | collective-permute-start | bytes 1572872 | tf_op jit(solution)/shard_map/ppermute | solution.py:84
  78.4 38.9 %collective-permute-start.19 = (bf16[256,512]{1,0:T(8,128)(2,1)}, bf16[256,512]{1,0:T(8,128)(2,1)S(1)}, u32[]{:S(2)}, u32[]{:S(2)}) collective-permute-start(bf16[256,512]{1,0:T(8,128)(2,1)} %arrange.1.refs_1_.refs_0_.refs_11_), channel_id=1, source_target_pairs={{0,24},{8,16},{16,8},{24,0},{1,25},{9,17},{17,9},{25,1},{2,26},{10... | collective-permute-start | bytes 786440 | tf_op jit(solution)/shard_map/ppermute | solution.py:672
  87.7 9.1 %copy-start.1 = (bf16[1,1024,2048]{2,1,0:T(8,128)(2,1)S(1)}, bf16[1,1024,2048]{2,1,0:T(8,128)(2,1)}, u32[]{:S(2)}) copy-start(bf16[1,1024,2048]{2,1,0:T(8,128)(2,1)} %key_ref.7) | copy-start | bytes 12582916
  87.7 9.1 %copy-start.3 = (bf16[1,1024,2048]{2,1,0:T(8,128)(2,1)S(1)}, bf16[1,1024,2048]{2,1,0:T(8,128)(2,1)}, u32[]{:S(2)}) copy-start(bf16[1,1024,2048]{2,1,0:T(8,128)(2,1)} %value_ref.7) | copy-start | bytes 12582916
  87.7 9.1 %copy-start.9 = (bf16[2,128,2048]{2,1,0:T(8,128)(2,1)S(1)}, bf16[2,128,2048]{2,1,0:T(8,128)(2,1)}, u32[]{:S(2)}) copy-start(bf16[2,128,2048]{2,1,0:T(8,128)(2,1)} %shared_key_ref.7) | copy-start | bytes 3145732
  87.7 9.1 %copy-start.11 = (bf16[2,128,2048]{2,1,0:T(8,128)(2,1)S(1)}, bf16[2,128,2048]{2,1,0:T(8,128)(2,1)}, u32[]{:S(2)}) copy-start(bf16[2,128,2048]{2,1,0:T(8,128)(2,1)} %shared_value_ref.7) | copy-start | bytes 3145732
  103.4 14.1 %copy-start.26 = (bf16[256,512]{1,0:T(8,128)(2,1)S(1)}, bf16[256,512]{1,0:T(8,128)(2,1)}, u32[]{:S(2)}) copy-start(bf16[256,512]{1,0:T(8,128)(2,1)} %arrange.1.refs_1_.refs_0_.refs_11_) | copy-start | bytes 786436
  103.5 14.1 %copy-start.27 = (bf16[1,512,512]{2,1,0:T(8,128)(2,1)S(1)}, bf16[1,512,512]{2,1,0:T(8,128)(2,1)}, u32[]{:S(2)}) copy-start(bf16[1,512,512]{2,1,0:T(8,128)(2,1)} %param.21) | copy-start | bytes 1572868
  118.2 17.7 %collective-permute-start.20 = (bf16[768,512]{1,0:T(8,128)(2,1)S(1)}, bf16[768,512]{1,0:T(8,128)(2,1)S(1)}, u32[]{:S(2)}, u32[]{:S(2)}) collective-permute-start(bf16[768,512]{1,0:T(8,128)(2,1)S(1)} %assemble.12.refs_0_), channel_id=1, source_target_pairs={{0,8},{8,0},{16,24},{24,16},{1,9},{9,1},{17,25},{25,17},{2,10},{10... | collective-permute-start | bytes 2359304 | tf_op jit(solution)/shard_map/ppermute | solution.py:89
  119.8 17.7 %collective-permute-start.22 = (bf16[768,512]{1,0:T(8,128)(2,1)S(1)}, bf16[768,512]{1,0:T(8,128)(2,1)S(1)}, u32[]{:S(2)}, u32[]{:S(2)}) collective-permute-start(bf16[768,512]{1,0:T(8,128)(2,1)S(1)} %assemble.12.refs_0_), channel_id=1, source_target_pairs={{0,16},{8,24},{16,0},{24,8},{1,17},{9,25},{17,1},{25,9},{2,18},{10... | collective-permute-start | bytes 2359304 | tf_op jit(solution)/shard_map/ppermute | solution.py:93
  120.3 19.1 %collective-permute-start.15 = (bf16[512,512]{1,0:T(8,128)(2,1)S(1)}, bf16[512,512]{1,0:T(8,128)(2,1)S(1)}, u32[]{:S(2)}, u32[]{:S(2)}) collective-permute-start(bf16[512,512]{1,0:T(8,128)(2,1)S(1)} %collective-permute-done.13.query_ref), channel_id=1, source_target_pairs={{0,2},{2,0},{4,6},{6,4},{1,3},{3,1},{5,7},{7,5},{8,10},{10,8},{12,... | collective-permute-start | bytes 1572872 | tf_op jit(solution)/shard_map/ppermute | solution.py:84
  121.7 20.4 %collective-permute-start.14 = (bf16[528,512]{1,0:T(8,128)(2,1)S(1)}, bf16[528,512]{1,0:T(8,128)(2,1)S(1)}, u32[]{:S(2)}, u32[]{:S(2)}) collective-permute-start(bf16[528,512]{1,0:T(8,128)(2,1)S(1)} %get-tuple-element.34), channel_id=1, source_target_pairs={{0,4},{2,6},{4,0},{6,2},{1,5},{3,7},{5,1},{7,3},{8,12},{10,14},{12... | collective-permute-start | bytes 1622024 | tf_op jit(solution)/shard_map/ppermute | solution.py:664
  135.9 10.6 %collective-permute-start.21 = (bf16[256,512]{1,0:T(8,128)(2,1)S(1)}, bf16[256,512]{1,0:T(8,128)(2,1)S(1)}, u32[]{:S(2)}, u32[]{:S(2)}) collective-permute-start(bf16[256,512]{1,0:T(8,128)(2,1)S(1)} %assemble.13), channel_id=1, source_target_pairs={{0,16},{8,24},{16,0},{24,8},{1,17},{9,25},{17,1},{25,9},{2,18},{10... | collective-permute-start | bytes 786440 | tf_op jit(solution)/shard_map/ppermute | solution.py:93
  137.5 9.0 %collective-permute-start.23 = (bf16[256,512]{1,0:T(8,128)(2,1)S(1)}, bf16[256,512]{1,0:T(8,128)(2,1)S(1)}, u32[]{:S(2)}, u32[]{:S(2)}) collective-permute-start(bf16[256,512]{1,0:T(8,128)(2,1)S(1)} %assemble.14), channel_id=1, source_target_pairs={{0,8},{8,0},{16,24},{24,16},{1,9},{9,1},{17,25},{25,17},{2,10},{10... | collective-permute-start | bytes 786440 | tf_op jit(solution)/shard_map/ppermute | solution.py:89
  139.2 17.5 %collective-permute-start.26 = (bf16[1024,512]{1,0:T(8,128)(2,1)S(1)}, bf16[1024,512]{1,0:T(8,128)(2,1)S(1)}, u32[]{:S(2)}, u32[]{:S(2)}) collective-permute-start(bf16[1024,512]{1,0:T(8,128)(2,1)S(1)} %assemble.17), channel_id=1, source_target_pairs={{0,1},{1,0},{2,3},{3,2},{4,5},{5,4},{6,7},{7,6},{8,9},{9,8},{10,11... | collective-permute-start | bytes 3145736 | tf_op jit(solution)/shard_map/ppermute | solution.py:109
  139.4 43.5 %collective-permute-start.28 = (bf16[1536,512]{1,0:T(8,128)(2,1)S(1)}, bf16[1536,512]{1,0:T(8,128)(2,1)S(1)}, u32[]{:S(2)}, u32[]{:S(2)}) collective-permute-start(bf16[1536,512]{1,0:T(8,128)(2,1)S(1)} %assemble.18), channel_id=1, source_target_pairs={{0,1},{1,0},{2,3},{3,2},{4,5},{5,4},{6,7},{7,6},{8,9},{9,8},{10,11... | collective-permute-start | bytes 4718600 | tf_op jit(solution)/shard_map/ppermute | solution.py:109
  142.1 14.5 %collective-permute-start.12 = (bf16[528,512]{1,0:T(8,128)(2,1)S(1)}, bf16[528,512]{1,0:T(8,128)(2,1)S(1)}, u32[]{:S(2)}, u32[]{:S(2)}) collective-permute-start(bf16[528,512]{1,0:T(8,128)(2,1)S(1)} %get-tuple-element.32), channel_id=1, source_target_pairs={{0,2},{2,0},{4,6},{6,4},{1,3},{3,1},{5,7},{7,5},{8,10},{10,8},{12,... | collective-permute-start | bytes 1622024 | tf_op jit(solution)/shard_map/ppermute | solution.py:664
  148.2 29.5 %collective-permute-start.25 = (bf16[1024,512]{1,0:T(8,128)(2,1)S(1)}, bf16[1024,512]{1,0:T(8,128)(2,1)S(1)}, u32[]{:S(2)}, u32[]{:S(2)}) collective-permute-start(bf16[1024,512]{1,0:T(8,128)(2,1)S(1)} %assemble.16), channel_id=1, source_target_pairs={{0,8},{8,0},{16,24},{24,16},{1,9},{9,1},{17,25},{25,17},{2,10},{10... | collective-permute-start | bytes 3145736 | tf_op jit(solution)/shard_map/ppermute | solution.py:89
  149.8 7.0 %copy-start.5 = (bf16[176,2048]{1,0:T(8,128)(2,1)S(1)}, bf16[176,2048]{1,0:T(8,128)(2,1)}, u32[]{:S(2)}) copy-start(bf16[176,2048]{1,0:T(8,128)(2,1)} %copy-done.4) | copy-start | bytes 2162692
  149.8 7.0 %copy-start.7 = (bf16[176,2048]{1,0:T(8,128)(2,1)S(1)}, bf16[176,2048]{1,0:T(8,128)(2,1)}, u32[]{:S(2)}) copy-start(bf16[176,2048]{1,0:T(8,128)(2,1)} %copy-done.6) | copy-start | bytes 2162692
  149.8 7.0 %copy-start.15 = (bf16[176,2048]{1,0:T(8,128)(2,1)S(1)}, bf16[176,2048]{1,0:T(8,128)(2,1)}, u32[]{:S(2)}) copy-start(bf16[176,2048]{1,0:T(8,128)(2,1)} %get-tuple-element.26.refs_0_) | copy-start | bytes 2162692
  149.9 27.8 %collective-permute-start.24 = (bf16[1024,512]{1,0:T(8,128)(2,1)S(1)}, bf16[1024,512]{1,0:T(8,128)(2,1)S(1)}, u32[]{:S(2)}, u32[]{:S(2)}) collective-permute-start(bf16[1024,512]{1,0:T(8,128)(2,1)S(1)} %assemble.15), channel_id=1, source_target_pairs={{0,16},{8,24},{16,0},{24,8},{1,17},{9,25},{17,1},{25,9},{2,18},{10... | collective-permute-start | bytes 3145736 | tf_op jit(solution)/shard_map/ppermute | solution.py:93
  156.6 21.1 %collective-permute-start.16 = (bf16[528,512]{1,0:T(8,128)(2,1)S(1)}, bf16[528,512]{1,0:T(8,128)(2,1)S(1)}, u32[]{:S(2)}, u32[]{:S(2)}) collective-permute-start(bf16[528,512]{1,0:T(8,128)(2,1)S(1)} %get-tuple-element.36), channel_id=1, source_target_pairs={{0,6},{2,4},{4,2},{6,0},{1,7},{3,5},{5,3},{7,1},{8,14},{10,12},{12... | collective-permute-start | bytes 1622024 | tf_op jit(solution)/shard_map/ppermute | solution.py:664
  156.7 26.1 %collective-permute-start.29 = (bf16[512,512]{1,0:T(8,128)(2,1)S(1)}, bf16[512,512]{1,0:T(8,128)(2,1)S(1)}, u32[]{:S(2)}, u32[]{:S(2)}) collective-permute-start(bf16[512,512]{1,0:T(8,128)(2,1)S(1)} %assemble.19), channel_id=1, source_target_pairs={{0,1},{1,0},{2,3},{3,2},{4,5},{5,4},{6,7},{7,6},{8,9},{9,8},{10,11... | collective-permute-start | bytes 1572872 | tf_op jit(solution)/shard_map/ppermute | solution.py:109
  182.7 1.6 collective-permute-start.27
  186.2 10.7 %collective-permute-start.30 = (bf16[64,2048]{1,0:T(8,128)(2,1)S(1)}, bf16[64,2048]{1,0:T(8,128)(2,1)S(1)}, u32[]{:S(2)}, u32[]{:S(2)}) collective-permute-start(bf16[64,2048]{1,0:T(8,128)(2,1)S(1)} %get-tuple-element.44), channel_id=1, source_target_pairs={{0,2},{2,0},{4,6},{6,4},{1,3},{3,1},{5,7},{7,5},{8,10},{10,8},{12,... | collective-permute-start | bytes 786440 | tf_op jit(solution)/shard_map/ppermute | solution.py:697
  186.3 19.9 %collective-permute-start.31 = (bf16[64,2048]{1,0:T(8,128)(2,1)S(1)}, bf16[64,2048]{1,0:T(8,128)(2,1)S(1)}, u32[]{:S(2)}, u32[]{:S(2)}) collective-permute-start(bf16[64,2048]{1,0:T(8,128)(2,1)S(1)} %get-tuple-element.45), channel_id=1, source_target_pairs={{0,4},{2,6},{4,0},{6,2},{1,5},{3,7},{5,1},{7,3},{8,12},{10,14},{12... | collective-permute-start | bytes 786440 | tf_op jit(solution)/shard_map/ppermute | solution.py:697
  188.3 24.4 %collective-permute-start.32 = (bf16[64,2048]{1,0:T(8,128)(2,1)S(1)}, bf16[64,2048]{1,0:T(8,128)(2,1)S(1)}, u32[]{:S(2)}, u32[]{:S(2)}) collective-permute-start(bf16[64,2048]{1,0:T(8,128)(2,1)S(1)} %get-tuple-element.46), channel_id=1, source_target_pairs={{0,6},{2,4},{4,2},{6,0},{1,7},{3,5},{5,3},{7,1},{8,14},{10,12},{12... | collective-permute-start | bytes 786440 | tf_op jit(solution)/shard_map/ppermute | solution.py:697
  (17 other events, 81.6 us)

commit v5 on v4

--- a/solution.py
+++ b/solution.py
@@ -110,14 +110,16 @@
 
 
 def norm_kernel(down_rows, at, *refs):
-    count = (len(refs) - 3) // 2
-    sources, (out_ref, mark), held, sems = (
-        refs[:count],
-        refs[count : count + 2],
-        refs[count + 2 : -1],
-        refs[-1],
-    )
-    mark[0] = jnp.int32(0)
+    count = 3 if down_rows is None else 4
+    sources, held, sems = refs[:count], refs[-1 - count : -1], refs[-1]
+    if down_rows is None:
+        out_ref = refs[count]
+    else:
+        weights_ref, out_ref, cut_ref = refs[count : count + 3]
+        cutting = pltpu.make_async_copy(
+            weights_ref.at[: cut_ref.shape[0], :], cut_ref, sems.at[count]
+        )
+        cutting.start()
     copies = [
         pltpu.make_async_copy(source, target, sems.at[n])
         for n, (source, target) in enumerate(zip(sources, held))
@@ -154,22 +156,27 @@
                 columns = slice(g * x.shape[1], (g + 1) * x.shape[1])
                 out_ref[rows : rows + step, columns] = x[g * step : (g + 1) * step, :]
             rows += step
-
-
-def norm(at, hidden, embed, gain, down, down_rows):
+        cutting.wait()
+
+
+def norm(at, hidden, embed, gain, down, down_rows, weights, shard):
     rows, width = hidden.shape
     arrays = (hidden, embed, gain)
     if down_rows is not None:
         arrays += (down,)
         rows += HD * down.shape[0] // width + 2 * HD * down_rows // width
+    shapes = [jax.ShapeDtypeStruct((rows, width), BF16)]
+    held = [pltpu.VMEM(x.shape, x.dtype) for x in arrays]
+    if down_rows is not None:
+        arrays += (weights,)
+        shapes.append(jax.ShapeDtypeStruct((shard, weights.shape[1]), BF16))
     return pl.pallas_call(
         functools.partial(norm_kernel, down_rows),
-        out_shape=(jax.ShapeDtypeStruct((rows, width), BF16), MARK),
+        out_shape=shapes,
         in_specs=[pl.BlockSpec(memory_space=SMEM)]
         + [pl.BlockSpec(memory_space=pltpu.MemorySpace.HBM)] * len(arrays),
-        out_specs=(pl.BlockSpec(memory_space=pltpu.VMEM), pl.BlockSpec(memory_space=SMEM)),
-        scratch_shapes=[pltpu.VMEM(x.shape, x.dtype) for x in arrays]
-        + [pltpu.SemaphoreType.DMA((len(arrays),))],
+        out_specs=[pl.BlockSpec(memory_space=pltpu.VMEM)] * len(shapes),
+        scratch_shapes=held + [pltpu.SemaphoreType.DMA((len(arrays),))],
         compiler_params=params(60),
         cost_estimate=cost(1, 1),
         name="norm",
@@ -312,7 +319,7 @@
             pltpu.VMEM((rows, width), BF16),
             pltpu.VMEM((width, ranks) if down_rows is None else (ranks, width), BF16),
         ],
-        compiler_params=params((20 if len(inputs) == 1 else 32) if down_rows is not None else 40),
+        compiler_params=params((18 if len(inputs) == 1 else 28) if down_rows is not None else 40),
         cost_estimate=cost(
             2 * rows * width * (columns + HD) * len(inputs), 2 * width * (rows + columns * len(inputs))
         ),
@@ -341,7 +348,7 @@
             pltpu.VMEM((rows, last[0].shape[0]), BF16),
             pltpu.VMEM((8, HD), BF16),
         ],
-        compiler_params=params(24),
+        compiler_params=params(18),
         cost_estimate=cost(1, 1),
         name="project_rest",
     )(at, *arrays)
@@ -455,7 +462,7 @@
         in_specs=[pl.BlockSpec(memory_space=pltpu.VMEM)] * 3,
         out_specs=pl.BlockSpec(memory_space=pltpu.VMEM),
         scratch_shapes=[pltpu.VMEM((STAT_ROWS, rows), F32)],
-        compiler_params=params(16),
+        compiler_params=params(10),
         cost_estimate=cost(8 * rows * rows * width, 8 * rows * width, rows * rows * heads),
         name="new_attention",
     )(queries, keys, values)
@@ -517,7 +524,7 @@
             there = other[0][k * depth : (k + 1) * depth, :]
         else:
             half = depth // 2
-            here = jnp.dot(keep_ref[:, :half], mine[3][...], preferred_element_type=F32)
+            here = jnp.dot(keep_ref[:, :half], mine[3][:half, :], preferred_element_type=F32)
             here += jnp.dot(keep_ref[:, half:], mine[4][...], preferred_element_type=F32)
             there = other[1][...]
         here += jnp.dot(got_ref[...], there, preferred_element_type=F32)
@@ -622,20 +629,22 @@
 
     own_rows = hidden_states.shape[0]
     rows = own_rows * seq_count
-    half, mark = norm(
+    shard, _, _, width = input_weights.shape
+    own_weights = jnp.transpose(input_weights[:, :, 0], (1, 0, 2)).reshape(-1, width)
+    half, *weights = norm(
         at,
         hidden_states,
         embeddings,
         norm_gain[None, :],
         adapter_down,
         down_rows if by_four else None,
+        own_weights,
+        shard,
     )
     mine = spread(half)
     blocks = [(block, other_core(block)) for block in mine]
-    shard, _, _, width = input_weights.shape
     if by_four:
-        own_weights = jnp.transpose(input_weights[:, :, 0], (1, 0, 2)).reshape(-1, width)
-        weights = cut(own_weights, 0, shard, mark)
+        weights = weights[0]
         query, mark, arrived = query_4(at, blocks, rows, weights, ups[0], down_rows, mine[2])
     else:
         whole = lax.all_gather(input_weights[:, :, 0], "dp", axis=0, tiled=True)

time: 215 us -> 215 us (level)
  Pallas kernels: 58.3 us -> 60.5 us
    unnamed x64 -> x68, local copies, waits for them, and re-layouts: 8.82 us -> 6.95 us
  transfers between devices with their start and end apart: 33 -> 33, of which waited for: 13 -> 13; matrix products, arithmetic and copies ran while one was open for 0% -> 0% of each run, Pallas kernels for 23% -> 24%
where the time goes in v5:
time: 215 us; the launch traced here: 214 us
  waiting for transfers between devices  109 us (51%)
  Pallas kernels  60.5 us (28%)
  starting transfers between devices  33.9 us (16%)
  local copies, waits for them, and re-layouts  8.44 us (4%)
    ppermute x6, waiting for transfers between devices, spread(): blocks[k] = lax.ppermute(blocks[k ^ step], 'seq', swap(count, step))  46.3 us
    pallas_call x4, Pallas kernels, cache_attention(): pl.pallas_call(functools.partial(cache_kernel, slot, heads), out_shape=(j...  24.8 us
    ppermute x3, waiting for transfers between devices, shards(): lax.ppermute(sums[k], 'seq', swap(seq_count, k))  22.9 us
    pallas_call x2, Pallas kernels, project(): pl.pallas_call(functools.partial(project_kernel, (placed, len(arrays), tu...  15.5 us
    ppermute x3, waiting for transfers between devices, shards(): lax.ppermute(parts[k], 'seq', swap(seq_count, k))  14.9 us
    ppermute x6, waiting for transfers between devices, along_x(): return lax.ppermute(x, 'dp', swap(4, 1))  14.2 us
    ppermute x6, starting transfers between devices, spread(): blocks[k] = lax.ppermute(blocks[k ^ step], 'seq', swap(count, step))  9.51 us
    ppermute x6, starting transfers between devices, along_x(): return lax.ppermute(x, 'dp', swap(4, 1))  7.35 us
  transfers between devices with their start and end apart: 33, of which 13 were waited for; matrix products, arithmetic and copies ran while one was open for 0% of the time, Pallas kernels for 24%

profile of v5, /device:TPU:16, one launch (start us, length us, event | category | flops | bytes accessed | tf_op | source)
XLA Modules:
  0.0 213.6 jit_solution(4491437066858411385)
XLA Ops:
  1.3 0.7 stack.15.at
  2.0 4.1 %norm.1 = (bf16[176,2048]{1,0:T(8,128)(2,1)}, bf16[1024,512]{1,0:T(8,128)(2,1)}) custom-call(s32[5]{0:T(128)} %stack.15.at, bf16[128,2048]{1,0:T(8,128)(2,1)} %refs_0_.1, bf16[128,2048]{1,0:T(8,128)(2,1)} %refs_1_.1, f32[1,4096]{1,0:T(1,128)} %bitcast.24, bf16[512,384]{1,0:T(8,128)(2,1)} %refs_3_.1, bf16[3072,512]{1,0:T(8,128)(2,1)} %bitcast.17), custom_call_target="tpu_custom_call" | custom-call | flops 1 | bytes 1 | tf_op jit(solution)/shard_map/norm/pallas_call | solution.py:173
  6.1 1.6 collective-permute-start.8
  7.7 1.5 collective-permute-start.7
  9.5 1.6 collective-permute-start.1
  11.1 29.1 %collective-permute-done.3.refs_1_.refs_4_.refs_2_ = bf16[176,2048]{1,0:T(8,128)(2,1)S(1)} collective-permute-done((bf16[176,2048]{1,0:T(8,128)(2,1)}, bf16[176,2048]{1,0:T(8,128)(2,1)S(1)}, u32[]{:S(2)}, u32[]{:S(2)}) %collective-permute-start.3) | collective-permute-done | bytes 720928 | tf_op jit(solution)/shard_map/ppermute | solution.py:84
  40.2 4.4 %collective-permute-start.5 = (bf16[176,2048]{1,0:T(8,128)(2,1)S(1)}, bf16[176,2048]{1,0:T(8,128)(2,1)S(1)}, u32[]{:S(2)}, u32[]{:S(2)}) collective-permute-start(bf16[176,2048]{1,0:T(8,128)(2,1)S(1)} %collective-permute-done.3.refs_1_.refs_4_.refs_2_), channel_id=1, source_target_pairs={{0,2},{2,0},{4,6},{6,4},{1,3},{3,1},{5,7},{7,5},{8,10},{10,8},{12,... | collective-permute-start | bytes 2162696 | tf_op jit(solution)/shard_map/ppermute | solution.py:84
  46.4 14.5 %collective-permute-done.5.refs_6_.refs_1_.refs_3_ = bf16[176,2048]{1,0:T(8,128)(2,1)S(1)} collective-permute-done((bf16[176,2048]{1,0:T(8,128)(2,1)S(1)}, bf16[176,2048]{1,0:T(8,128)(2,1)S(1)}, u32[]{:S(2)}, u32[]{:S(2)}) %collective-permute-start.5) | collective-permute-done | bytes 720928 | tf_op jit(solution)/shard_map/ppermute | solution.py:84
  60.9 1.6 cut.1.refs_8_
  63.6 0.7 slice_bitcast_fusion
  64.4 1.5 collective-permute-done.6.refs_7_
  65.9 7.4 %project.2 = (bf16[512,512]{1,0:T(8,128)(2,1)}, s32[1]{0:T(128)}) custom-call(s32[5]{0:T(128)S(1)} %copy-done.30, bf16[176,2048]{1,0:T(8,128)(2,1)S(1)} %copy-done.13, bf16[176,2048]{1,0:T(8,128)(2,1)S(1)} %collective-permute-done.refs_1_.refs_2_, bf16[176,2048]{1,0:T(8,128)(2,1)S(1)} %collective-permute-done.1.refs_2_.refs_1_, ...), custom_call_target="tpu_custom_call" | custom-call | flops 1 | bytes 1 | tf_op jit(solution)/shard_map/project/pallas_call | solution.py:309
  73.3 1.8 collective-permute-start.11
  75.1 2.3 %arrange.1.refs_1_.refs_0_.refs_11_ = bf16[256,512]{1,0:T(8,128)(2,1)} custom-call(bf16[176,2048]{1,0:T(8,128)(2,1)} %get-tuple-element.26.refs_0_, bf16[176,2048]{1,0:T(8,128)(2,1)} %copy-done.15, bf16[176,2048]{1,0:T(8,128)(2,1)} %copy-done.4, bf16[176,2048]{1,0:T(8,128)(2,1)} %copy-done.6, s32[1]{0:T(128)} %get-tuple-element.28.earlier.refs_4_), custom_call_target="tpu_custom_call" | custom-call | flops 1 | bytes 1 | tf_op jit(solution)/shard_map/arrange/pallas_call | solution.py:209
  77.5 2.5 %collective-permute-start.19 = (bf16[256,512]{1,0:T(8,128)(2,1)}, bf16[256,512]{1,0:T(8,128)(2,1)S(1)}, u32[]{:S(2)}, u32[]{:S(2)}) collective-permute-start(bf16[256,512]{1,0:T(8,128)(2,1)} %arrange.1.refs_1_.refs_0_.refs_11_), channel_id=1, source_target_pairs={{0,24},{8,16},{16,8},{24,0},{1,25},{9,17},{17,9},{25,1},{2,26},{10... | collective-permute-start | bytes 786440 | tf_op jit(solution)/shard_map/ppermute | solution.py:681
  80.0 2.2 %copy-done = bf16[1,1024,2048]{2,1,0:T(8,128)(2,1)S(1)} copy-done((bf16[1,1024,2048]{2,1,0:T(8,128)(2,1)S(1)}, bf16[1,1024,2048]{2,1,0:T(8,128)(2,1)}, u32[]{:S(2)}) %copy-start) | copy-done | bytes 4194328
  82.2 2.2 %copy-done.2 = bf16[1,1024,2048]{2,1,0:T(8,128)(2,1)S(1)} copy-done((bf16[1,1024,2048]{2,1,0:T(8,128)(2,1)S(1)}, bf16[1,1024,2048]{2,1,0:T(8,128)(2,1)}, u32[]{:S(2)}) %copy-start.2) | copy-done | bytes 4194328
  84.4 1.2 copy-done.8
  85.6 1.2 copy-done.10
  86.8 6.8 %cache_attention.4 = (bf16[528,512]{1,0:T(8,128)(2,1)S(1)}, s32[1]{0:T(128)}) custom-call(s32[5]{0:T(128)S(1)} %copy-done.30, s32[1]{0:T(128)} %get-tuple-element.28.earlier.refs_4_, s32[16]{0:T(128)S(1)} %bitcast.20, bf16[512,512]{1,0:T(8,128)(2,1)} %get-tuple-element.29.query_ref, bf16[1,1024,2048]{2,1,0:T(8,128)(2,1)S(1)} %copy-done, ...), custom_call_target="tpu_custom_call" | custom-call | flops 1 | bytes 1 | tf_op jit(solution)/shard_map/cache_attention/pallas_call | solution.py:424
  93.6 2.7 %collective-permute-done.11.query_ref = bf16[512,512]{1,0:T(8,128)(2,1)S(1)} collective-permute-done((bf16[512,512]{1,0:T(8,128)(2,1)}, bf16[512,512]{1,0:T(8,128)(2,1)S(1)}, u32[]{:S(2)}, u32[]{:S(2)}) %collective-permute-start.11) | collective-permute-done | bytes 524320 | tf_op jit(solution)/shard_map/ppermute | solution.py:84
  96.4 6.0 %cache_attention.5 = (bf16[528,512]{1,0:T(8,128)(2,1)S(1)}, s32[1]{0:T(128)}) custom-call(s32[5]{0:T(128)S(1)} %copy-done.30, s32[1]{0:T(128)} %get-tuple-element.31.earlier, s32[16]{0:T(128)S(1)} %bitcast.21, bf16[512,512]{1,0:T(8,128)(2,1)S(1)} %collective-permute-done.11.query_ref, bf16[1,1024,2048]{2,1,0:T(8,128)(2,1)S(1)} %copy-done.1, ...), custom_call_target="tpu_custom_call" | custom-call | flops 1 | bytes 1 | tf_op jit(solution)/shard_map/cache_attention/pallas_call | solution.py:424
  102.4 5.8 %cache_attention.6 = (bf16[528,512]{1,0:T(8,128)(2,1)S(1)}, s32[1]{0:T(128)}) custom-call(s32[5]{0:T(128)S(1)} %copy-done.30, s32[1]{0:T(128)} %get-tuple-element.33.earlier, s32[16]{0:T(128)S(1)} %bitcast.22, bf16[512,512]{1,0:T(8,128)(2,1)S(1)} %collective-permute-done.13.query_ref, bf16[1,1024,2048]{2,1,0:T(8,128)(2,1)S(1)} %copy-done.1, ...), custom_call_target="tpu_custom_call" | custom-call | flops 1 | bytes 1 | tf_op jit(solution)/shard_map/cache_attention/pallas_call | solution.py:424
  108.2 7.2 %collective-permute-done.19.refs_4_.refs_3_.refs_14_ = bf16[256,512]{1,0:T(8,128)(2,1)S(1)} collective-permute-done((bf16[256,512]{1,0:T(8,128)(2,1)}, bf16[256,512]{1,0:T(8,128)(2,1)S(1)}, u32[]{:S(2)}, u32[]{:S(2)}) %collective-permute-start.19) | collective-permute-done | bytes 262176 | tf_op jit(solution)/shard_map/ppermute | solution.py:681
  115.8 0.7 assemble.12.refs_0_
  116.5 1.6 collective-permute-start.20
  118.5 1.4 collective-permute-start.15
  120.0 14.2 %collective-permute-done.20.refs_0_.refs_1_.refs_12_ = bf16[768,512]{1,0:T(8,128)(2,1)S(1)} collective-permute-done((bf16[768,512]{1,0:T(8,128)(2,1)S(1)}, bf16[768,512]{1,0:T(8,128)(2,1)S(1)}, u32[]{:S(2)}, u32[]{:S(2)}) %collective-permute-start.20) | collective-permute-done | bytes 786464 | tf_op jit(solution)/shard_map/ppermute | solution.py:89
  134.2 1.5 collective-permute-start.21
  135.8 1.6 collective-permute-start.23
  138.2 2.3 %collective-permute-done.14.refs_2_ = bf16[528,512]{1,0:T(8,128)(2,1)S(1)} collective-permute-done((bf16[528,512]{1,0:T(8,128)(2,1)S(1)}, bf16[528,512]{1,0:T(8,128)(2,1)S(1)}, u32[]{:S(2)}, u32[]{:S(2)}) %collective-permute-start.14) | collective-permute-done | bytes 540704 | tf_op jit(solution)/shard_map/ppermute | solution.py:673
  140.5 4.3 %collective-permute-start.12 = (bf16[528,512]{1,0:T(8,128)(2,1)S(1)}, bf16[528,512]{1,0:T(8,128)(2,1)S(1)}, u32[]{:S(2)}, u32[]{:S(2)}) collective-permute-start(bf16[528,512]{1,0:T(8,128)(2,1)S(1)} %get-tuple-element.32), channel_id=1, source_target_pairs={{0,2},{2,0},{4,6},{6,4},{1,3},{3,1},{5,7},{7,5},{8,10},{10,8},{12,... | collective-permute-start | bytes 1622024 | tf_op jit(solution)/shard_map/ppermute | solution.py:673
  144.8 1.7 assemble.16
  146.5 1.5 collective-permute-start.25
  148.8 6.1 %cache_attention.7 = (bf16[528,512]{1,0:T(8,128)(2,1)S(1)}, s32[1]{0:T(128)}) custom-call(s32[5]{0:T(128)S(1)} %copy-done.30, s32[1]{0:T(128)} %get-tuple-element.35.earlier.refs_5_, s32[16]{0:T(128)S(1)} %bitcast.23, bf16[512,512]{1,0:T(8,128)(2,1)S(1)} %collective-permute-done.15.query_ref.refs_1_, bf16[1,1024,2048]{2,1,0:T(8,128)(2,1)S(1)} %copy-done.1, ...), custom_call_target="tpu_custom_call" | custom-call | flops 1 | bytes 1 | tf_op jit(solution)/shard_map/cache_attention/pallas_call | solution.py:424
  155.2 8.1 %project.3 = (f32[512,512]{1,0:T(8,128)S(1)}, f32[512,512]{1,0:T(8,128)S(1)}, s32[1]{0:T(128)}) custom-call(s32[5]{0:T(128)S(1)} %copy-done.30, bf16[176,2048]{1,0:T(8,128)(2,1)S(1)} %copy-done.14, bf16[176,2048]{1,0:T(8,128)(2,1)S(1)} %copy-done.18, bf16[176,2048]{1,0:T(8,128)(2,1)S(1)} %copy-done.16, bf16[176,2048]{1,0:T(8,128)(2,1)S(1)} %copy-done.22, ...), custom_call_target="tpu_custom_call" | custom-call | flops 1 | bytes 1 | tf_op jit(solution)/shard_map/project/pallas_call | solution.py:309
  163.4 12.6 %collective-permute-done.16.refs_13_.refs_3_ = bf16[528,512]{1,0:T(8,128)(2,1)S(1)} collective-permute-done((bf16[528,512]{1,0:T(8,128)(2,1)S(1)}, bf16[528,512]{1,0:T(8,128)(2,1)S(1)}, u32[]{:S(2)}, u32[]{:S(2)}) %collective-permute-start.16) | collective-permute-done | bytes 540704 | tf_op jit(solution)/shard_map/ppermute | solution.py:673
  176.0 1.9 project_rest.1
  177.9 2.9 %new_attention.1.refs_4_ = bf16[528,512]{1,0:T(8,128)(2,1)S(1)} custom-call(bf16[512,512]{1,0:T(8,128)(2,1)} %get-tuple-element.29.query_ref, bf16[512,512]{1,0:T(8,128)(2,1)S(1)} %get-tuple-element.39.key_ref, bf16[512,512]{1,0:T(8,128)(2,1)S(1)} %get-tuple-element.40.value_ref), custom_call_target="tpu_custom_call" | custom-call | flops 1 | bytes 1 | tf_op jit(solution)/shard_map/new_attention/pallas_call | solution.py:459
  180.8 1.3 merge.1
  182.2 1.5 collective-permute-done.27.got_ref
  183.7 1.9 output_projection.1
  185.7 2.2 %collective-permute-start.31 = (bf16[64,2048]{1,0:T(8,128)(2,1)S(1)}, bf16[64,2048]{1,0:T(8,128)(2,1)S(1)}, u32[]{:S(2)}, u32[]{:S(2)}) collective-permute-start(bf16[64,2048]{1,0:T(8,128)(2,1)S(1)} %get-tuple-element.45), channel_id=1, source_target_pairs={{0,4},{2,6},{4,0},{6,2},{1,5},{3,7},{5,1},{7,3},{8,12},{10,14},{12... | collective-permute-start | bytes 786440 | tf_op jit(solution)/shard_map/ppermute | solution.py:706
  187.9 1.3 collective-permute-start.32
  189.1 7.3 %collective-permute-done.30.refs_1_ = bf16[64,2048]{1,0:T(8,128)(2,1)S(1)} collective-permute-done((bf16[64,2048]{1,0:T(8,128)(2,1)S(1)}, bf16[64,2048]{1,0:T(8,128)(2,1)S(1)}, u32[]{:S(2)}, u32[]{:S(2)}) %collective-permute-start.30) | collective-permute-done | bytes 262176 | tf_op jit(solution)/shard_map/ppermute | solution.py:706
  196.4 9.4 %collective-permute-done.31.refs_2_ = bf16[64,2048]{1,0:T(8,128)(2,1)S(1)} collective-permute-done((bf16[64,2048]{1,0:T(8,128)(2,1)S(1)}, bf16[64,2048]{1,0:T(8,128)(2,1)S(1)}, u32[]{:S(2)}, u32[]{:S(2)}) %collective-permute-start.31) | collective-permute-done | bytes 262176 | tf_op jit(solution)/shard_map/ppermute | solution.py:706
  205.8 6.3 %collective-permute-done.32.refs_3_ = bf16[64,2048]{1,0:T(8,128)(2,1)S(1)} collective-permute-done((bf16[64,2048]{1,0:T(8,128)(2,1)S(1)}, bf16[64,2048]{1,0:T(8,128)(2,1)S(1)}, u32[]{:S(2)}, u32[]{:S(2)}) %collective-permute-start.32) | collective-permute-done | bytes 262176 | tf_op jit(solution)/shard_map/ppermute | solution.py:706
  212.1 1.4 final_sum.1
  (114 shorter events, 6.1 us)
Async XLA Ops:
  6.1 38.4 %collective-permute-start.8 = (bf16[1024,512]{1,0:T(8,128)(2,1)}, bf16[1024,512]{1,0:T(8,128)(2,1)S(1)}, u32[]{:S(2)}, u32[]{:S(2)}) collective-permute-start(bf16[1024,512]{1,0:T(8,128)(2,1)} %get-tuple-element.27.refs_8_), channel_id=1, source_target_pairs={{0,16},{8,24},{16,0},{24,8},{1,17},{9,25},{17,1},{25,9},{2,18},{10... | collective-permute-start | bytes 3145736 | tf_op jit(solution)/shard_map/ppermute | solution.py:93
  7.7 37.4 %collective-permute-start.7 = (bf16[1024,512]{1,0:T(8,128)(2,1)}, bf16[1024,512]{1,0:T(8,128)(2,1)S(1)}, u32[]{:S(2)}, u32[]{:S(2)}) collective-permute-start(bf16[1024,512]{1,0:T(8,128)(2,1)} %get-tuple-element.27.refs_8_), channel_id=1, source_target_pairs={{0,8},{8,0},{16,24},{24,16},{1,9},{9,1},{17,25},{25,17},{2,10},{10... | collective-permute-start | bytes 3145736 | tf_op jit(solution)/shard_map/ppermute | solution.py:89
  9.2 51.7 %copy-start.12 = (bf16[1024,3,1,512]{3,0,2,1:T(8,128)(2,1)S(1)}, bf16[1024,3,1,512]{3,0,2,1:T(8,128)(2,1)}, u32[]{:S(2)}) copy-start(bf16[1024,3,1,512]{3,0,2,1:T(8,128)(2,1)} %param.18) | copy-start | bytes 9437188
  9.2 31.0 %collective-permute-start.3 = (bf16[176,2048]{1,0:T(8,128)(2,1)}, bf16[176,2048]{1,0:T(8,128)(2,1)S(1)}, u32[]{:S(2)}, u32[]{:S(2)}) collective-permute-start(bf16[176,2048]{1,0:T(8,128)(2,1)} %get-tuple-element.26.refs_0_), channel_id=1, source_target_pairs={{0,4},{2,6},{4,0},{6,2},{1,5},{3,7},{5,1},{7,3},{8,12},{10,14},{12... | collective-permute-start | bytes 2162696 | tf_op jit(solution)/shard_map/ppermute | solution.py:84
  9.5 35.0 %collective-permute-start.1 = (bf16[176,2048]{1,0:T(8,128)(2,1)}, bf16[176,2048]{1,0:T(8,128)(2,1)S(1)}, u32[]{:S(2)}, u32[]{:S(2)}) collective-permute-start(bf16[176,2048]{1,0:T(8,128)(2,1)} %get-tuple-element.26.refs_0_), channel_id=1, source_target_pairs={{0,2},{2,0},{4,6},{6,4},{1,3},{3,1},{5,7},{7,5},{8,10},{10,8},{12,... | collective-permute-start | bytes 2162696 | tf_op jit(solution)/shard_map/ppermute | solution.py:84
  11.1 34.7 %collective-permute-start = (bf16[176,2048]{1,0:T(8,128)(2,1)}, bf16[176,2048]{1,0:T(8,128)(2,1)S(1)}, u32[]{:S(2)}, u32[]{:S(2)}) collective-permute-start(bf16[176,2048]{1,0:T(8,128)(2,1)} %get-tuple-element.26.refs_0_), channel_id=1, source_target_pairs={{0,1},{1,0},{2,3},{3,2},{4,5},{5,4},{6,7},{7,6},{8,9},{9,8},{10,11... | collective-permute-start | bytes 2162696 | tf_op jit(solution)/shard_map/ppermute | solution.py:109
  40.1 25.7 %copy-start.4 = (bf16[176,2048]{1,0:T(8,128)(2,1)}, bf16[176,2048]{1,0:T(8,128)(2,1)S(1)}, u32[]{:S(2)}) copy-start(bf16[176,2048]{1,0:T(8,128)(2,1)S(1)} %collective-permute-done.3.refs_1_.refs_4_.refs_2_) | copy-start | bytes 2162692
  40.2 20.7 %collective-permute-start.5 = (bf16[176,2048]{1,0:T(8,128)(2,1)S(1)}, bf16[176,2048]{1,0:T(8,128)(2,1)S(1)}, u32[]{:S(2)}, u32[]{:S(2)}) collective-permute-start(bf16[176,2048]{1,0:T(8,128)(2,1)S(1)} %collective-permute-done.3.refs_1_.refs_4_.refs_2_), channel_id=1, source_target_pairs={{0,2},{2,0},{4,6},{6,4},{1,3},{3,1},{5,7},{7,5},{8,10},{10,8},{12,... | collective-permute-start | bytes 2162696 | tf_op jit(solution)/shard_map/ppermute | solution.py:84
  44.5 21.3 %copy-start.15 = (bf16[176,2048]{1,0:T(8,128)(2,1)}, bf16[176,2048]{1,0:T(8,128)(2,1)S(1)}, u32[]{:S(2)}) copy-start(bf16[176,2048]{1,0:T(8,128)(2,1)S(1)} %collective-permute-done.1.refs_2_.refs_1_) | copy-start | bytes 2162692
  44.5 16.3 %collective-permute-start.4 = (bf16[176,2048]{1,0:T(8,128)(2,1)S(1)}, bf16[176,2048]{1,0:T(8,128)(2,1)S(1)}, u32[]{:S(2)}, u32[]{:S(2)}) collective-permute-start(bf16[176,2048]{1,0:T(8,128)(2,1)S(1)} %collective-permute-done.3.refs_1_.refs_4_.refs_2_), channel_id=1, source_target_pairs={{0,1},{1,0},{2,3},{3,2},{4,5},{5,4},{6,7},{7,6},{8,9},{9,8},{10,11... | collective-permute-start | bytes 2162696 | tf_op jit(solution)/shard_map/ppermute | solution.py:109
  44.5 16.3 %collective-permute-start.2 = (bf16[176,2048]{1,0:T(8,128)(2,1)S(1)}, bf16[176,2048]{1,0:T(8,128)(2,1)S(1)}, u32[]{:S(2)}, u32[]{:S(2)}) collective-permute-start(bf16[176,2048]{1,0:T(8,128)(2,1)S(1)} %collective-permute-done.1.refs_2_.refs_1_), channel_id=1, source_target_pairs={{0,1},{1,0},{2,3},{3,2},{4,5},{5,4},{6,7},{7,6},{8,9},{9,8},{10,11... | collective-permute-start | bytes 2162696 | tf_op jit(solution)/shard_map/ppermute | solution.py:109
  45.1 15.8 %collective-permute-start.10 = (bf16[512,512]{1,0:T(8,128)(2,1)S(1)}, bf16[512,512]{1,0:T(8,128)(2,1)S(1)}, u32[]{:S(2)}, u32[]{:S(2)}) collective-permute-start(bf16[512,512]{1,0:T(8,128)(2,1)S(1)} %assemble.11), channel_id=1, source_target_pairs={{0,8},{8,0},{16,24},{24,16},{1,9},{9,1},{17,25},{25,17},{2,10},{10... | collective-permute-start | bytes 1572872 | tf_op jit(solution)/shard_map/ppermute | solution.py:89
  45.7 17.9 %copy-start.32 = (bf16[3,128,1,512]{3,1,2,0:T(8,128)(2,1)S(1)}, bf16[3,128,1,512]{3,1,2,0:T(8,128)(2,1)}, u32[]{:S(2)}) copy-start(bf16[3,128,1,512]{3,1,2,0:T(8,128)(2,1)} %param.20) | copy-start | bytes 1179652
  45.7 20.1 %copy-start.13 = (bf16[176,2048]{1,0:T(8,128)(2,1)S(1)}, bf16[176,2048]{1,0:T(8,128)(2,1)}, u32[]{:S(2)}) copy-start(bf16[176,2048]{1,0:T(8,128)(2,1)} %get-tuple-element.26.refs_0_) | copy-start | bytes 2162692
  45.7 20.1 %copy-start.26 = (bf16[1024,512]{1,0:T(8,128)(2,1)S(1)}, bf16[1024,512]{1,0:T(8,128)(2,1)}, u32[]{:S(2)}) copy-start(bf16[1024,512]{1,0:T(8,128)(2,1)} %get-tuple-element.27.refs_8_) | copy-start | bytes 3145732
  45.7 20.1 %copy-start.30 = (s32[5]{0:T(128)S(1)}, s32[5]{0:T(128)}, u32[]{:S(2)}) copy-start(s32[5]{0:T(128)} %stack.15.at) | copy-start | bytes 64
  45.8 20.1 %copy-start.17 = (bf16[176,2048]{1,0:T(8,128)(2,1)}, bf16[176,2048]{1,0:T(8,128)(2,1)S(1)}, u32[]{:S(2)}) copy-start(bf16[176,2048]{1,0:T(8,128)(2,1)S(1)} %collective-permute-done.refs_1_.refs_2_) | copy-start | bytes 2162692
  45.8 15.1 %collective-permute-start.9 = (bf16[512,512]{1,0:T(8,128)(2,1)S(1)}, bf16[512,512]{1,0:T(8,128)(2,1)S(1)}, u32[]{:S(2)}, u32[]{:S(2)}) collective-permute-start(bf16[512,512]{1,0:T(8,128)(2,1)S(1)} %assemble.10), channel_id=1, source_target_pairs={{0,16},{8,24},{16,0},{24,8},{1,17},{9,25},{17,1},{25,9},{2,18},{10... | collective-permute-start | bytes 1572872 | tf_op jit(solution)/shard_map/ppermute | solution.py:93
  62.5 53.0 %collective-permute-start.17 = (bf16[2048,512]{1,0:T(8,128)(2,1)}, bf16[2048,512]{1,0:T(8,128)(2,1)S(1)}, u32[]{:S(2)}, u32[]{:S(2)}) collective-permute-start(bf16[2048,512]{1,0:T(8,128)(2,1)} %cut.1.refs_8_), channel_id=1, source_target_pairs={{0,8},{8,0},{16,24},{24,16},{1,9},{9,1},{17,25},{25,17},{2,10},{10... | collective-permute-start | bytes 6291464 | tf_op jit(solution)/shard_map/ppermute | solution.py:89
  63.1 52.7 %collective-permute-start.18 = (bf16[2048,512]{1,0:T(8,128)(2,1)}, bf16[2048,512]{1,0:T(8,128)(2,1)}, u32[]{:S(2)}, u32[]{:S(2)}) collective-permute-start(bf16[2048,512]{1,0:T(8,128)(2,1)} %cut.1.refs_8_), channel_id=1, source_target_pairs={{0,16},{8,24},{16,0},{24,8},{1,17},{9,25},{17,1},{25,9},{2,18},{10... | collective-permute-start | bytes 6291464 | tf_op jit(solution)/shard_map/ppermute | solution.py:93
  63.6 2.2 %collective-permute-start.6 = (bf16[176,2048]{1,0:T(8,128)(2,1)S(1)}, bf16[176,2048]{1,0:T(8,128)(2,1)S(1)}, u32[]{:S(2)}, u32[]{:S(2)}) collective-permute-start(bf16[176,2048]{1,0:T(8,128)(2,1)S(1)} %collective-permute-done.5.refs_6_.refs_1_.refs_3_), channel_id=1, source_target_pairs={{0,1},{1,0},{2,3},{3,2},{4,5},{5,4},{6,7},{7,6},{8,9},{9,8},{10,11... | collective-permute-start | bytes 2162696 | tf_op jit(solution)/shard_map/ppermute | solution.py:109
  65.8 7.5 %copy-start.23 = (bf16[176,2048]{1,0:T(8,128)(2,1)}, bf16[176,2048]{1,0:T(8,128)(2,1)S(1)}, u32[]{:S(2)}) copy-start(bf16[176,2048]{1,0:T(8,128)(2,1)S(1)} %collective-permute-done.6.refs_7_) | copy-start | bytes 2162692
  73.3 23.0 %collective-permute-start.11 = (bf16[512,512]{1,0:T(8,128)(2,1)}, bf16[512,512]{1,0:T(8,128)(2,1)S(1)}, u32[]{:S(2)}, u32[]{:S(2)}) collective-permute-start(bf16[512,512]{1,0:T(8,128)(2,1)} %get-tuple-element.29.query_ref), channel_id=1, source_target_pairs={{0,2},{2,0},{4,6},{6,4},{1,3},{3,1},{5,7},{7,5},{8,10},{10,8},{12,... | collective-permute-start | bytes 1572872 | tf_op jit(solution)/shard_map/ppermute | solution.py:84
  75.1 27.2 %collective-permute-start.13 = (bf16[512,512]{1,0:T(8,128)(2,1)}, bf16[512,512]{1,0:T(8,128)(2,1)S(1)}, u32[]{:S(2)}, u32[]{:S(2)}) collective-permute-start(bf16[512,512]{1,0:T(8,128)(2,1)} %get-tuple-element.29.query_ref), channel_id=1, source_target_pairs={{0,4},{2,6},{4,0},{6,2},{1,5},{3,7},{5,1},{7,3},{8,12},{10,14},{12... | collective-permute-start | bytes 1572872 | tf_op jit(solution)/shard_map/ppermute | solution.py:84
  77.5 38.0 %collective-permute-start.19 = (bf16[256,512]{1,0:T(8,128)(2,1)}, bf16[256,512]{1,0:T(8,128)(2,1)S(1)}, u32[]{:S(2)}, u32[]{:S(2)}) collective-permute-start(bf16[256,512]{1,0:T(8,128)(2,1)} %arrange.1.refs_1_.refs_0_.refs_11_), channel_id=1, source_target_pairs={{0,24},{8,16},{16,8},{24,0},{1,25},{9,17},{17,9},{25,1},{2,26},{10... | collective-permute-start | bytes 786440 | tf_op jit(solution)/shard_map/ppermute | solution.py:681
  86.8 9.5 %copy-start.1 = (bf16[1,1024,2048]{2,1,0:T(8,128)(2,1)S(1)}, bf16[1,1024,2048]{2,1,0:T(8,128)(2,1)}, u32[]{:S(2)}) copy-start(bf16[1,1024,2048]{2,1,0:T(8,128)(2,1)} %key_ref.7) | copy-start | bytes 12582916
  86.8 9.5 %copy-start.3 = (bf16[1,1024,2048]{2,1,0:T(8,128)(2,1)S(1)}, bf16[1,1024,2048]{2,1,0:T(8,128)(2,1)}, u32[]{:S(2)}) copy-start(bf16[1,1024,2048]{2,1,0:T(8,128)(2,1)} %value_ref.7) | copy-start | bytes 12582916
  86.8 9.5 %copy-start.9 = (bf16[2,128,2048]{2,1,0:T(8,128)(2,1)S(1)}, bf16[2,128,2048]{2,1,0:T(8,128)(2,1)}, u32[]{:S(2)}) copy-start(bf16[2,128,2048]{2,1,0:T(8,128)(2,1)} %shared_key_ref.7) | copy-start | bytes 3145732
  86.8 9.5 %copy-start.11 = (bf16[2,128,2048]{2,1,0:T(8,128)(2,1)S(1)}, bf16[2,128,2048]{2,1,0:T(8,128)(2,1)}, u32[]{:S(2)}) copy-start(bf16[2,128,2048]{2,1,0:T(8,128)(2,1)} %shared_value_ref.7) | copy-start | bytes 3145732
  102.4 13.4 %copy-start.25 = (bf16[256,512]{1,0:T(8,128)(2,1)S(1)}, bf16[256,512]{1,0:T(8,128)(2,1)}, u32[]{:S(2)}) copy-start(bf16[256,512]{1,0:T(8,128)(2,1)} %arrange.1.refs_1_.refs_0_.refs_11_) | copy-start | bytes 786436
  102.4 13.4 %copy-start.29 = (bf16[1,512,512]{2,1,0:T(8,128)(2,1)S(1)}, bf16[1,512,512]{2,1,0:T(8,128)(2,1)}, u32[]{:S(2)}) copy-start(bf16[1,512,512]{2,1,0:T(8,128)(2,1)} %param.21) | copy-start | bytes 1572868
  116.5 17.7 %collective-permute-start.20 = (bf16[768,512]{1,0:T(8,128)(2,1)S(1)}, bf16[768,512]{1,0:T(8,128)(2,1)S(1)}, u32[]{:S(2)}, u32[]{:S(2)}) collective-permute-start(bf16[768,512]{1,0:T(8,128)(2,1)S(1)} %assemble.12.refs_0_), channel_id=1, source_target_pairs={{0,8},{8,0},{16,24},{24,16},{1,9},{9,1},{17,25},{25,17},{2,10},{10... | collective-permute-start | bytes 2359304 | tf_op jit(solution)/shard_map/ppermute | solution.py:89
  118.0 17.7 %collective-permute-start.22 = (bf16[768,512]{1,0:T(8,128)(2,1)S(1)}, bf16[768,512]{1,0:T(8,128)(2,1)S(1)}, u32[]{:S(2)}, u32[]{:S(2)}) collective-permute-start(bf16[768,512]{1,0:T(8,128)(2,1)S(1)} %assemble.12.refs_0_), channel_id=1, source_target_pairs={{0,16},{8,24},{16,0},{24,8},{1,17},{9,25},{17,1},{25,9},{2,18},{10... | collective-permute-start | bytes 2359304 | tf_op jit(solution)/shard_map/ppermute | solution.py:93
  118.5 19.1 %collective-permute-start.15 = (bf16[512,512]{1,0:T(8,128)(2,1)S(1)}, bf16[512,512]{1,0:T(8,128)(2,1)S(1)}, u32[]{:S(2)}, u32[]{:S(2)}) collective-permute-start(bf16[512,512]{1,0:T(8,128)(2,1)S(1)} %collective-permute-done.13.query_ref), channel_id=1, source_target_pairs={{0,2},{2,0},{4,6},{6,4},{1,3},{3,1},{5,7},{7,5},{8,10},{10,8},{12,... | collective-permute-start | bytes 1572872 | tf_op jit(solution)/shard_map/ppermute | solution.py:84
  120.0 20.5 %collective-permute-start.14 = (bf16[528,512]{1,0:T(8,128)(2,1)S(1)}, bf16[528,512]{1,0:T(8,128)(2,1)S(1)}, u32[]{:S(2)}, u32[]{:S(2)}) collective-permute-start(bf16[528,512]{1,0:T(8,128)(2,1)S(1)} %get-tuple-element.34), channel_id=1, source_target_pairs={{0,4},{2,6},{4,0},{6,2},{1,5},{3,7},{5,1},{7,3},{8,12},{10,14},{12... | collective-permute-start | bytes 1622024 | tf_op jit(solution)/shard_map/ppermute | solution.py:673
  134.2 10.6 %collective-permute-start.21 = (bf16[256,512]{1,0:T(8,128)(2,1)S(1)}, bf16[256,512]{1,0:T(8,128)(2,1)S(1)}, u32[]{:S(2)}, u32[]{:S(2)}) collective-permute-start(bf16[256,512]{1,0:T(8,128)(2,1)S(1)} %assemble.13), channel_id=1, source_target_pairs={{0,16},{8,24},{16,0},{24,8},{1,17},{9,25},{17,1},{25,9},{2,18},{10... | collective-permute-start | bytes 786440 | tf_op jit(solution)/shard_map/ppermute | solution.py:93
  135.8 9.0 %collective-permute-start.23 = (bf16[256,512]{1,0:T(8,128)(2,1)S(1)}, bf16[256,512]{1,0:T(8,128)(2,1)S(1)}, u32[]{:S(2)}, u32[]{:S(2)}) collective-permute-start(bf16[256,512]{1,0:T(8,128)(2,1)S(1)} %assemble.14), channel_id=1, source_target_pairs={{0,8},{8,0},{16,24},{24,16},{1,9},{9,1},{17,25},{25,17},{2,10},{10... | collective-permute-start | bytes 786440 | tf_op jit(solution)/shard_map/ppermute | solution.py:89
  137.4 17.6 %collective-permute-start.26 = (bf16[1024,512]{1,0:T(8,128)(2,1)S(1)}, bf16[1024,512]{1,0:T(8,128)(2,1)S(1)}, u32[]{:S(2)}, u32[]{:S(2)}) collective-permute-start(bf16[1024,512]{1,0:T(8,128)(2,1)S(1)} %assemble.17), channel_id=1, source_target_pairs={{0,1},{1,0},{2,3},{3,2},{4,5},{5,4},{6,7},{7,6},{8,9},{9,8},{10,11... | collective-permute-start | bytes 3145736 | tf_op jit(solution)/shard_map/ppermute | solution.py:109
  137.6 44.5 %collective-permute-start.28 = (bf16[1536,512]{1,0:T(8,128)(2,1)S(1)}, bf16[1536,512]{1,0:T(8,128)(2,1)S(1)}, u32[]{:S(2)}, u32[]{:S(2)}) collective-permute-start(bf16[1536,512]{1,0:T(8,128)(2,1)S(1)} %assemble.18), channel_id=1, source_target_pairs={{0,1},{1,0},{2,3},{3,2},{4,5},{5,4},{6,7},{7,6},{8,9},{9,8},{10,11... | collective-permute-start | bytes 4718600 | tf_op jit(solution)/shard_map/ppermute | solution.py:109
  140.5 14.4 %collective-permute-start.12 = (bf16[528,512]{1,0:T(8,128)(2,1)S(1)}, bf16[528,512]{1,0:T(8,128)(2,1)S(1)}, u32[]{:S(2)}, u32[]{:S(2)}) collective-permute-start(bf16[528,512]{1,0:T(8,128)(2,1)S(1)} %get-tuple-element.32), channel_id=1, source_target_pairs={{0,2},{2,0},{4,6},{6,4},{1,3},{3,1},{5,7},{7,5},{8,10},{10,8},{12,... | collective-permute-start | bytes 1622024 | tf_op jit(solution)/shard_map/ppermute | solution.py:673
  146.5 29.5 %collective-permute-start.25 = (bf16[1024,512]{1,0:T(8,128)(2,1)S(1)}, bf16[1024,512]{1,0:T(8,128)(2,1)S(1)}, u32[]{:S(2)}, u32[]{:S(2)}) collective-permute-start(bf16[1024,512]{1,0:T(8,128)(2,1)S(1)} %assemble.16), channel_id=1, source_target_pairs={{0,8},{8,0},{16,24},{24,16},{1,9},{9,1},{17,25},{25,17},{2,10},{10... | collective-permute-start | bytes 3145736 | tf_op jit(solution)/shard_map/ppermute | solution.py:89
  148.2 27.8 %collective-permute-start.24 = (bf16[1024,512]{1,0:T(8,128)(2,1)S(1)}, bf16[1024,512]{1,0:T(8,128)(2,1)S(1)}, u32[]{:S(2)}, u32[]{:S(2)}) collective-permute-start(bf16[1024,512]{1,0:T(8,128)(2,1)S(1)} %assemble.15), channel_id=1, source_target_pairs={{0,16},{8,24},{16,0},{24,8},{1,17},{9,25},{17,1},{25,9},{2,18},{10... | collective-permute-start | bytes 3145736 | tf_op jit(solution)/shard_map/ppermute | solution.py:93
  154.9 21.0 %collective-permute-start.16 = (bf16[528,512]{1,0:T(8,128)(2,1)S(1)}, bf16[528,512]{1,0:T(8,128)(2,1)S(1)}, u32[]{:S(2)}, u32[]{:S(2)}) collective-permute-start(bf16[528,512]{1,0:T(8,128)(2,1)S(1)} %get-tuple-element.36), channel_id=1, source_target_pairs={{0,6},{2,4},{4,2},{6,0},{1,7},{3,5},{5,3},{7,1},{8,14},{10,12},{12... | collective-permute-start | bytes 1622024 | tf_op jit(solution)/shard_map/ppermute | solution.py:673
  155.1 27.1 %collective-permute-start.29 = (bf16[512,512]{1,0:T(8,128)(2,1)S(1)}, bf16[512,512]{1,0:T(8,128)(2,1)S(1)}, u32[]{:S(2)}, u32[]{:S(2)}) collective-permute-start(bf16[512,512]{1,0:T(8,128)(2,1)S(1)} %assemble.19), channel_id=1, source_target_pairs={{0,1},{1,0},{2,3},{3,2},{4,5},{5,4},{6,7},{7,6},{8,9},{9,8},{10,11... | collective-permute-start | bytes 1572872 | tf_op jit(solution)/shard_map/ppermute | solution.py:109
  182.1 1.6 collective-permute-start.27
  185.6 10.8 %collective-permute-start.30 = (bf16[64,2048]{1,0:T(8,128)(2,1)S(1)}, bf16[64,2048]{1,0:T(8,128)(2,1)S(1)}, u32[]{:S(2)}, u32[]{:S(2)}) collective-permute-start(bf16[64,2048]{1,0:T(8,128)(2,1)S(1)} %get-tuple-element.44), channel_id=1, source_target_pairs={{0,2},{2,0},{4,6},{6,4},{1,3},{3,1},{5,7},{7,5},{8,10},{10,8},{12,... | collective-permute-start | bytes 786440 | tf_op jit(solution)/shard_map/ppermute | solution.py:706
  185.7 20.1 %collective-permute-start.31 = (bf16[64,2048]{1,0:T(8,128)(2,1)S(1)}, bf16[64,2048]{1,0:T(8,128)(2,1)S(1)}, u32[]{:S(2)}, u32[]{:S(2)}) collective-permute-start(bf16[64,2048]{1,0:T(8,128)(2,1)S(1)} %get-tuple-element.45), channel_id=1, source_target_pairs={{0,4},{2,6},{4,0},{6,2},{1,5},{3,7},{5,1},{7,3},{8,12},{10,14},{12... | collective-permute-start | bytes 786440 | tf_op jit(solution)/shard_map/ppermute | solution.py:706
  187.9 24.2 %collective-permute-start.32 = (bf16[64,2048]{1,0:T(8,128)(2,1)S(1)}, bf16[64,2048]{1,0:T(8,128)(2,1)S(1)}, u32[]{:S(2)}, u32[]{:S(2)}) collective-permute-start(bf16[64,2048]{1,0:T(8,128)(2,1)S(1)} %get-tuple-element.46), channel_id=1, source_target_pairs={{0,6},{2,4},{4,2},{6,0},{1,7},{3,5},{5,3},{7,1},{8,14},{10,12},{12... | collective-permute-start | bytes 786440 | tf_op jit(solution)/shard_map/ppermute | solution.py:706
  (19 other events, 104.9 us)
